TPU v7x, 256 devices: a whole 4x4x8 slice. The times are simulated.
256 devices in a mesh: seq: 64 (over x, z_hi, y), head: 4 (over z_lo, core).
Axes of the slice: x: 4, y: 4, z: 8 (z_hi: 4, z_lo: 2; z = z_hi * 2 + z_lo), core: 2. Of those that a mesh axis runs over, the one named last changes fastest.
Arguments:
- query_act: bfloat16 [32768, 1024], P('seq', 'head'), may hold values from -24 to 24
- key_act: bfloat16 [32768, 1024], P('seq', 'head'), may hold values from -6 to 6
- value_act: bfloat16 [32768, 1024], P('seq', 'head'), may hold values from -6 to 6
- out_weight: bfloat16 [1024, 1024], P('head'), may hold values from -0.1875 to 0.1875
- cotangent: bfloat16 [32768, 1024], P('seq', 'head'), may hold values from -16 to 16
Outputs:
- mixed_out: bfloat16 [32768, 1024], P('seq', 'head')
- query_grad: bfloat16 [32768, 1024], P('seq', 'head')
- key_grad: bfloat16 [32768, 1024], P('seq', 'head')
- value_grad: bfloat16 [32768, 1024], P('seq', 'head')
- weight_grad: float32 [1024, 1024], P('head', 'seq')
All inputs are finite; a program needn't handle non-finite values.
Results may differ from a plain program's by a relative error of at most 0.0065.
Values may be sent and summed in bfloat16 or wider, within the bound.
No kernel may reach another device: no remote copies, remote signals or barrier semaphores. Data moves between devices by JAX's collectives and lax.ppermute only.
A program may use at most 128 MiB of HBM per device.

v0:
```python
import jax
import jax.numpy as jnp
from jax import lax
from jax.sharding import PartitionSpec as P

HEAD_DIM = 64


NEG = -1e30


def partner_2(value, axis, bit):
    mask = 2**bit
    pairs = [(source, source ^ mask) for source in range(lax.axis_size(axis))]
    return lax.ppermute(value, axis, pairs)


def pick_rows(source, group_size, offsets):
    blocked = source.reshape((source.shape[0] // group_size, group_size) + source.shape[1:])
    pieces = [
        lax.dynamic_index_in_dim(blocked[:, :, member], offsets[member], 1, False)
        for member in range(len(offsets))
    ]
    return jnp.stack(pieces, 1)


def spread_rows(picked, group_size, offsets, filler):
    chosen = jnp.arange(group_size)[:, None] == jnp.stack(offsets)[None, :]
    chosen = chosen.reshape((1, group_size, len(offsets)) + (1,) * (picked.ndim - 2))
    widened = jnp.where(chosen, picked[:, None], filler)
    return widened.reshape((picked.shape[0] * group_size,) + picked.shape[1:])


def gather_doubling(block, bit_count, seq_pos):
    for bit_num in range(bit_count):
        partner = partner_2(block, "seq", bit_num)
        upper = seq_pos // (1 << bit_num) % 2 == 1
        block = jnp.where(
            upper, jnp.concatenate([partner, block], 1), jnp.concatenate([block, partner], 1)
        )
    return block


def reduce_halving(terms, bit_count, seq_pos):
    for bit_num in reversed(range(bit_count)):
        half_len = terms.shape[1] // 2
        lower_half = terms[:, :half_len]
        upper_half = terms[:, half_len:]
        upper = seq_pos // (1 << bit_num) % 2 == 1
        kept = jnp.where(upper, upper_half, lower_half)
        sent = jnp.where(upper, lower_half, upper_half)
        terms = kept + partner_2(sent.astype(jnp.bfloat16), "seq", bit_num).astype(sent.dtype)
    return terms


def block_scores(query_rows, key_rows, scaling):
    return (
        jnp.einsum("ihd,khd->hik", query_rows, key_rows, preferred_element_type=jnp.float32)
        * scaling
    )


def forward_block(query_rows, key_rows, value_rows, scaling):
    scores = block_scores(query_rows, key_rows, scaling)
    peaks = jnp.max(scores, axis=2)
    weights = jnp.exp(scores - peaks[:, :, None])
    totals = jnp.sum(weights, axis=2)
    weighted = jnp.einsum(
        "hik,khd->ihd", weights.astype(jnp.bfloat16), value_rows, preferred_element_type=jnp.float32
    )
    return (peaks.T, totals.T, weighted)


def backward_block(query_rows, key_rows, value_rows, grad_rows, log_total, delta_rows, scaling):
    scores = block_scores(query_rows, key_rows, scaling)
    softmax = jnp.exp(scores - log_total.T[:, :, None])
    value_term = jnp.einsum(
        "hik,ihd->khd", softmax.astype(jnp.bfloat16), grad_rows, preferred_element_type=jnp.float32
    )
    prob_grad = jnp.einsum(
        "ihd,khd->hik", grad_rows, value_rows, preferred_element_type=jnp.float32
    )
    score_grad = (softmax * (prob_grad - delta_rows.T[:, :, None])).astype(jnp.bfloat16)
    query_term = (
        jnp.einsum("hik,khd->ihd", score_grad, key_rows, preferred_element_type=jnp.float32)
        * scaling
    )
    key_term = (
        jnp.einsum("hik,ihd->khd", score_grad, query_rows, preferred_element_type=jnp.float32)
        * scaling
    )
    return (query_term, key_term, value_term)


def level_forward(query_rows, key_rows, value_rows, scaling):
    collected = [forward_block(query_rows, key_rows, value_rows, scaling)]
    return tuple(
        (jnp.concatenate([outcome[member] for outcome in collected], 0) for member in range(3))
    )


def level_backward(query_rows, key_rows, value_rows, grad_rows, log_rows, delta_rows, scaling):
    query_term, key_term, value_term = backward_block(
        query_rows, key_rows, value_rows, grad_rows, log_rows, delta_rows, scaling
    )
    return (query_term, key_term, value_term)


def body(query_act, key_act, value_act, out_weight, cotangent):
    tok_rows = query_act.shape[0]
    feat_dev = query_act.shape[1]
    heads_here = feat_dev // HEAD_DIM
    scaling = HEAD_DIM ** (-0.5)
    seq_pos = lax.axis_index("seq")
    head_pos = lax.axis_index("head")
    seq_count = lax.axis_size("seq")
    seq_bits = seq_count.bit_length() - 1
    level_bits = [0, 2, min(4, seq_bits), seq_bits]
    shaped = [
        member.reshape(tok_rows, heads_here, HEAD_DIM) for member in (query_act, key_act, value_act)
    ]
    levels = []
    for bit_count in level_bits:
        group_size = 1 << bit_count
        offsets = [(head_pos * heads_here + member) % group_size for member in range(heads_here)]
        picked = [pick_rows(member, group_size, offsets) for member in shaped]
        paired = jnp.stack([picked[1], picked[2]], 0).reshape(2, picked[1].shape[0], feat_dev)
        levels.append((bit_count, group_size, offsets, picked[0], paired))
    gathered = [levels[0][4], gather_doubling(levels[1][4], levels[1][0], seq_pos)]
    gathered.append(gather_doubling(levels[2][4], levels[2][0], seq_pos))
    gathered.append(lax.all_gather(levels[3][4], "seq", axis=1, tiled=True))
    results = []
    for number in range(4):
        group_size = levels[number][1]
        offsets = levels[number][2]
        query_rows = levels[number][3]
        key_value = gathered[number].reshape(2, -1, heads_here, HEAD_DIM)
        peaks, totals, weighted = level_forward(query_rows, key_value[0], key_value[1], scaling)
        results.append(
            (
                spread_rows(peaks, group_size, offsets, NEG),
                spread_rows(totals, group_size, offsets, 0.0),
                spread_rows(weighted, group_size, offsets, 0.0),
            )
        )
    top_peak = jnp.max(jnp.stack([outcome[0] for outcome in results], 0), axis=0)
    factors = [jnp.exp(outcome[0] - top_peak) for outcome in results]
    denominator = sum((factors[number] * results[number][1] for number in range(4)))
    numerator = sum((factors[number][:, :, None] * results[number][2] for number in range(4)))
    out_full = numerator / denominator[:, :, None]
    log_total = top_peak + jnp.log(denominator)
    attended = out_full.reshape(tok_rows, feat_dev).astype(jnp.bfloat16)
    partial_out = jnp.dot(attended, out_weight, preferred_element_type=jnp.float32)
    mixed_out = lax.psum_scatter(partial_out, "head", scatter_dimension=1, tiled=True).astype(
        jnp.bfloat16
    )
    grad_full = lax.all_gather(cotangent, "head", axis=1, tiled=True)
    attn_grad = jnp.einsum(
        "tc,fc->tf", grad_full, out_weight, preferred_element_type=jnp.float32
    ).astype(jnp.bfloat16)
    weight_term = jnp.einsum("tf,tc->fc", attended, grad_full, preferred_element_type=jnp.float32)
    grad_shaped = attn_grad.reshape(tok_rows, heads_here, HEAD_DIM)
    delta_all = jnp.sum(grad_shaped.astype(jnp.float32) * out_full, axis=2)
    query_total = jnp.zeros((tok_rows, heads_here, HEAD_DIM), jnp.float32)
    pair_terms = []
    for number in range(4):
        group_size = levels[number][1]
        offsets = levels[number][2]
        query_rows = levels[number][3]
        key_value = gathered[number].reshape(2, -1, heads_here, HEAD_DIM)
        grad_rows = pick_rows(grad_shaped, group_size, offsets)
        log_rows = pick_rows(log_total, group_size, offsets)
        delta_rows = pick_rows(delta_all, group_size, offsets)
        query_term, key_term, value_term = level_backward(
            query_rows, key_value[0], key_value[1], grad_rows, log_rows, delta_rows, scaling
        )
        query_total = query_total + spread_rows(query_term, group_size, offsets, 0.0)
        pair_terms.append(jnp.stack([key_term, value_term], 0).reshape(2, -1, feat_dev))
    reduced = [pair_terms[0], reduce_halving(pair_terms[1], levels[1][0], seq_pos)]
    reduced.append(reduce_halving(pair_terms[2], levels[2][0], seq_pos))
    fourth, weight_grad = (
        lax.psum_scatter(pair_terms[3], "seq", scatter_dimension=1, tiled=True),
        lax.psum_scatter(weight_term, "seq", scatter_dimension=1, tiled=True),
    )
    reduced.append(fourth)
    key_total = jnp.zeros((tok_rows, heads_here, HEAD_DIM), jnp.float32)
    value_total = jnp.zeros((tok_rows, heads_here, HEAD_DIM), jnp.float32)
    for number in range(4):
        split_pair = reduced[number].reshape(2, -1, heads_here, HEAD_DIM)
        key_total = key_total + spread_rows(
            split_pair[0], levels[number][1], levels[number][2], 0.0
        )
        value_total = value_total + spread_rows(
            split_pair[1], levels[number][1], levels[number][2], 0.0
        )
    query_grad = query_total.reshape(tok_rows, feat_dev).astype(jnp.bfloat16)
    key_grad = key_total.reshape(tok_rows, feat_dev).astype(jnp.bfloat16)
    value_grad = value_total.reshape(tok_rows, feat_dev).astype(jnp.bfloat16)
    return (mixed_out, query_grad, key_grad, value_grad, weight_grad)


def solution(mesh):
    placed = (
        P("seq", "head"),
        P("seq", "head"),
        P("seq", "head"),
        P("head", None),
        P("seq", "head"),
    )
    return jax.shard_map(
        body,
        mesh=mesh,
        in_specs=placed,
        out_specs=(
            P("seq", "head"),
            P("seq", "head"),
            P("seq", "head"),
            P("seq", "head"),
            P("head", "seq"),
        ),
        check_vma=False,
    )
```

profile of v0, /device:TPU:32, one launch (start us, length us, event | category | flops | bytes accessed | tf_op | source)
XLA Modules:
  0.0 1558.5 jit_solution(5889722909411585305)
XLA Ops:
  22.2 2.1 reshape_reshape.57
  26.9 1.9 copy-done.1
  45.3 1.9 fusion.120
  56.9 4.0 fusion.121
  64.8 3.0 fusion.118
  102.6 196.4 %all_gather.6 = bf16[2,512,256]{2,1,0:T(8,128)(2,1)S(1)} all-gather(bf16[2,8,256]{2,1,0:T(8,128)(2,1)S(1)} %pad_maximum_fusion.31), channel_id=1, replica_groups=mesh['seq'=64,'head'=4] {'seq'}, dimensions={1}, use_global_device_ids=true | all-gather | bytes 532480 | tf_op jit(solution)/shard_map/all_gather | solution.py:131
  314.7 2.0 collective-permute-start.2
  338.4 3.6 collective-permute-start.1
  344.3 2.1 collective-permute-done.1
  355.4 1.9 collective-permute-done.5
  364.8 4.6 fusion.34
  377.9 2.1 copy.376
  398.8 3.2 pad_maximum_fusion
  412.4 2.6 divide_convert_fusion
  424.9 3.5 collective-permute-start.6
  430.3 1.9 collective-permute-start.8
  434.2 3.6 multiply_convert_fusion
  437.8 2.2 convolution_multiply_fusion.5
  440.1 2.0 copy.406
  442.1 2.5 convolution_multiply_fusion.4
  444.6 2.0 copy.423
  448.2 2.0 broadcast_in_dim.515
  450.3 2.6 broadcast_in_dim.516
  454.0 2.7 broadcast_in_dim.520
  456.7 2.8 fusion.139
  463.1 2.1 collective-permute-start.7
  468.2 5.6 collective-permute-done.10
  474.1 1.9 collective-permute-start.11
  484.6 648.2 %all-reduce.3.cloned.1.call-done = f32[2,512,256]{2,0,1:T(2,128)} async-done(((f32[2,512,256]{2,0,1:T(2,128)}), f32[2,512,256]{2,0,1:T(2,128)}) %all-reduce.3.cloned.1.call-update) | async-done | bytes 1048592
  1138.3 3.8 add_convert_fusion
  1142.1 21.8 %reduce-scatter.3.cloned.1.call-done = f32[512,256]{1,0:T(8,128)} async-done(((f32[512,1024]{1,0:T(8,128)}), f32[512,256]{1,0:T(8,128)}) %reduce-scatter.3.cloned.1.call-update) | async-done | bytes 524304 | tf_op jit(solution)/shard_map/reduce_scatter | solution.py:154
  1165.6 385.9 %reduce-scatter.5.cloned.1.call-done = f32[256,16]{0,1:T(8,128)} async-done(((f32[256,1024]{0,1:T(8,128)}), f32[256,16]{0,1:T(8,128)}) %reduce-scatter.5.cloned.1.call-update) | async-done | bytes 16400 | tf_op jit(solution)/shard_map/reduce_scatter | solution.py:183
  (579 shorter events, 212.8 us)
Async XLA Ops:
  7.2 87.3 %copy-start = (bf16[256,1024]{1,0:T(8,128)(2,1)S(1)}, bf16[256,1024]{1,0:T(8,128)(2,1)}, u32[]{:S(2)}) copy-start(bf16[256,1024]{1,0:T(8,128)(2,1)} %param.8) | copy-start | bytes 1572868
  7.2 87.3 %all-gather.2.cloned.1.call-start = ((), (), s32[]{:S(2)}) async-start(), calls=%async_computation.3 | async-start | bytes 1310720 | tf_op jit(solution)/shard_map/all_gather | solution.py:157
  7.9 1124.8 %all-reduce.3.cloned.1.call-start = ((), (), s32[]{:S(2)}) async-start(), calls=%async_computation.5 | async-start | bytes 2097152
  71.8 19.1 %copy-start.25 = (bf16[8,64,4,64]{1,0,3,2:T(8,128)(2,1)S(1)}, bf16[8,64,4,64]{1,0,3,2:T(8,128)(2,1)}, u32[]{:S(2)}) copy-start(bf16[8,64,4,64]{1,0,3,2:T(8,128)(2,1)} %reshape_reshape.57) | copy-start | bytes 786436
  299.1 21.2 %copy-start.14 = (bf16[1,512,256]{1,2,0:T(8,128)(2,1)}, bf16[1,512,256]{1,2,0:T(8,128)(2,1)S(1)}, u32[]{:S(2)}) copy-start(bf16[1,512,256]{1,2,0:T(8,128)(2,1)S(1)} %copy.381) | copy-start | bytes 786436
  299.3 21.1 %copy-start.12 = (bf16[1,512,256]{1,2,0:T(8,128)(2,1)}, bf16[1,512,256]{1,2,0:T(8,128)(2,1)S(1)}, u32[]{:S(2)}) copy-start(bf16[1,512,256]{1,2,0:T(8,128)(2,1)S(1)} %copy.369) | copy-start | bytes 786436
  307.7 23.1 %copy-start.52 = (bf16[128,1,1,64]{3,2,1,0:T(2,128)(2,1)S(1)}, bf16[128,1,1,64]{3,2,1,0:T(2,128)(2,1)}, u32[]{:S(2)}) copy-start(bf16[128,1,1,64]{3,2,1,0:T(2,128)(2,1)} %get-tuple-element.146) | copy-start | bytes 49156
  307.7 23.8 %copy-start.51 = (bf16[128,1,1,64]{3,2,1,0:T(2,128)(2,1)S(1)}, bf16[128,1,1,64]{3,2,1,0:T(2,128)(2,1)}, u32[]{:S(2)}) copy-start(bf16[128,1,1,64]{3,2,1,0:T(2,128)(2,1)} %get-tuple-element.144) | copy-start | bytes 49156
  307.7 29.6 %collective-permute-start = (bf16[2,128,256]{1,2,0:T(8,128)(2,1)}, bf16[2,128,256]{1,2,0:T(8,128)(2,1)}, u32[]{:S(2)}, u32[]{:S(2)}) collective-permute-start(bf16[2,128,256]{1,2,0:T(8,128)(2,1)} %pad_maximum_fusion.7), channel_id=1, source_target_pairs={{0,4},{4,0},{8,12},{12,8},{16,20},{20,16},{24,28},{28,24},{32,36},... | collective-permute-start | bytes 393224 | tf_op jit(solution)/shard_map/ppermute | solution.py:15
  313.9 20.2 %copy-start.77 = (bf16[32,1,1,64]{3,2,1,0:T(2,128)(2,1)S(1)}, bf16[32,1,1,64]{3,2,1,0:T(2,128)(2,1)}, u32[]{:S(2)}) copy-start(bf16[32,1,1,64]{3,2,1,0:T(2,128)(2,1)} %get-tuple-element.160) | copy-start | bytes 12292
  313.9 20.8 %copy-start.76 = (bf16[32,1,1,64]{3,2,1,0:T(2,128)(2,1)S(1)}, bf16[32,1,1,64]{3,2,1,0:T(2,128)(2,1)}, u32[]{:S(2)}) copy-start(bf16[32,1,1,64]{3,2,1,0:T(2,128)(2,1)} %get-tuple-element.166) | copy-start | bytes 12292
  314.7 4.1 collective-permute-start.2
  317.6 25.1 %copy-start.60 = (f32[4,8]{1,0:T(4,128)}, f32[4,8]{1,0:T(4,128)S(1)}, u32[]{:S(2)}) copy-start(f32[4,8]{1,0:T(4,128)S(1)} %get-tuple-element.132) | copy-start | bytes 388
  319.7 16.6 %collective-permute-start.3 = (bf16[2,64,256]{2,1,0:T(8,128)(2,1)S(1)}, bf16[2,64,256]{2,1,0:T(8,128)(2,1)}, u32[]{:S(2)}, u32[]{:S(2)}) collective-permute-start(bf16[2,64,256]{2,1,0:T(8,128)(2,1)S(1)} %maximum_select_fusion.5), channel_id=1, source_target_pairs={{0,8},{4,12},{8,0},{12,4},{16,24},{20,28},{24,16},{28,20},{32,40},... | collective-permute-start | bytes 196616 | tf_op jit(solution)/shard_map/ppermute | solution.py:15
  319.9 24.2 %copy-start.82 = (f32[4,8]{1,0:T(4,128)}, f32[4,8]{1,0:T(4,128)S(1)}, u32[]{:S(2)}) copy-start(f32[4,8]{1,0:T(4,128)S(1)} %fusion.50) | copy-start | bytes 388
  337.2 6.1 collective-permute-start.4
  338.4 8.0 collective-permute-start.1
  344.1 13.2 collective-permute-start.5
  376.4 18.4 %copy-start.15 = (bf16[1,512,256]{1,2,0:T(8,128)(2,1)S(1)}, bf16[1,512,256]{1,2,0:T(8,128)(2,1)}, u32[]{:S(2)}) copy-start(bf16[1,512,256]{1,2,0:T(8,128)(2,1)} %copy-done.14) | copy-start | bytes 786436
  402.0 761.8 %reduce-scatter.3.cloned.1.call-start = ((), (), s32[]{:S(2)}) async-start(), calls=%async_computation.2 | async-start | bytes 2621440 | tf_op jit(solution)/shard_map/reduce_scatter | solution.py:154
  416.7 1134.8 %reduce-scatter.5.cloned.1.call-start = ((), (), s32[]{:S(2)}) async-start(), calls=%async_computation.4 | async-start | bytes 1064960 | tf_op jit(solution)/shard_map/reduce_scatter | solution.py:183
  424.9 37.1 %collective-permute-start.6 = (bf16[2,256,256]{1,2,0:T(8,128)(2,1)}, bf16[2,256,256]{1,2,0:T(8,128)(2,1)}, u32[]{:S(2)}, u32[]{:S(2)}) collective-permute-start(bf16[2,256,256]{1,2,0:T(8,128)(2,1)} %select_convert_fusion.1), channel_id=1, source_target_pairs={{0,8},{4,12},{8,0},{12,4},{16,24},{20,28},{24,16},{28,20},{32,40},... | collective-permute-start | bytes 786440 | tf_op jit(solution)/shard_map/ppermute | solution.py:15
  430.3 29.2 %collective-permute-start.8 = (bf16[2,256,256]{1,2,0:T(8,128)(2,1)}, bf16[2,256,256]{1,2,0:T(8,128)(2,1)}, u32[]{:S(2)}, u32[]{:S(2)}) collective-permute-start(bf16[2,256,256]{1,2,0:T(8,128)(2,1)} %select_convert_fusion), channel_id=1, source_target_pairs={{0,32},{4,36},{8,40},{12,44},{16,48},{20,52},{24,56},{28,60},{32,0... | collective-permute-start | bytes 786440 | tf_op jit(solution)/shard_map/ppermute | solution.py:15
  460.6 6.1 collective-permute-start.9
  463.1 5.1 collective-permute-start.7
  466.9 6.9 collective-permute-start.10
  474.1 5.3 collective-permute-start.11
  482.0 656.3 %copy-start.22 = (f32[512,256]{1,0:T(8,128)S(1)}, f32[512,256]{1,0:T(8,128)}, u32[]{:S(2)}) copy-start(f32[512,256]{1,0:T(8,128)} %broadcast_in_dim.505) | copy-start | bytes 1572868
  482.0 656.3 %copy-start.23 = (f32[512,256]{1,0:T(8,128)S(1)}, f32[512,256]{1,0:T(8,128)}, u32[]{:S(2)}) copy-start(f32[512,256]{1,0:T(8,128)} %broadcast_in_dim.516) | copy-start | bytes 1572868
  482.0 656.3 %copy-start.24 = (f32[512,256]{1,0:T(8,128)S(1)}, f32[512,256]{1,0:T(8,128)}, u32[]{:S(2)}) copy-start(f32[512,256]{1,0:T(8,128)} %broadcast_in_dim.520) | copy-start | bytes 1572868
  482.0 656.3 %copy-start.27 = (pred[512,256]{1,0:T(8,128)(4,1)S(1)}, pred[512,256]{1,0:T(8,128)(4,1)}, u32[]{:S(2)}) copy-start(pred[512,256]{1,0:T(8,128)(4,1)} %copy.379) | copy-start | bytes 393220
  482.0 656.3 %copy-start.28 = (pred[512,256]{1,0:T(8,128)(4,1)S(1)}, pred[512,256]{1,0:T(8,128)(4,1)}, u32[]{:S(2)}) copy-start(pred[512,256]{1,0:T(8,128)(4,1)} %copy.384) | copy-start | bytes 393220
  (95 other events, 735.2 us)
Sparse Core Ops, SparseCore 0:
  9.8 25.8 all-gather.1
  402.1 730.5 all-reduce.2
  1135.5 28.2 reduce-scatter.2
  1166.7 384.7 reduce-scatter.4
where the time goes:
time: 1570 us; the launch traced here: 1560 us
  waiting for transfers between devices  1070 us (68%)
  blocking collectives  196 us (12%)
  local copies, waits for them, and re-layouts  190 us (12%)
  matrix products  34.5 us (2%)
  other arithmetic  32.5 us (2%)
  starting transfers between devices  17.7 us (1%)
  between operations  17.2 us (1%)
    unnamed x5, waiting for transfers between devices  649 us
    reduce_scatter x1, waiting for transfers between devices, body(): lax.psum_scatter(weight_term, 'seq', scatter_dimension=1, tiled=True)  386 us
    all_gather x1, blocking collectives, body(): gathered.append(lax.all_gather(levels[3][4], 'seq', axis=1, tiled=True))  196 us
    dynamic_slice x76, local copies, waits for them, and re-layouts, pick_rows(): lax.dynamic_index_in_dim(blocked[:, :, member], offsets[member], 1, False)  51.9 us
    broadcast_in_dim x77, local copies, waits for them, and re-layouts, spread_rows(): widened = jnp.where(chosen, picked[:, None], filler)  50.5 us
  transfers between devices with their start and end apart: 16, of which 10 were waited for; matrix products, arithmetic and copies ran while one was open for 12% of the time, Pallas kernels for 0%

commit v1 on v0

v1 whole, which is shorter than its diff:
```python
import functools

import jax
import jax.numpy as jnp
from jax import lax
from jax.experimental import pallas as pl
from jax.experimental.pallas import tpu as pltpu
from jax.sharding import PartitionSpec as P

HD = 64
NH = 4
T = 512
F = NH * HD
SEL2, SEL3, SEL4 = 128, 32, 8
SCALE = HD ** -0.5
NEG = -1e30
BF = jnp.bfloat16
F32 = jnp.float32


def iota(shape, dim):
    return lax.broadcasted_iota(jnp.int32, shape, dim)


def token_of(index):
    return (index >> 7) + ((index >> 5) & 3) * 4 + ((index >> 3) & 3) * 16 + (index & 7) * 64


def pick_mat(head, rows):
    wanted = (token_of(iota((rows, T), 0)) + head) & (T - 1)
    return jnp.where(wanted == iota((rows, T), 1), 1.0, 0.0).astype(BF)


def put_mat(head, cols):
    wanted = (token_of(iota((T, cols), 1)) + head) & (T - 1)
    return jnp.where(wanted == iota((T, cols), 0), 1.0, 0.0).astype(BF)


def dot(a, b, dims=((1,), (0,))):
    return lax.dot_general(a, b, (dims, ((), ())), preferred_element_type=F32)


def per_head_rows(mats, arrays):
    pairs = []
    for p in range(2):
        both = jnp.concatenate([a[:, 128 * p:128 * p + 128] for a in arrays], 1)
        even = dot(mats[2 * p], both)
        odd = dot(mats[2 * p + 1], both)
        pairs.append(jnp.where((iota(even.shape, 1) & 127) < HD, even, odd))
    return [
        jnp.concatenate([pair[:, 128 * n:128 * n + 128] for pair in pairs], 1)
        for n in range(len(arrays))
    ]


def head_blocks(rows, n):
    part = rows[:n]
    lane_head = iota(part.shape, 1) >> 6
    return jnp.concatenate([jnp.where(lane_head == h, part, 0.0) for h in range(NH)], 0)


def blocks_both(rows, n):
    full = head_blocks(rows, n)
    if NH * n < 128:
        full = jnp.concatenate([full, jnp.zeros((128 - NH * n, F), F32)], 0)
    return full.astype(BF), full.T.astype(BF)


def to_lanes(rows, n):
    total = None
    for h in range(NH):
        row = jnp.broadcast_to(jnp.where(iota((1, 128), 1) < n, rows[h], 0.0), (8, 128))
        if h:
            row = pltpu.roll(row, n * h, 1)
        total = row if total is None else total + row
    return total[0:1]


def from_lanes(rows, h, n, fill):
    if h:
        rows = pltpu.roll(rows, 128 - n * h, 1)
    return jnp.where(iota(rows.shape, 1) < n, rows, fill)


def soft(scores):
    peak = jnp.max(scores, axis=0, keepdims=True)
    weights = jnp.exp(scores - peak)
    return peak, jnp.sum(weights, axis=0, keepdims=True), weights.astype(BF)


def forward(keys, values, q_t):
    peak, total, weights = soft(dot(keys, q_t))
    return peak, total, dot(values, weights, ((0,), (0,)))


def backward(keys, values, q, q_t, g, g_t, lse, delta):
    prob = jnp.exp(dot(keys, q_t) - lse)
    ds = (prob * (dot(values, g_t) - delta)).astype(BF)
    d_values = dot(prob.astype(BF), g)
    d_keys = dot(ds, q)
    return d_keys, d_values, dot(keys, ds, ((0,), (0,)))


def diag_lanes(wide, n):
    return jnp.concatenate(
        [from_lanes(wide[HD * h:HD * h + HD], h, n, 0.0) for h in range(NH)], 0
    )


def half_mask(rows, h):
    return jnp.where((iota(rows.shape, 1) < HD) == (h % 2 == 0), rows.astype(F32), 0.0).astype(BF)


def half_pad(cols, h):
    zero = jnp.zeros_like(cols)
    return jnp.concatenate([cols, zero] if h % 2 == 0 else [zero, cols], 0)


def level1_backward(p, q_ref, q_t_ref, k_ref, k_t_ref, v_ref, g_ref, g_t_ref, lse_ref, delta_ref,
                    dk_ref, dv_ref, dq_ref):
    cols = slice(128 * p, 128 * p + 128)
    for h in (2 * p, 2 * p + 1):
        rows = slice(HD * h, HD * h + HD)
        for c in range(2):
            lanes = slice(256 * c, 256 * c + 256)
            q_t = half_pad(q_t_ref[rows, lanes], h)
            g_t = half_pad(g_t_ref[rows, lanes], h)
            prob = jnp.exp(dot(k_ref[:, cols], q_t) - lse_ref[h:h + 1, lanes])
            ds = (prob * (dot(v_ref[:, cols], g_t) - delta_ref[h:h + 1, lanes])).astype(BF)
            dv = dot(prob.astype(BF), half_mask(g_ref[lanes, cols], h))
            dk = dot(ds, half_mask(q_ref[lanes, cols], h))
            dq_ref[HD * (h % 2):HD * (h % 2) + HD, lanes] = dot(k_t_ref[rows, :], ds)
            if h % 2 == 0 and c == 0:
                dv_ref[...] = dv
                dk_ref[...] = dk
            else:
                dv_ref[...] += dv
                dk_ref[...] += dk


def pack1_kernel(pos, k, v, out):
    mats = [pick_mat(pos[0] * NH + m, SEL2) for m in range(NH)]
    ks, vs = per_head_rows(mats, [k[...], v[...]])
    out[0:SEL2] = ks.astype(BF)
    out[SEL2:2 * SEL2] = vs.astype(BF)


def first_kernel(pos, q, k, v, _p1, q_out, q_t_out, k_out, k_t_out, v_out, m_out, l_out, o_out):
    mats = [pick_mat(pos[0] * NH + m, T) for m in range(NH)]
    qs, ks, vs = per_head_rows(mats, [q[...], k[...], v[...]])
    qs = qs * SCALE
    q_out[...] = qs.astype(BF)
    q_t_out[...] = qs.T.astype(BF)
    k_out[...] = ks.astype(BF)
    k_t_out[...] = ks.T.astype(BF)
    v_out[...] = vs.astype(BF)
    v_t = vs.T.astype(BF)
    m_out[...] = jnp.zeros_like(m_out)
    l_out[...] = jnp.zeros_like(l_out)
    for h in range(NH):
        cols = slice(128 * (h // 2), 128 * (h // 2) + 128)
        rows = slice(HD * h, HD * h + HD)
        for c in range(2):
            lanes = slice(256 * c, 256 * c + 256)
            peak, total, weights = soft(dot(k_out[:, cols], half_pad(q_t_out[rows, lanes], h)))
            m_out[h:h + 1, lanes] = peak
            l_out[h:h + 1, lanes] = total
            o_out[rows, lanes] = dot(v_t[rows, :], weights)


def pack2_kernel(a0, a1, a2, a3, out):
    for n, a in enumerate((a0, a1, a2, a3)):
        out[SEL3 * n:SEL3 * n + SEL3] = a[0:SEL3]
        out[128 + SEL3 * n:128 + SEL3 * n + SEL3] = a[SEL2:SEL2 + SEL3]


def pack3_kernel(a0, a1, a2, a3, out):
    for base in (0, 128):
        parts = []
        for a in (a0, a1, a2, a3):
            for n in range(4):
                start = base + SEL3 * n
                parts.append(a[start:start + 16].astype(F32)[:SEL4])
        out[base:base + 128] = jnp.concatenate(parts, 0).astype(BF)


def stack_kv(refs):
    keys = jnp.concatenate([a[0:128] for a in refs], 0)
    values = jnp.concatenate([a[128:256] for a in refs], 0)
    return keys, values


def second_kernel(a0, a1, a2, a3, q, _p2, m_out, l_out, o_out):
    keys, values = stack_kv((a0, a1, a2, a3))
    _, q_t = blocks_both(q[0:SEL2].astype(F32), SEL2)
    peak, total, wide = forward(keys, values, q_t)
    m_out[...] = jnp.broadcast_to(peak, m_out.shape)
    l_out[...] = jnp.broadcast_to(total, l_out.shape)
    o_out[...] = jnp.concatenate(
        [wide[HD * h:HD * h + HD, 128 * h:128 * h + 128] for h in range(NH)], 0
    )


def third_kernel(pos, a0, a1, a2, a3, q, m1, l1, o1, m2, l2, o2, c0, c1, c2, c3, w, _p3,
                 m_out, l_out, o_out, g_out, g_t_out, lse_out, delta_out, att_out):
    here = pos[0]
    grad = None
    for r, c in enumerate((c0, c1, c2, c3)):
        at = pl.multiple_of((here ^ r) * F, F)
        term = dot(c[...], w[:, pl.ds(at, F)], ((1,), (1,)))
        grad = term if grad is None else grad + term
    mats = [pick_mat(here * NH + m, T) for m in range(NH)]
    (gs,) = per_head_rows(mats, [grad.astype(BF)])
    g_t = gs.T
    g_out[...] = gs.astype(BF)
    g_t_out[...] = g_t.astype(BF)

    keys, values = stack_kv((a0, a1, a2, a3))
    _, q_t = blocks_both(q[0:SEL3].astype(F32), SEL3)
    m3, l3, wide = forward(keys, values, q_t)
    m3 = jnp.broadcast_to(m3, (8, 128))
    l3 = jnp.broadcast_to(l3, (8, 128))
    lse_out[...] = jnp.zeros_like(lse_out)
    delta_out[...] = jnp.zeros_like(delta_out)
    m_out[...] = jnp.zeros_like(m_out)
    l_out[...] = jnp.zeros_like(l_out)
    for h in range(NH):
        rows = slice(HD * h, HD * h + HD)
        ma, la, oa = m1[h:h + 1, 0:128], l1[h:h + 1, 0:128], o1[rows, 0:128]
        mb, lb = m2[0:1, 128 * h:128 * h + 128], l2[0:1, 128 * h:128 * h + 128]
        mc = from_lanes(m3, h, SEL3, NEG)[0:1]
        lc = from_lanes(l3, h, SEL3, 0.0)[0:1]
        oc = from_lanes(wide[rows], h, SEL3, 0.0)
        top = jnp.maximum(jnp.maximum(ma, mb), mc)
        fa, fb, fc = jnp.exp(ma - top), jnp.exp(mb - top), jnp.exp(mc - top)
        m_out[h:h + 1] = top
        l_out[h:h + 1] = fa * la + fb * lb + fc * lc
        o_out[rows] = fa * oa + fb * o2[rows] + fc * oc
        total = l1[h:h + 1, 128:T]
        out = o1[rows, 128:T] / total
        lse_out[h:h + 1, 128:T] = m1[h:h + 1, 128:T] + jnp.log(total)
        delta_out[h:h + 1, 128:T] = jnp.sum(g_t_out[rows, 128:T].astype(F32) * out, axis=0, keepdims=True)
        att_out[rows] = dot(out.astype(BF), mats[h][128:T])


def fourth_kernel(pos, a0, a1, a2, a3, q, m, l, o, g, g_t, lse_in, delta_in, att_in, c0, c1, c2, c3,
                  lse_out, delta_out, att_out, dq_out, s0, s1, s2, s3, blocks):
    here, x_pos = pos[0], pos[1]
    keys, values = stack_kv((a0, a1, a2, a3))
    q4, q4_t = blocks_both(q[0:16].astype(F32), SEL4)
    g4, g4_t = blocks_both(g[0:16].astype(F32), SEL4)
    peak, total, weights = soft(dot(keys, q4_t))
    wide = dot(values, weights, ((0,), (0,)))
    peak = jnp.broadcast_to(peak, (8, 128))
    total = jnp.broadcast_to(total, (8, 128))
    lse_out[...] = lse_in[...]
    delta_out[...] = delta_in[...]
    lse_rows, delta_rows = [], []
    for h in range(NH):
        rows = slice(HD * h, HD * h + HD)
        ma, la, oa = m[h:h + 1], l[h:h + 1], o[rows]
        mb = from_lanes(peak, h, SEL4, NEG)[0:1]
        lb = from_lanes(total, h, SEL4, 0.0)[0:1]
        ob = from_lanes(wide[rows], h, SEL4, 0.0)
        top = jnp.maximum(ma, mb)
        fa, fb = jnp.exp(ma - top), jnp.exp(mb - top)
        denominator = fa * la + fb * lb
        out = (fa * oa + fb * ob) / denominator
        lse = top + jnp.log(denominator)
        delta = jnp.sum(g_t[rows, 0:128].astype(F32) * out, axis=0, keepdims=True)
        lse_out[h:h + 1, 0:128] = lse
        delta_out[h:h + 1, 0:128] = delta
        lse_rows.append(lse)
        delta_rows.append(delta)
        att = att_in[rows] + dot(out.astype(BF), pick_mat(here * NH + h, SEL2))
        att_out[rows] = att.astype(BF)
    d_keys, d_values, dq = backward(
        keys, values, q4, q4_t, g4, g4_t, to_lanes(lse_rows, SEL4), to_lanes(delta_rows, SEL4)
    )
    dq_out[...] = diag_lanes(dq, SEL4)
    for r, c in enumerate((c0, c1, c2, c3)):
        blocks[here ^ r] = c[...]
    for d, s in enumerate((s0, s1, s2, s3)):
        s[0:128] = d_keys[128 * d:128 * d + 128].astype(s.dtype)
        s[128:256] = d_values[128 * d:128 * d + 128].astype(s.dtype)
        term = dot(att_out[...], blocks[(x_pos - d) & 3])
        s[256:512] = term.T.astype(s.dtype)


def project_kernel(pos, att, w, send, keep_a, keep_b):
    here = pos[0]
    for r, ref in ((0, keep_a), (2, keep_b), (1, send.at[0:T]), (3, send.at[T:2 * T])):
        at = pl.multiple_of((here ^ r) * F, F)
        ref[...] = dot(att[...], w[:, pl.ds(at, F)], ((0,), (0,))).astype(ref.dtype)


def fifth_kernel(a0, a1, a2, a3, q, q_t, k, k_t, v, g, g_t, lse, delta, dq_in,
                 dk3, dv3, dq_first, dk, dv, dq):
    keys, values = stack_kv((a0, a1, a2, a3))
    q3, q3_t = blocks_both(q[0:SEL3].astype(F32), SEL3)
    g3, g3_t = blocks_both(g[0:SEL3].astype(F32), SEL3)
    lse3 = to_lanes([lse[h:h + 1, 0:128] for h in range(NH)], SEL3)
    delta3 = to_lanes([delta[h:h + 1, 0:128] for h in range(NH)], SEL3)
    dk3[...], dv3[...], wide = backward(keys, values, q3, q3_t, g3, g3_t, lse3, delta3)
    dq_first[...] = dq_in[...] + diag_lanes(wide, SEL3)
    level1_backward(0, q, q_t, k, k_t, v, g, g_t, lse, delta, dk, dv, dq)


def reduce_z_kernel(pos, own, b1, b2, b3, dk3, dv3, s0, s1, s2, s3, total):
    z_pos = pos[2]
    total[...] = own[...] + b1[...].astype(F32) + b2[...].astype(F32) + b3[...].astype(F32)
    for d, s in enumerate((s0, s1, s2, s3)):
        for base, level in ((0, dk3), (128, dv3)):
            parts = []
            for n in range(4):
                at = 128 * d + SEL3 * n
                start = base + SEL3 * d + SEL4 * n
                parts.append(level[at:at + SEL4] + total[start:start + SEL4])
                parts.append(level[at + SEL4:at + SEL3])
            s[base:base + 128] = jnp.concatenate(parts, 0).astype(s.dtype)
        start = pl.multiple_of(256 + 64 * ((z_pos - d) & 3), 64)
        s[256:320] = total[pl.ds(start, 64)].astype(s.dtype)


def sixth_kernel(a0, a1, a2, a3, q, g, lse, delta, dq_in, _s, dk2, dv2, dq_first):
    keys, values = stack_kv((a0, a1, a2, a3))
    q2, q2_t = blocks_both(q[0:SEL2].astype(F32), SEL2)
    g2, g2_t = blocks_both(g[0:SEL2].astype(F32), SEL2)
    lse2 = jnp.concatenate([lse[h:h + 1, 0:128] for h in range(NH)], 1)
    delta2 = jnp.concatenate([delta[h:h + 1, 0:128] for h in range(NH)], 1)
    dk2[...], dv2[...], wide = backward(keys, values, q2, q2_t, g2, g2_t, lse2, delta2)
    diag = [wide[HD * h:HD * h + HD, 128 * h:128 * h + 128] for h in range(NH)]
    dq_first[...] = dq_in[...] + jnp.concatenate(diag, 0)


def reduce_y_kernel(pos, own, b1, b2, b3, dk2, dv2, s0, s1, s2, s3, total):
    y_pos = pos[3]
    total[...] = own[...] + b1[...].astype(F32) + b2[...].astype(F32) + b3[...].astype(F32)
    for d, s in enumerate((s0, s1, s2, s3)):
        for base, level in ((0, dk2), (128, dv2)):
            at = 128 * d
            start = base + SEL3 * d
            s[base:base + SEL3] = (level[at:at + SEL3] + total[start:start + SEL3]).astype(s.dtype)
            s[base + SEL3:base + 128] = level[at + SEL3:at + 128].astype(s.dtype)
        start = pl.multiple_of(256 + 16 * ((y_pos - d) & 3), 16)
        s[256:272] = total[pl.ds(start, 16)].astype(s.dtype)


def mix_kernel(keep_a, keep_b, got, own, send):
    own[...] = keep_a[...] + got[0:T].astype(F32)
    send[...] = (keep_b[...] + got[T:2 * T].astype(F32)).astype(BF)


def seventh_kernel(pos, q, q_t, k, k_t, v, g, g_t, lse, delta, dq_first, dk_a, dv_a, dq_a, _s,
                   dq_out, dk_part, dv_part, dk_head, dv_head, dk, dv, dq):
    level1_backward(1, q, q_t, k, k_t, v, g, g_t, lse, delta, dk, dv, dq)
    for p, (dk_p, dv_p, dq_p) in enumerate(((dk_a, dv_a, dq_a), (dk, dv, dq))):
        cols = slice(128 * p, 128 * p + 128)
        dk_head[:, cols] = dk_p[0:SEL2]
        dv_head[:, cols] = dv_p[0:SEL2]
        first = dq_p[:, 0:128] + dq_first[cols]
        dq_t = jnp.concatenate([first, dq_p[:, 128:T]], 1) * SCALE
        later = jnp.concatenate([dk_p[SEL2:T], dv_p[SEL2:T]], 1).astype(BF)
        both = jnp.concatenate([jnp.zeros((SEL2, 256), BF), later], 0)
        both = jnp.concatenate([both, dq_t.T.astype(BF)], 1)
        even = dot(put_mat(pos[0] * NH + 2 * p, T), both)
        odd = dot(put_mat(pos[0] * NH + 2 * p + 1, T), both)
        natural = jnp.where((iota(even.shape, 1) & 127) < HD, even, odd)
        dk_part[:, cols] = natural[:, 0:128].astype(BF)
        dv_part[:, cols] = natural[:, 128:256].astype(BF)
        dq_out[:, cols] = natural[:, 256:384].astype(BF)


def last_kernel(pos, own, b1, b2, b3, dk_head, dv_head, dk_part, dv_part, mix_own, mix_got,
                dk_out, dv_out, w_out, mixed_out):
    total = own[...] + b1[...].astype(F32) + b2[...].astype(F32) + b3[...].astype(F32)
    ks = (total[0:128] + dk_head[...]).astype(BF)
    vs = (total[128:256] + dv_head[...]).astype(BF)
    w_out[...] = total[256:272].T
    mats = [put_mat(pos[0] * NH + m, SEL2) for m in range(NH)]
    ks, vs = per_head_rows(mats, [ks, vs])
    dk_out[...] = (ks + dk_part[...].astype(F32)).astype(BF)
    dv_out[...] = (vs + dv_part[...].astype(F32)).astype(BF)
    mixed_out[...] = (mix_own[...] + mix_got[...].astype(F32)).astype(BF)


def call(kernel, outs, *args, us=5, scratch=()):
    def spec(arg):
        return pl.BlockSpec(memory_space=pltpu.SMEM if arg.dtype == jnp.int32 else pltpu.VMEM)

    return pl.pallas_call(
        kernel,
        out_shape=[jax.ShapeDtypeStruct(shape, dtype) for shape, dtype in outs],
        in_specs=[spec(a) for a in args],
        out_specs=[pl.BlockSpec(memory_space=pltpu.VMEM)] * len(outs),
        scratch_shapes=scratch,
        compiler_params=pltpu.CompilerParams(vmem_limit_bytes=40 * 2 ** 20),
        cost_estimate=pl.CostEstimate(flops=us * 500_000_000, bytes_accessed=us * 1_000_000, transcendentals=0),
        name=kernel.__name__,
    )(*args)


def step(stride, shift):
    pairs = []
    for s in range(64):
        at = s // stride % 4
        pairs.append((s, s + ((at + shift) % 4 - at) * stride))
    return pairs


def spread(block, stride):
    return [block] + [lax.ppermute(block, "seq", step(stride, d)) for d in (1, 2, 3)]


def bring(blocks, stride):
    return [blocks[0]] + [lax.ppermute(blocks[d], "seq", step(stride, -d)) for d in (1, 2, 3)]


def swap(block, mask):
    return lax.ppermute(block, "head", [(s, s ^ mask) for s in range(4)])


def body(query_act, key_act, value_act, out_weight, cotangent):
    seq = lax.axis_index("seq")
    head = lax.axis_index("head")
    pos = jnp.stack([head, seq // 16, seq // 4 % 4, seq % 4]).astype(jnp.int32)
    wide, tall, stat = (T, F), (F, T), (8, T)

    (p1,) = call(pack1_kernel, [((256, F), BF)], pos, key_act, value_act, us=2)
    kv2 = spread(p1, 1)
    cot_z = swap(cotangent, 2)
    cot_c = swap(cotangent, 1)
    cot_zc = swap(cot_z, 1)
    cots = [cotangent, cot_c, cot_z, cot_zc]

    q, q_t, k, k_t, v, m1, l1, o1 = call(
        first_kernel,
        [(wide, BF), (tall, BF), (wide, BF), (tall, BF), (wide, BF), (stat, F32), (stat, F32), (tall, F32)],
        pos, query_act, key_act, value_act, p1, us=10,
    )
    (p2,) = call(pack2_kernel, [((256, F), BF)], *kv2, us=1)
    kv3 = spread(p2, 4)
    m2, l2, o2 = call(
        second_kernel, [(stat, F32), (stat, F32), ((F, 128), F32)], *kv2, q, p2, us=6
    )
    (p3,) = call(pack3_kernel, [((256, F), BF)], *kv3, us=1)
    kv4 = spread(p3, 16)
    m, l, o, g, g_t, lse, delta, att_part = call(
        third_kernel,
        [((8, 128), F32), ((8, 128), F32), ((F, 128), F32), (wide, BF), (tall, BF), (stat, F32), (stat, F32),
         (tall, F32)],
        pos, *kv3, q, m1, l1, o1, m2, l2, o2, *cots, out_weight, p3, us=8,
    )
    lse, delta, att, dq4, *sent = call(
        fourth_kernel,
        [(stat, F32), (stat, F32), (tall, BF), ((F, 128), F32), ((512, F), F32)] + [((512, F), BF)] * 3,
        pos, *kv4, q, m, l, o, g, g_t, lse, delta, att_part, *cots, us=6,
        scratch=[pltpu.VMEM((4, T, F), BF)],
    )
    r4 = bring(sent, 16)
    send_c, keep_a, keep_b = call(
        project_kernel, [((2 * T, F), BF), (wide, F32), (wide, F32)], pos, att, out_weight, us=2
    )
    got_c = swap(send_c, 1)
    dk3, dv3, dq_first, dk_a, dv_a, dq_a = call(
        fifth_kernel,
        [(wide, F32), (wide, F32), ((F, 128), F32), ((T, 128), F32), ((T, 128), F32), ((128, T), F32)],
        *kv3, q, q_t, k, k_t, v, g, g_t, lse, delta, dq4, us=10,
    )
    *sent, _ = call(
        reduce_z_kernel, [((320, F), F32)] + [((320, F), BF)] * 3 + [((512, F), F32)],
        pos, *r4, dk3, dv3, us=1,
    )
    r3 = bring(sent, 4)
    mix_own, mix_send = call(mix_kernel, [(wide, F32), (wide, BF)], keep_a, keep_b, got_c, us=1)
    mix_got = swap(mix_send, 2)
    dk2, dv2, dq_first = call(
        sixth_kernel, [(wide, F32), (wide, F32), ((F, 128), F32)],
        *kv2, q, g, lse, delta, dq_first, sent[1], us=7,
    )
    *sent, _ = call(
        reduce_y_kernel, [((272, F), F32)] + [((272, F), BF)] * 3 + [((320, F), F32)],
        pos, *r3, dk2, dv2, us=1,
    )
    r2 = bring(sent, 1)
    query_grad, dk_part, dv_part, dk_head, dv_head, *_ = call(
        seventh_kernel,
        [(wide, BF), (wide, BF), (wide, BF), ((SEL2, F), F32), ((SEL2, F), F32),
         ((T, 128), F32), ((T, 128), F32), ((128, T), F32)],
        pos, q, q_t, k, k_t, v, g, g_t, lse, delta, dq_first, dk_a, dv_a, dq_a, sent[1], us=9,
    )
    key_grad, value_grad, weight_grad, mixed_out = call(
        last_kernel, [(wide, BF), (wide, BF), ((F, 16), F32), (wide, BF)],
        pos, *r2, dk_head, dv_head, dk_part, dv_part, mix_own, mix_got, us=2,
    )
    return mixed_out, query_grad, key_grad, value_grad, weight_grad


def solution(mesh):
    rows = P("seq", "head")
    return jax.shard_map(
        body,
        mesh=mesh,
        in_specs=(rows, rows, rows, P("head", None), rows),
        out_specs=(rows, rows, rows, rows, P("head", "seq")),
        check_vma=False,
    )
```

time: 1570 us -> 103 us (0.07)
  waiting for transfers between devices: 1070 us -> 37 us
  blocking collectives: 196 us -> 0 us
  local copies, waits for them, and re-layouts: 190 us -> 2.59 us
  matrix products: 34.5 us -> 0 us
  other arithmetic: 32.5 us -> 0.08 us
  Pallas kernels: 0 us -> 24.4 us
  starting transfers between devices: 17.7 us -> 36.7 us
  between operations: 17.2 us -> 0.81 us
    unnamed x5 -> x0, waiting for transfers between devices: 649 us -> none
    reduce_scatter x2 -> x0, waiting for transfers between devices: 408 us -> none  [the longest x1 386 us: body(): lax.psum_scatter(weight_term, 'seq', scatter_dimension=1, tiled=True)]
    all_gather x1 -> x0, blocking collectives: 196 us -> none  [body(): gathered.append(lax.all_gather(levels[3][4], 'seq', axis=1, tiled=True))]
    dynamic_slice x76 -> x0, local copies, waits for them, and re-layouts: 51.9 us -> none  [pick_rows(): lax.dynamic_index_in_dim(blocked[:, :, member], offsets[member], 1, False)]
    broadcast_in_dim x77 -> x0, local copies, waits for them, and re-layouts: 50.5 us -> none  [spread_rows(): widened = jnp.where(chosen, picked[:, None], filler)]
    dot_general x27 -> x0, matrix products: 34.5 us -> none  [the longest x4 6.88 us: backward_block(): jnp.einsum('ihd,khd->hik', grad_rows, value_rows, preferred_element_type=...]
    pallas_call x0 -> x15, Pallas kernels: none -> 24.4 us  [call(): pl.pallas_call(kernel, out_shape=[jax.ShapeDtypeStruct(shape, dtype) for...]
    ppermute x12 -> x23, waiting for transfers between devices: 13.4 us -> 37 us  [the longest x9 18.7 us: bring(): lax.ppermute(blocks[d], 'seq', step(stride, -d))]
  transfers between devices with their start and end apart: 16 -> 23, of which waited for: 10 -> 15; matrix products, arithmetic and copies ran while one was open for 12% -> 0% of each run, Pallas kernels for 0% -> 19%
where the time goes in v1:
time: 103 us; the launch traced here: 102 us
  waiting for transfers between devices  37 us (36%)
  starting transfers between devices  36.7 us (36%)
  Pallas kernels  24.4 us (24%)
  local copies, waits for them, and re-layouts  2.59 us (3%)
    pallas_call x15, Pallas kernels, call(): pl.pallas_call(kernel, out_shape=[jax.ShapeDtypeStruct(shape, dtype) for...  24.4 us
    ppermute x9, waiting for transfers between devices, bring(): lax.ppermute(blocks[d], 'seq', step(stride, -d))  18.7 us
    ppermute x9, starting transfers between devices, spread(): lax.ppermute(block, 'seq', step(stride, d))  18.5 us
    ppermute x9, starting transfers between devices, bring(): lax.ppermute(blocks[d], 'seq', step(stride, -d))  16.7 us
    ppermute x9, waiting for transfers between devices, spread(): lax.ppermute(block, 'seq', step(stride, d))  16 us
    unnamed x11, local copies, waits for them, and re-layouts  2.59 us
    ppermute x5, waiting for transfers between devices, swap(): return lax.ppermute(block, 'head', [(s, s ^ mask) for s in range(4)])  2.38 us
  transfers between devices with their start and end apart: 23, of which 15 were waited for; matrix products, arithmetic and copies ran while one was open for 0% of the time, Pallas kernels for 19%

profile of v1, /device:TPU:32, one launch (start us, length us, event | category | flops | bytes accessed | tf_op | source)
XLA Modules:
  0.0 101.6 jit_solution(13521188094337031612)
XLA Ops:
  3.5 3.1 %collective-permute-start.2 = (bf16[256,256]{1,0:T(8,128)(2,1)S(1)}, bf16[256,256]{1,0:T(8,128)(2,1)S(1)}, u32[]{:S(2)}, u32[]{:S(2)}) collective-permute-start(bf16[256,256]{1,0:T(8,128)(2,1)S(1)} %pack1_kernel.1.a0._p1), channel_id=1, source_target_pairs={{0,12},{4,0},{8,4},{12,8},{16,28},{20,16},{24,20},{28,24},{32,44},... | collective-permute-start | bytes 393224 | tf_op jit(solution)/shard_map/ppermute | solution.py:412
  8.4 5.0 %first_kernel.1 = (bf16[512,256]{1,0:T(8,128)(2,1)S(1)}, bf16[256,512]{1,0:T(8,128)(2,1)S(1)}, bf16[512,256]{1,0:T(8,128)(2,1)S(1)}, bf16[256,512]{1,0:T(8,128)(...) custom-call(s32[4]{0:T(128)S(1)} %pad_add_fusion.pos, ...), custom_call_target="tpu_custom_call" | custom-call | flops 5000000000 | bytes 10000000 | tf_op jit(solution)/shard_map/first_kernel/pallas_call | solution.py:391
  13.4 1.1 %collective-permute-done.1.a2 = bf16[256,256]{1,0:T(8,128)(2,1)S(1)} collective-permute-done((bf16[256,256]{1,0:T(8,128)(2,1)S(1)}, bf16[256,256]{1,0:T(8,128)(2,1)S(1)}, u32[]{:S(2)}, u32[]{:S(2)}) %collective-permute-start.1) | collective-permute-done | bytes 131104 | tf_op jit(solution)/shard_map/ppermute | solution.py:412
  14.5 1.4 %collective-permute-done.a1 = bf16[256,256]{1,0:T(8,128)(2,1)S(1)} collective-permute-done((bf16[256,256]{1,0:T(8,128)(2,1)S(1)}, bf16[256,256]{1,0:T(8,128)(2,1)S(1)}, u32[]{:S(2)}, u32[]{:S(2)}) %collective-permute-start) | collective-permute-done | bytes 131104 | tf_op jit(solution)/shard_map/ppermute | solution.py:412
  15.9 5.5 %collective-permute-start.5 = (bf16[256,256]{1,0:T(8,128)(2,1)S(1)}, bf16[256,256]{1,0:T(8,128)(2,1)S(1)}, u32[]{:S(2)}, u32[]{:S(2)}) collective-permute-start(bf16[256,256]{1,0:T(8,128)(2,1)S(1)} %pack2_kernel.1.a0._p2), channel_id=1, source_target_pairs={{0,48},{4,52},{8,56},{12,60},{16,0},{20,4},{24,8},{28,12},{32,16},... | collective-permute-start | bytes 393224 | tf_op jit(solution)/shard_map/ppermute | solution.py:412
  21.4 1.4 %collective-permute-start.4 = (bf16[256,256]{1,0:T(8,128)(2,1)S(1)}, bf16[256,256]{1,0:T(8,128)(2,1)S(1)}, u32[]{:S(2)}, u32[]{:S(2)}) collective-permute-start(bf16[256,256]{1,0:T(8,128)(2,1)S(1)} %pack2_kernel.1.a0._p2), channel_id=1, source_target_pairs={{0,32},{4,36},{8,40},{12,44},{16,48},{20,52},{24,56},{28,60},{32,0... | collective-permute-start | bytes 393224 | tf_op jit(solution)/shard_map/ppermute | solution.py:412
  22.8 2.4 %collective-permute-start.3 = (bf16[256,256]{1,0:T(8,128)(2,1)S(1)}, bf16[256,256]{1,0:T(8,128)(2,1)S(1)}, u32[]{:S(2)}, u32[]{:S(2)}) collective-permute-start(bf16[256,256]{1,0:T(8,128)(2,1)S(1)} %pack2_kernel.1.a0._p2), channel_id=1, source_target_pairs={{0,16},{4,20},{8,24},{12,28},{16,32},{20,36},{24,40},{28,44},{32,4... | collective-permute-start | bytes 393224 | tf_op jit(solution)/shard_map/ppermute | solution.py:412
  26.1 1.2 %collective-permute-done.5.a3 = bf16[256,256]{1,0:T(8,128)(2,1)S(1)} collective-permute-done((bf16[256,256]{1,0:T(8,128)(2,1)S(1)}, bf16[256,256]{1,0:T(8,128)(2,1)S(1)}, u32[]{:S(2)}, u32[]{:S(2)}) %collective-permute-start.5) | collective-permute-done | bytes 131104 | tf_op jit(solution)/shard_map/ppermute | solution.py:412
  27.3 7.5 %collective-permute-done.4.a2 = bf16[256,256]{1,0:T(8,128)(2,1)S(1)} collective-permute-done((bf16[256,256]{1,0:T(8,128)(2,1)S(1)}, bf16[256,256]{1,0:T(8,128)(2,1)S(1)}, u32[]{:S(2)}, u32[]{:S(2)}) %collective-permute-start.4) | collective-permute-done | bytes 131104 | tf_op jit(solution)/shard_map/ppermute | solution.py:412
  35.3 2.8 %collective-permute-start.8 = (bf16[256,256]{1,0:T(8,128)(2,1)S(1)}, bf16[256,256]{1,0:T(8,128)(2,1)S(1)}, u32[]{:S(2)}, u32[]{:S(2)}) collective-permute-start(bf16[256,256]{1,0:T(8,128)(2,1)S(1)} %pack3_kernel.1._p3.a0), channel_id=1, source_target_pairs={{0,192},{4,196},{8,200},{12,204},{16,208},{20,212},{24,216},{28,22... | collective-permute-start | bytes 393224 | tf_op jit(solution)/shard_map/ppermute | solution.py:412
  39.9 2.9 %third_kernel.1 = (f32[8,128]{1,0:T(8,128)S(1)}, f32[8,128]{1,0:T(8,128)S(1)}, f32[256,128]{1,0:T(8,128)S(1)}, bf16[512,256]{1,0:T(8,128)(2,1)S(1)}, bf16[256,51...) custom-call(s32[4]{0:T(128)S(1)} %pad_add_fusion.pos, ...), custom_call_target="tpu_custom_call" | custom-call | flops 4000000000 | bytes 8000000 | tf_op jit(solution)/shard_map/third_kernel/pallas_call | solution.py:391
  43.4 2.3 %collective-permute-done.7.a2 = bf16[256,256]{1,0:T(8,128)(2,1)S(1)} collective-permute-done((bf16[256,256]{1,0:T(8,128)(2,1)S(1)}, bf16[256,256]{1,0:T(8,128)(2,1)S(1)}, u32[]{:S(2)}, u32[]{:S(2)}) %collective-permute-start.7) | collective-permute-done | bytes 131104 | tf_op jit(solution)/shard_map/ppermute | solution.py:412
  45.7 1.3 %collective-permute-done.6.a1 = bf16[256,256]{1,0:T(8,128)(2,1)S(1)} collective-permute-done((bf16[256,256]{1,0:T(8,128)(2,1)S(1)}, bf16[256,256]{1,0:T(8,128)(2,1)S(1)}, u32[]{:S(2)}, u32[]{:S(2)}) %collective-permute-start.6) | collective-permute-done | bytes 131104 | tf_op jit(solution)/shard_map/ppermute | solution.py:412
  47.0 2.2 %fourth_kernel.1 = (f32[8,512]{1,0:T(8,128)S(1)}, f32[8,512]{1,0:T(8,128)S(1)}, bf16[256,512]{1,0:T(8,128)(2,1)S(1)}, f32[256,128]{1,0:T(8,128)S(1)}, f32[512,25...) custom-call(s32[4]{0:T(128)S(1)} %pad_add_fusion.pos, ...), custom_call_target="tpu_custom_call" | custom-call | flops 3000000000 | bytes 6000000 | tf_op jit(solution)/shard_map/fourth_kernel/pallas_call | solution.py:391
  51.6 1.0 %project_kernel.1 = (bf16[1024,256]{1,0:T(8,128)(2,1)S(1)}, f32[512,256]{1,0:T(8,128)S(1)}, f32[512,256]{1,0:T(8,128)S(1)}) custom-call(s32[4]{0:T(128)S(1)} %pad_add_fusion.pos, bf16[256,512]{1,0:T(8,128)(2,1)S(1)} %get-tuple-element.110.att, bf16[256,1024]{1,0:T(8,128)(2,1)S(1)} %copy-done), custom_call_target="tpu_custom_call" | custom-call | flops 1000000000 | bytes 2000000 | tf_op jit(solution)/shard_map/project_kernel/pallas_call | solution.py:391
  52.7 1.8 %fifth_kernel.1 = (f32[512,256]{1,0:T(8,128)S(1)}, f32[512,256]{1,0:T(8,128)S(1)}, f32[256,128]{1,0:T(8,128)S(1)}, f32[512,128]{1,0:T(8,128)S(1)}, f32[512,128]{1,0:T(8,128)S(1)}, /*index=5*/f32[128,512]{1,0:T(8,128)S(1)}) custom-call(bf16[256,256]{1,0:T(8,128)(2,1)S(1)} %pack2_kernel.1.a0._p2, bf16[256,256]{1,0:T(8,128)(2,1)S(1)} %collective-permute-done.3.a1, ...), custom_call_target="tpu_custom_call" | custom-call | flops 5000000000 | bytes 10000000 | tf_op jit(solution)/shard_map/fifth_kernel/pallas_call | solution.py:391
  54.5 4.1 %collective-permute-done.12.b1 = bf16[512,256]{1,0:T(8,128)(2,1)S(1)} collective-permute-done((bf16[512,256]{1,0:T(8,128)(2,1)S(1)}, bf16[512,256]{1,0:T(8,128)(2,1)S(1)}, u32[]{:S(2)}, u32[]{:S(2)}) %collective-permute-start.12) | collective-permute-done | bytes 262176 | tf_op jit(solution)/shard_map/ppermute | solution.py:416
  58.6 2.1 %collective-permute-done.13.b2 = bf16[512,256]{1,0:T(8,128)(2,1)S(1)} collective-permute-done((bf16[512,256]{1,0:T(8,128)(2,1)S(1)}, bf16[512,256]{1,0:T(8,128)(2,1)S(1)}, u32[]{:S(2)}, u32[]{:S(2)}) %collective-permute-start.13) | collective-permute-done | bytes 262176 | tf_op jit(solution)/shard_map/ppermute | solution.py:416
  60.7 3.4 %collective-permute-done.14.b3 = bf16[512,256]{1,0:T(8,128)(2,1)S(1)} collective-permute-done((bf16[512,256]{1,0:T(8,128)(2,1)S(1)}, bf16[512,256]{1,0:T(8,128)(2,1)S(1)}, u32[]{:S(2)}, u32[]{:S(2)}) %collective-permute-start.14) | collective-permute-done | bytes 262176 | tf_op jit(solution)/shard_map/ppermute | solution.py:416
  64.1 1.5 %reduce_z_kernel.1 = (f32[320,256]{1,0:T(8,128)S(1)}, bf16[320,256]{1,0:T(8,128)(2,1)S(1)}, bf16[320,256]{1,0:T(8,128)(2,1)S(1)}, bf16[320,256]{1,0:T(8,128)(2,1)S(1)}, f32[512,256]{1,0:T(8,128)}) custom-call(s32[4]{0:T(128)S(1)} %pad_add_fusion.pos, f32[512,256]{1,0:T(8,128)S(1)} %get-tuple-element.78.own, bf16[512,256]{1,0:T(8,128)(2,1)S(1)} %collective-permute-done.12.b1, ...), custom_call_target="tpu_custom_call" | custom-call | flops 500000000 | bytes 1000000 | tf_op jit(solution)/shard_map/reduce_z_kernel/pallas_call | solution.py:391
  65.6 5.6 %collective-permute-start.16 = (bf16[320,256]{1,0:T(8,128)(2,1)S(1)}, bf16[320,256]{1,0:T(8,128)(2,1)S(1)}, u32[]{:S(2)}, u32[]{:S(2)}) collective-permute-start(bf16[320,256]{1,0:T(8,128)(2,1)S(1)} %get-tuple-element.93), channel_id=1, source_target_pairs={{0,32},{4,36},{8,40},{12,44},{16,48},{20,52},{24,56},{28,60},{32,0... | collective-permute-start | bytes 491528 | tf_op jit(solution)/shard_map/ppermute | solution.py:416
  72.3 3.1 %collective-permute-start.15 = (bf16[320,256]{1,0:T(8,128)(2,1)S(1)}, bf16[320,256]{1,0:T(8,128)(2,1)S(1)}, u32[]{:S(2)}, u32[]{:S(2)}) collective-permute-start(bf16[320,256]{1,0:T(8,128)(2,1)S(1)} %get-tuple-element.92._s), channel_id=1, source_target_pairs={{0,48},{4,52},{8,56},{12,60},{16,0},{20,4},{24,8},{28,12},{32,16},... | collective-permute-start | bytes 491528 | tf_op jit(solution)/shard_map/ppermute | solution.py:416
  76.4 3.9 %collective-permute-done.16.b2 = bf16[320,256]{1,0:T(8,128)(2,1)S(1)} collective-permute-done((bf16[320,256]{1,0:T(8,128)(2,1)S(1)}, bf16[320,256]{1,0:T(8,128)(2,1)S(1)}, u32[]{:S(2)}, u32[]{:S(2)}) %collective-permute-start.16) | collective-permute-done | bytes 163872 | tf_op jit(solution)/shard_map/ppermute | solution.py:416
  80.3 2.7 %collective-permute-done.17.b3 = bf16[320,256]{1,0:T(8,128)(2,1)S(1)} collective-permute-done((bf16[320,256]{1,0:T(8,128)(2,1)S(1)}, bf16[320,256]{1,0:T(8,128)(2,1)S(1)}, u32[]{:S(2)}, u32[]{:S(2)}) %collective-permute-start.17) | collective-permute-done | bytes 163872 | tf_op jit(solution)/shard_map/ppermute | solution.py:416
  83.0 2.5 %collective-permute-done.15.b1 = bf16[320,256]{1,0:T(8,128)(2,1)S(1)} collective-permute-done((bf16[320,256]{1,0:T(8,128)(2,1)S(1)}, bf16[320,256]{1,0:T(8,128)(2,1)S(1)}, u32[]{:S(2)}, u32[]{:S(2)}) %collective-permute-start.15) | collective-permute-done | bytes 163872 | tf_op jit(solution)/shard_map/ppermute | solution.py:416
  85.5 1.4 %reduce_y_kernel.1 = (f32[272,256]{1,0:T(8,128)S(1)}, bf16[272,256]{1,0:T(8,128)(2,1)S(1)}, bf16[272,256]{1,0:T(8,128)(2,1)S(1)}, bf16[272,256]{1,0:T(8,128)(2,1)S(1)}, f32[320,256]{1,0:T(8,128)}) custom-call(s32[4]{0:T(128)S(1)} %pad_add_fusion.pos, f32[320,256]{1,0:T(8,128)S(1)} %get-tuple-element.91.own, bf16[320,256]{1,0:T(8,128)(2,1)S(1)} %collective-permute-done.15.b1, ...), custom_call_target="tpu_custom_call" | custom-call | flops 500000000 | bytes 1000000 | tf_op jit(solution)/shard_map/reduce_y_kernel/pallas_call | solution.py:391
  86.8 1.4 %collective-permute-start.19 = (bf16[272,256]{1,0:T(8,128)(2,1)S(1)}, bf16[272,256]{1,0:T(8,128)(2,1)S(1)}, u32[]{:S(2)}, u32[]{:S(2)}) collective-permute-start(bf16[272,256]{1,0:T(8,128)(2,1)S(1)} %get-tuple-element.100), channel_id=1, source_target_pairs={{0,8},{4,12},{8,0},{12,4},{16,24},{20,28},{24,16},{28,20},{32,40},... | collective-permute-start | bytes 417800 | tf_op jit(solution)/shard_map/ppermute | solution.py:416
  89.1 2.4 %collective-permute-start.18 = (bf16[272,256]{1,0:T(8,128)(2,1)S(1)}, bf16[272,256]{1,0:T(8,128)(2,1)S(1)}, u32[]{:S(2)}, u32[]{:S(2)}) collective-permute-start(bf16[272,256]{1,0:T(8,128)(2,1)S(1)} %get-tuple-element.99._s), channel_id=1, source_target_pairs={{0,12},{4,0},{8,4},{12,8},{16,28},{20,16},{24,20},{28,24},{32,44},... | collective-permute-start | bytes 417800 | tf_op jit(solution)/shard_map/ppermute | solution.py:416
  91.6 1.3 %collective-permute-start.22 = (bf16[512,256]{1,0:T(8,128)(2,1)S(1)}, bf16[512,256]{1,0:T(8,128)(2,1)S(1)}, u32[]{:S(2)}, u32[]{:S(2)}) collective-permute-start(bf16[512,256]{1,0:T(8,128)(2,1)S(1)} %get-tuple-element.115), channel_id=1, source_target_pairs={{0,2},{1,3},{2,0},{3,1},{4,6},{5,7},{6,4},{7,5},{8,10},{9,11},{10,... | collective-permute-start | bytes 786440 | tf_op jit(solution)/shard_map/ppermute | solution.py:420
  92.8 3.8 %seventh_kernel.1 = (bf16[512,256]{1,0:T(8,128)(2,1)}, bf16[512,256]{1,0:T(8,128)(2,1)S(1)}, bf16[512,256]{1,0:T(8,128)(2,1)S(1)}, f32[128,256]{1,0:T(8,128)S(1)...) custom-call(s32[4]{0:T(128)S(1)} %pad_add_fusion.pos, ...), custom_call_target="tpu_custom_call" | custom-call | flops 4499999744 | bytes 9000000 | tf_op jit(solution)/shard_map/seventh_kernel/pallas_call | solution.py:391
  96.6 2.4 %collective-permute-done.22.mix_got = bf16[512,256]{1,0:T(8,128)(2,1)S(1)} collective-permute-done((bf16[512,256]{1,0:T(8,128)(2,1)S(1)}, bf16[512,256]{1,0:T(8,128)(2,1)S(1)}, u32[]{:S(2)}, u32[]{:S(2)}) %collective-permute-start.22) | collective-permute-done | bytes 262176 | tf_op jit(solution)/shard_map/ppermute | solution.py:420
  99.0 1.9 %last_kernel.1 = (bf16[512,256]{1,0:T(8,128)(2,1)}, bf16[512,256]{1,0:T(8,128)(2,1)}, f32[256,16]{1,0:T(8,128)S(1)}, bf16[512,256]{1,0:T(8,128)(2,1)}) custom-call(s32[4]{0:T(128)S(1)} %pad_add_fusion.pos, f32[272,256]{1,0:T(8,128)S(1)} %get-tuple-element.98.own, bf16[272,256]{1,0:T(8,128)(2,1)S(1)} %collective-permute-done.18.b1, ...), custom_call_target="tpu_custom_call" | custom-call | flops 1000000000 | bytes 2000000 | tf_op jit(solution)/shard_map/last_kernel/pallas_call | solution.py:391
  (41 shorter events, 14.2 us)
Async XLA Ops:
  0.8 1.0 copy-start.1
  1.7 0.9 copy-start.2
  2.7 5.6 %copy-start.4 = (bf16[512,256]{1,0:T(8,128)(2,1)S(1)}, bf16[512,256]{1,0:T(8,128)(2,1)}, u32[]{:S(2)}) copy-start(bf16[512,256]{1,0:T(8,128)(2,1)} %c0.3) | copy-start | bytes 786436
  2.7 5.7 %copy-start.3 = (bf16[512,256]{1,0:T(8,128)(2,1)S(1)}, bf16[512,256]{1,0:T(8,128)(2,1)}, u32[]{:S(2)}) copy-start(bf16[512,256]{1,0:T(8,128)(2,1)} %q.1) | copy-start | bytes 786436
  3.5 9.8 %collective-permute-start.2 = (bf16[256,256]{1,0:T(8,128)(2,1)S(1)}, bf16[256,256]{1,0:T(8,128)(2,1)S(1)}, u32[]{:S(2)}, u32[]{:S(2)}) collective-permute-start(bf16[256,256]{1,0:T(8,128)(2,1)S(1)} %pack1_kernel.1.a0._p1), channel_id=1, source_target_pairs={{0,12},{4,0},{8,4},{12,8},{16,28},{20,16},{24,20},{28,24},{32,44},... | collective-permute-start | bytes 393224 | tf_op jit(solution)/shard_map/ppermute | solution.py:412
  6.6 7.9 %collective-permute-start.1 = (bf16[256,256]{1,0:T(8,128)(2,1)S(1)}, bf16[256,256]{1,0:T(8,128)(2,1)S(1)}, u32[]{:S(2)}, u32[]{:S(2)}) collective-permute-start(bf16[256,256]{1,0:T(8,128)(2,1)S(1)} %pack1_kernel.1.a0._p1), channel_id=1, source_target_pairs={{0,8},{4,12},{8,0},{12,4},{16,24},{20,28},{24,16},{28,20},{32,40},... | collective-permute-start | bytes 393224 | tf_op jit(solution)/shard_map/ppermute | solution.py:412
  7.3 8.6 %collective-permute-start = (bf16[256,256]{1,0:T(8,128)(2,1)S(1)}, bf16[256,256]{1,0:T(8,128)(2,1)S(1)}, u32[]{:S(2)}, u32[]{:S(2)}) collective-permute-start(bf16[256,256]{1,0:T(8,128)(2,1)S(1)} %pack1_kernel.1.a0._p1), channel_id=1, source_target_pairs={{0,4},{4,8},{8,12},{12,0},{16,20},{20,24},{24,28},{28,16},{32,36},... | collective-permute-start | bytes 393224 | tf_op jit(solution)/shard_map/ppermute | solution.py:412
  8.2 17.0 %collective-permute-start.10 = (bf16[512,256]{1,0:T(8,128)(2,1)S(1)}, bf16[512,256]{1,0:T(8,128)(2,1)S(1)}, u32[]{:S(2)}, u32[]{:S(2)}) collective-permute-start(bf16[512,256]{1,0:T(8,128)(2,1)S(1)} %copy-done.4), channel_id=1, source_target_pairs={{0,2},{1,3},{2,0},{3,1},{4,6},{5,7},{6,4},{7,5},{8,10},{9,11},{10,... | collective-permute-start | bytes 786440 | tf_op jit(solution)/shard_map/ppermute | solution.py:420
  8.4 31.5 %collective-permute-start.9 = (bf16[512,256]{1,0:T(8,128)(2,1)S(1)}, bf16[512,256]{1,0:T(8,128)(2,1)S(1)}, u32[]{:S(2)}, u32[]{:S(2)}) collective-permute-start(bf16[512,256]{1,0:T(8,128)(2,1)S(1)} %copy-done.4), channel_id=1, source_target_pairs={{0,1},{1,0},{2,3},{3,2},{4,5},{5,4},{6,7},{7,6},{8,9},{9,8},{10,11... | collective-permute-start | bytes 786440 | tf_op jit(solution)/shard_map/ppermute | solution.py:420
  15.9 11.4 %collective-permute-start.5 = (bf16[256,256]{1,0:T(8,128)(2,1)S(1)}, bf16[256,256]{1,0:T(8,128)(2,1)S(1)}, u32[]{:S(2)}, u32[]{:S(2)}) collective-permute-start(bf16[256,256]{1,0:T(8,128)(2,1)S(1)} %pack2_kernel.1.a0._p2), channel_id=1, source_target_pairs={{0,48},{4,52},{8,56},{12,60},{16,0},{20,4},{24,8},{28,12},{32,16},... | collective-permute-start | bytes 393224 | tf_op jit(solution)/shard_map/ppermute | solution.py:412
  21.4 13.4 %collective-permute-start.4 = (bf16[256,256]{1,0:T(8,128)(2,1)S(1)}, bf16[256,256]{1,0:T(8,128)(2,1)S(1)}, u32[]{:S(2)}, u32[]{:S(2)}) collective-permute-start(bf16[256,256]{1,0:T(8,128)(2,1)S(1)} %pack2_kernel.1.a0._p2), channel_id=1, source_target_pairs={{0,32},{4,36},{8,40},{12,44},{16,48},{20,52},{24,56},{28,60},{32,0... | collective-permute-start | bytes 393224 | tf_op jit(solution)/shard_map/ppermute | solution.py:412
  22.8 12.5 %collective-permute-start.3 = (bf16[256,256]{1,0:T(8,128)(2,1)S(1)}, bf16[256,256]{1,0:T(8,128)(2,1)S(1)}, u32[]{:S(2)}, u32[]{:S(2)}) collective-permute-start(bf16[256,256]{1,0:T(8,128)(2,1)S(1)} %pack2_kernel.1.a0._p2), channel_id=1, source_target_pairs={{0,16},{4,20},{8,24},{12,28},{16,32},{20,36},{24,40},{28,44},{32,4... | collective-permute-start | bytes 393224 | tf_op jit(solution)/shard_map/ppermute | solution.py:412
  25.2 14.7 %collective-permute-start.11 = (bf16[512,256]{1,0:T(8,128)(2,1)S(1)}, bf16[512,256]{1,0:T(8,128)(2,1)S(1)}, u32[]{:S(2)}, u32[]{:S(2)}) collective-permute-start(bf16[512,256]{1,0:T(8,128)(2,1)S(1)} %collective-permute-done.10.c2), channel_id=1, source_target_pairs={{0,1},{1,0},{2,3},{3,2},{4,5},{5,4},{6,7},{7,6},{8,9},{9,8},{10,11... | collective-permute-start | bytes 786440 | tf_op jit(solution)/shard_map/ppermute | solution.py:420
  26.1 13.8 %copy-start = (bf16[256,1024]{1,0:T(8,128)(2,1)S(1)}, bf16[256,1024]{1,0:T(8,128)(2,1)}, u32[]{:S(2)}) copy-start(bf16[256,1024]{1,0:T(8,128)(2,1)} %w.3) | copy-start | bytes 1572868
  35.3 8.0 %collective-permute-start.8 = (bf16[256,256]{1,0:T(8,128)(2,1)S(1)}, bf16[256,256]{1,0:T(8,128)(2,1)S(1)}, u32[]{:S(2)}, u32[]{:S(2)}) collective-permute-start(bf16[256,256]{1,0:T(8,128)(2,1)S(1)} %pack3_kernel.1._p3.a0), channel_id=1, source_target_pairs={{0,192},{4,196},{8,200},{12,204},{16,208},{20,212},{24,216},{28,22... | collective-permute-start | bytes 393224 | tf_op jit(solution)/shard_map/ppermute | solution.py:412
  38.2 7.5 %collective-permute-start.7 = (bf16[256,256]{1,0:T(8,128)(2,1)S(1)}, bf16[256,256]{1,0:T(8,128)(2,1)S(1)}, u32[]{:S(2)}, u32[]{:S(2)}) collective-permute-start(bf16[256,256]{1,0:T(8,128)(2,1)S(1)} %pack3_kernel.1._p3.a0), channel_id=1, source_target_pairs={{0,128},{4,132},{8,136},{12,140},{16,144},{20,148},{24,152},{28,15... | collective-permute-start | bytes 393224 | tf_op jit(solution)/shard_map/ppermute | solution.py:412
  39.0 8.0 %collective-permute-start.6 = (bf16[256,256]{1,0:T(8,128)(2,1)S(1)}, bf16[256,256]{1,0:T(8,128)(2,1)S(1)}, u32[]{:S(2)}, u32[]{:S(2)}) collective-permute-start(bf16[256,256]{1,0:T(8,128)(2,1)S(1)} %pack3_kernel.1._p3.a0), channel_id=1, source_target_pairs={{0,64},{4,68},{8,72},{12,76},{16,80},{20,84},{24,88},{28,92},{32,9... | collective-permute-start | bytes 393224 | tf_op jit(solution)/shard_map/ppermute | solution.py:412
  49.3 9.3 %collective-permute-start.12 = (bf16[512,256]{1,0:T(8,128)(2,1)S(1)}, bf16[512,256]{1,0:T(8,128)(2,1)S(1)}, u32[]{:S(2)}, u32[]{:S(2)}) collective-permute-start(bf16[512,256]{1,0:T(8,128)(2,1)S(1)} %get-tuple-element.79), channel_id=1, source_target_pairs={{0,192},{4,196},{8,200},{12,204},{16,208},{20,212},{24,216},{28,22... | collective-permute-start | bytes 786440 | tf_op jit(solution)/shard_map/ppermute | solution.py:416
  49.9 10.8 %collective-permute-start.13 = (bf16[512,256]{1,0:T(8,128)(2,1)S(1)}, bf16[512,256]{1,0:T(8,128)(2,1)S(1)}, u32[]{:S(2)}, u32[]{:S(2)}) collective-permute-start(bf16[512,256]{1,0:T(8,128)(2,1)S(1)} %get-tuple-element.80), channel_id=1, source_target_pairs={{0,128},{4,132},{8,136},{12,140},{16,144},{20,148},{24,152},{28,15... | collective-permute-start | bytes 786440 | tf_op jit(solution)/shard_map/ppermute | solution.py:416
  50.7 13.4 %collective-permute-start.14 = (bf16[512,256]{1,0:T(8,128)(2,1)S(1)}, bf16[512,256]{1,0:T(8,128)(2,1)S(1)}, u32[]{:S(2)}, u32[]{:S(2)}) collective-permute-start(bf16[512,256]{1,0:T(8,128)(2,1)S(1)} %get-tuple-element.81), channel_id=1, source_target_pairs={{0,64},{4,68},{8,72},{12,76},{16,80},{20,84},{24,88},{28,92},{32,9... | collective-permute-start | bytes 786440 | tf_op jit(solution)/shard_map/ppermute | solution.py:416
  52.6 38.9 %collective-permute-start.21 = (bf16[1024,256]{1,0:T(8,128)(2,1)S(1)}, bf16[1024,256]{1,0:T(8,128)(2,1)S(1)}, u32[]{:S(2)}, u32[]{:S(2)}) collective-permute-start(bf16[1024,256]{1,0:T(8,128)(2,1)S(1)} %get-tuple-element.113), channel_id=1, source_target_pairs={{0,1},{1,0},{2,3},{3,2},{4,5},{5,4},{6,7},{7,6},{8,9},{9,8},{10,11... | collective-permute-start | bytes 1572872 | tf_op jit(solution)/shard_map/ppermute | solution.py:420
  65.6 14.6 %collective-permute-start.16 = (bf16[320,256]{1,0:T(8,128)(2,1)S(1)}, bf16[320,256]{1,0:T(8,128)(2,1)S(1)}, u32[]{:S(2)}, u32[]{:S(2)}) collective-permute-start(bf16[320,256]{1,0:T(8,128)(2,1)S(1)} %get-tuple-element.93), channel_id=1, source_target_pairs={{0,32},{4,36},{8,40},{12,44},{16,48},{20,52},{24,56},{28,60},{32,0... | collective-permute-start | bytes 491528 | tf_op jit(solution)/shard_map/ppermute | solution.py:416
  71.3 11.7 %collective-permute-start.17 = (bf16[320,256]{1,0:T(8,128)(2,1)S(1)}, bf16[320,256]{1,0:T(8,128)(2,1)S(1)}, u32[]{:S(2)}, u32[]{:S(2)}) collective-permute-start(bf16[320,256]{1,0:T(8,128)(2,1)S(1)} %get-tuple-element.94), channel_id=1, source_target_pairs={{0,16},{4,20},{8,24},{12,28},{16,32},{20,36},{24,40},{28,44},{32,4... | collective-permute-start | bytes 491528 | tf_op jit(solution)/shard_map/ppermute | solution.py:416
  72.3 13.2 %collective-permute-start.15 = (bf16[320,256]{1,0:T(8,128)(2,1)S(1)}, bf16[320,256]{1,0:T(8,128)(2,1)S(1)}, u32[]{:S(2)}, u32[]{:S(2)}) collective-permute-start(bf16[320,256]{1,0:T(8,128)(2,1)S(1)} %get-tuple-element.92._s), channel_id=1, source_target_pairs={{0,48},{4,52},{8,56},{12,60},{16,0},{20,4},{24,8},{28,12},{32,16},... | collective-permute-start | bytes 491528 | tf_op jit(solution)/shard_map/ppermute | solution.py:416
  86.8 9.8 %collective-permute-start.19 = (bf16[272,256]{1,0:T(8,128)(2,1)S(1)}, bf16[272,256]{1,0:T(8,128)(2,1)S(1)}, u32[]{:S(2)}, u32[]{:S(2)}) collective-permute-start(bf16[272,256]{1,0:T(8,128)(2,1)S(1)} %get-tuple-element.100), channel_id=1, source_target_pairs={{0,8},{4,12},{8,0},{12,4},{16,24},{20,28},{24,16},{28,20},{32,40},... | collective-permute-start | bytes 417800 | tf_op jit(solution)/shard_map/ppermute | solution.py:416
  88.2 8.4 %collective-permute-start.20 = (bf16[272,256]{1,0:T(8,128)(2,1)S(1)}, bf16[272,256]{1,0:T(8,128)(2,1)S(1)}, u32[]{:S(2)}, u32[]{:S(2)}) collective-permute-start(bf16[272,256]{1,0:T(8,128)(2,1)S(1)} %get-tuple-element.101), channel_id=1, source_target_pairs={{0,4},{4,8},{8,12},{12,0},{16,20},{20,24},{24,28},{28,16},{32,36},... | collective-permute-start | bytes 417800 | tf_op jit(solution)/shard_map/ppermute | solution.py:416
  89.1 7.6 %collective-permute-start.18 = (bf16[272,256]{1,0:T(8,128)(2,1)S(1)}, bf16[272,256]{1,0:T(8,128)(2,1)S(1)}, u32[]{:S(2)}, u32[]{:S(2)}) collective-permute-start(bf16[272,256]{1,0:T(8,128)(2,1)S(1)} %get-tuple-element.99._s), channel_id=1, source_target_pairs={{0,12},{4,0},{8,4},{12,8},{16,28},{20,16},{24,20},{28,24},{32,44},... | collective-permute-start | bytes 417800 | tf_op jit(solution)/shard_map/ppermute | solution.py:416
  91.6 7.5 %collective-permute-start.22 = (bf16[512,256]{1,0:T(8,128)(2,1)S(1)}, bf16[512,256]{1,0:T(8,128)(2,1)S(1)}, u32[]{:S(2)}, u32[]{:S(2)}) collective-permute-start(bf16[512,256]{1,0:T(8,128)(2,1)S(1)} %get-tuple-element.115), channel_id=1, source_target_pairs={{0,2},{1,3},{2,0},{3,1},{4,6},{5,7},{6,4},{7,5},{8,10},{9,11},{10,... | collective-permute-start | bytes 786440 | tf_op jit(solution)/shard_map/ppermute | solution.py:420

commit v2 on v1

--- a/solution.py
+++ b/solution.py
@@ -1,3 +1,5 @@
+import functools
+
 import functools
 
 import jax
@@ -138,14 +140,21 @@
                 dk_ref[...] += dk
 
 
-def pack1_kernel(pos, k, v, out):
+def pick3_kernel(pos, k, v, out):
+    mats = [pick_mat(pos[0] * NH + m, SEL3) for m in range(NH)]
+    ks, vs = per_head_rows(mats, [k[...], v[...]])
+    out[0:SEL3] = ks.astype(BF)
+    out[SEL3:2 * SEL3] = vs.astype(BF)
+
+
+def pick2_kernel(pos, k, v, _p3, out):
     mats = [pick_mat(pos[0] * NH + m, SEL2) for m in range(NH)]
     ks, vs = per_head_rows(mats, [k[...], v[...]])
     out[0:SEL2] = ks.astype(BF)
     out[SEL2:2 * SEL2] = vs.astype(BF)
 
 
-def first_kernel(pos, q, k, v, _p1, q_out, q_t_out, k_out, k_t_out, v_out, m_out, l_out, o_out):
+def order_kernel(pos, q, k, v, _s, q_out, q_t_out, k_out, k_t_out, v_out, v_t_out):
     mats = [pick_mat(pos[0] * NH + m, T) for m in range(NH)]
     qs, ks, vs = per_head_rows(mats, [q[...], k[...], v[...]])
     qs = qs * SCALE
@@ -154,27 +163,40 @@
     k_out[...] = ks.astype(BF)
     k_t_out[...] = ks.T.astype(BF)
     v_out[...] = vs.astype(BF)
-    v_t = vs.T.astype(BF)
+    v_t_out[...] = vs.T.astype(BF)
+
+
+def first_kernel(p, q_t, k, v_t, _s, m_out, l_out, o_out):
     m_out[...] = jnp.zeros_like(m_out)
     l_out[...] = jnp.zeros_like(l_out)
-    for h in range(NH):
-        cols = slice(128 * (h // 2), 128 * (h // 2) + 128)
+    cols = slice(128 * p, 128 * p + 128)
+    for h in range(2):
+        rows_in = slice(HD * (2 * p + h), HD * (2 * p + h) + HD)
         rows = slice(HD * h, HD * h + HD)
         for c in range(2):
             lanes = slice(256 * c, 256 * c + 256)
-            peak, total, weights = soft(dot(k_out[:, cols], half_pad(q_t_out[rows, lanes], h)))
+            peak, total, weights = soft(dot(k[:, cols], half_pad(q_t[rows_in, lanes], h)))
             m_out[h:h + 1, lanes] = peak
             l_out[h:h + 1, lanes] = total
-            o_out[rows, lanes] = dot(v_t[rows, :], weights)
-
-
-def pack2_kernel(a0, a1, a2, a3, out):
-    for n, a in enumerate((a0, a1, a2, a3)):
-        out[SEL3 * n:SEL3 * n + SEL3] = a[0:SEL3]
-        out[128 + SEL3 * n:128 + SEL3 * n + SEL3] = a[SEL2:SEL2 + SEL3]
-
-
-def pack3_kernel(a0, a1, a2, a3, out):
+            o_out[rows, lanes] = dot(v_t[rows_in, :], weights)
+
+
+def pair_kernel(a, b, _s, out):
+    rows = a.shape[0]
+    out[0:rows] = a[...]
+    out[rows:2 * rows] = b[...]
+
+
+def pack3_kernel(a, b, c, cot, _s, out, cot_out):
+    cot_out[...] = cot[...]
+    for half in range(2):
+        base = SEL3 * half
+        rows = [a[base:base + SEL3], b[base:base + SEL3], c[64 + base:64 + base + SEL3], c[base:base + SEL3]]
+        for n, part in enumerate(rows):
+            out[128 * half + SEL3 * n:128 * half + SEL3 * n + SEL3] = part
+
+
+def pack4_kernel(a0, a1, a2, a3, _s, _t, out):
     for base in (0, 128):
         parts = []
         for a in (a0, a1, a2, a3):
@@ -190,8 +212,8 @@
     return keys, values
 
 
-def second_kernel(a0, a1, a2, a3, q, _p2, m_out, l_out, o_out):
-    keys, values = stack_kv((a0, a1, a2, a3))
+def second_kernel(a, b, q, m_out, l_out, o_out):
+    keys, values = stack_kv((a.at[0:256], a.at[256:512], b.at[0:256], b.at[256:512]))
     _, q_t = blocks_both(q[0:SEL2].astype(F32), SEL2)
     peak, total, wide = forward(keys, values, q_t)
     m_out[...] = jnp.broadcast_to(peak, m_out.shape)
@@ -201,7 +223,7 @@
     )
 
 
-def third_kernel(pos, a0, a1, a2, a3, q, m1, l1, o1, m2, l2, o2, c0, c1, c2, c3, w, _p3,
+def third_kernel(pos, a0, a1, a2, a3, q, m1a, l1a, o1a, m1b, l1b, o1b, m2, l2, o2, c0, c1, c2, c3, w, _p3,
                  m_out, l_out, o_out, g_out, g_t_out, lse_out, delta_out, att_out):
     here = pos[0]
     grad = None
@@ -226,7 +248,9 @@
     l_out[...] = jnp.zeros_like(l_out)
     for h in range(NH):
         rows = slice(HD * h, HD * h + HD)
-        ma, la, oa = m1[h:h + 1, 0:128], l1[h:h + 1, 0:128], o1[rows, 0:128]
+        m1, l1, o1 = ((m1a, l1a, o1a), (m1b, l1b, o1b))[h // 2]
+        one, half = slice(h % 2, h % 2 + 1), slice(HD * (h % 2), HD * (h % 2) + HD)
+        ma, la, oa = m1[one, 0:128], l1[one, 0:128], o1[half, 0:128]
         mb, lb = m2[0:1, 128 * h:128 * h + 128], l2[0:1, 128 * h:128 * h + 128]
         mc = from_lanes(m3, h, SEL3, NEG)[0:1]
         lc = from_lanes(l3, h, SEL3, 0.0)[0:1]
@@ -236,9 +260,9 @@
         m_out[h:h + 1] = top
         l_out[h:h + 1] = fa * la + fb * lb + fc * lc
         o_out[rows] = fa * oa + fb * o2[rows] + fc * oc
-        total = l1[h:h + 1, 128:T]
-        out = o1[rows, 128:T] / total
-        lse_out[h:h + 1, 128:T] = m1[h:h + 1, 128:T] + jnp.log(total)
+        total = l1[one, 128:T]
+        out = o1[half, 128:T] / total
+        lse_out[h:h + 1, 128:T] = m1[one, 128:T] + jnp.log(total)
         delta_out[h:h + 1, 128:T] = jnp.sum(g_t_out[rows, 128:T].astype(F32) * out, axis=0, keepdims=True)
         att_out[rows] = dot(out.astype(BF), mats[h][128:T])
 
@@ -287,15 +311,34 @@
         s[256:512] = term.T.astype(s.dtype)
 
 
-def project_kernel(pos, att, w, send, keep_a, keep_b):
+def project_kernel(pos, att, w, _s, send, keep_a, keep_b):
     here = pos[0]
     for r, ref in ((0, keep_a), (2, keep_b), (1, send.at[0:T]), (3, send.at[T:2 * T])):
         at = pl.multiple_of((here ^ r) * F, F)
         ref[...] = dot(att[...], w[:, pl.ds(at, F)], ((0,), (0,))).astype(ref.dtype)
 
 
-def fifth_kernel(a0, a1, a2, a3, q, q_t, k, k_t, v, g, g_t, lse, delta, dq_in,
-                 dk3, dv3, dq_first, dk, dv, dq):
+def second_back_kernel(a, b, q, g, lse, delta, dq_in, own, send, dq_first):
+    keys, values = stack_kv((a.at[0:256], a.at[256:512], b.at[0:256], b.at[256:512]))
+    q2, q2_t = blocks_both(q[0:SEL2].astype(F32), SEL2)
+    g2, g2_t = blocks_both(g[0:SEL2].astype(F32), SEL2)
+    lse2 = jnp.concatenate([lse[h:h + 1, 0:128] for h in range(NH)], 1)
+    delta2 = jnp.concatenate([delta[h:h + 1, 0:128] for h in range(NH)], 1)
+    d_keys, d_values, wide = backward(keys, values, q2, q2_t, g2, g2_t, lse2, delta2)
+    diag = [wide[HD * h:HD * h + HD, 128 * h:128 * h + 128] for h in range(NH)]
+    dq_first[...] = dq_in[...] + jnp.concatenate(diag, 0)
+    for n, (out, at) in enumerate(((own, 0), (own, 256), (send, 0), (send, 256))):
+        out[at:at + 128] = d_keys[128 * n:128 * n + 128].astype(out.dtype)
+        out[at + 128:at + 256] = d_values[128 * n:128 * n + 128].astype(out.dtype)
+
+
+def fold_kernel(own, got, keep, send):
+    keep[...] = own[0:256] + got[0:256].astype(F32)
+    send[...] = (own[256:512] + got[256:512].astype(F32)).astype(BF)
+
+
+def third_back_kernel(a0, a1, a2, a3, q, q_t, k, k_t, v, g, g_t, lse, delta, dq_in,
+                      dk3, dv3, dq_first, dk, dv, dq):
     keys, values = stack_kv((a0, a1, a2, a3))
     q3, q3_t = blocks_both(q[0:SEL3].astype(F32), SEL3)
     g3, g3_t = blocks_both(g[0:SEL3].astype(F32), SEL3)
@@ -306,8 +349,12 @@
     level1_backward(0, q, q_t, k, k_t, v, g, g_t, lse, delta, dk, dv, dq)
 
 
-def reduce_z_kernel(pos, own, b1, b2, b3, dk3, dv3, s0, s1, s2, s3, total):
-    z_pos = pos[2]
+def pair_back_kernel(q, q_t, k, k_t, v, g, g_t, lse, delta, _s, dk, dv, dq):
+    level1_backward(1, q, q_t, k, k_t, v, g, g_t, lse, delta, dk, dv, dq)
+
+
+def reduce_y_kernel(pos, own, b1, b2, b3, dk3, dv3, _s, s0, s1, s2, s3, total):
+    y_pos = pos[3]
     total[...] = own[...] + b1[...].astype(F32) + b2[...].astype(F32) + b3[...].astype(F32)
     for d, s in enumerate((s0, s1, s2, s3)):
         for base, level in ((0, dk3), (128, dv3)):
@@ -318,32 +365,19 @@
                 parts.append(level[at:at + SEL4] + total[start:start + SEL4])
                 parts.append(level[at + SEL4:at + SEL3])
             s[base:base + 128] = jnp.concatenate(parts, 0).astype(s.dtype)
-        start = pl.multiple_of(256 + 64 * ((z_pos - d) & 3), 64)
-        s[256:320] = total[pl.ds(start, 64)].astype(s.dtype)
-
-
-def sixth_kernel(a0, a1, a2, a3, q, g, lse, delta, dq_in, _s, dk2, dv2, dq_first):
-    keys, values = stack_kv((a0, a1, a2, a3))
-    q2, q2_t = blocks_both(q[0:SEL2].astype(F32), SEL2)
-    g2, g2_t = blocks_both(g[0:SEL2].astype(F32), SEL2)
-    lse2 = jnp.concatenate([lse[h:h + 1, 0:128] for h in range(NH)], 1)
-    delta2 = jnp.concatenate([delta[h:h + 1, 0:128] for h in range(NH)], 1)
-    dk2[...], dv2[...], wide = backward(keys, values, q2, q2_t, g2, g2_t, lse2, delta2)
-    diag = [wide[HD * h:HD * h + HD, 128 * h:128 * h + 128] for h in range(NH)]
-    dq_first[...] = dq_in[...] + jnp.concatenate(diag, 0)
-
-
-def reduce_y_kernel(pos, own, b1, b2, b3, dk2, dv2, s0, s1, s2, s3, total):
-    y_pos = pos[3]
+        for n in range(4):
+            start = pl.multiple_of(256 + 64 * n + 16 * ((y_pos - d) & 3), 16)
+            s[256 + 16 * n:272 + 16 * n] = total[pl.ds(start, 16)].astype(s.dtype)
+
+
+def reduce_z_kernel(pos, own, b1, b2, b3, s0, s1, s2, s3, total):
+    z_pos = pos[2]
     total[...] = own[...] + b1[...].astype(F32) + b2[...].astype(F32) + b3[...].astype(F32)
     for d, s in enumerate((s0, s1, s2, s3)):
-        for base, level in ((0, dk2), (128, dv2)):
-            at = 128 * d
-            start = base + SEL3 * d
-            s[base:base + SEL3] = (level[at:at + SEL3] + total[start:start + SEL3]).astype(s.dtype)
-            s[base + SEL3:base + 128] = level[at + SEL3:at + 128].astype(s.dtype)
-        start = pl.multiple_of(256 + 16 * ((y_pos - d) & 3), 16)
-        s[256:272] = total[pl.ds(start, 16)].astype(s.dtype)
+        s[0:SEL3] = total[SEL3 * d:SEL3 * d + SEL3].astype(s.dtype)
+        s[SEL3:2 * SEL3] = total[128 + SEL3 * d:128 + SEL3 * d + SEL3].astype(s.dtype)
+        start = pl.multiple_of(256 + 16 * (z_pos ^ d), 16)
+        s[64:80] = total[pl.ds(start, 16)].astype(s.dtype)
 
 
 def mix_kernel(keep_a, keep_b, got, own, send):
@@ -351,18 +385,22 @@
     send[...] = (keep_b[...] + got[T:2 * T].astype(F32)).astype(BF)
 
 
-def seventh_kernel(pos, q, q_t, k, k_t, v, g, g_t, lse, delta, dq_first, dk_a, dv_a, dq_a, _s,
-                   dq_out, dk_part, dv_part, dk_head, dv_head, dk, dv, dq):
-    level1_backward(1, q, q_t, k, k_t, v, g, g_t, lse, delta, dk, dv, dq)
-    for p, (dk_p, dv_p, dq_p) in enumerate(((dk_a, dv_a, dq_a), (dk, dv, dq))):
+def natural_kernel(pos, dq_first, dk_a, dv_a, dq_a, dk_b, dv_b, dq_b, own2, got2, mix_own, mix_got, _s,
+                   dq_out, dk_part, dv_part, dk_head, dv_head, mixed_out):
+    level2 = own2[...] + got2[...].astype(F32)
+    mixed_out[...] = (mix_own[...] + mix_got[...].astype(F32)).astype(BF)
+    for p, (dk, dv, dq) in enumerate(((dk_a, dv_a, dq_a), (dk_b, dv_b, dq_b))):
         cols = slice(128 * p, 128 * p + 128)
-        dk_head[:, cols] = dk_p[0:SEL2]
-        dv_head[:, cols] = dv_p[0:SEL2]
-        first = dq_p[:, 0:128] + dq_first[cols]
-        dq_t = jnp.concatenate([first, dq_p[:, 128:T]], 1) * SCALE
-        later = jnp.concatenate([dk_p[SEL2:T], dv_p[SEL2:T]], 1).astype(BF)
-        both = jnp.concatenate([jnp.zeros((SEL2, 256), BF), later], 0)
-        both = jnp.concatenate([both, dq_t.T.astype(BF)], 1)
+        dk_top = dk[0:SEL2] + level2[0:SEL2, cols]
+        dv_top = dv[0:SEL2] + level2[SEL2:2 * SEL2, cols]
+        dk_head[:, cols] = dk_top[0:SEL3]
+        dv_head[:, cols] = dv_top[0:SEL3]
+        dq_t = jnp.concatenate([dq[:, 0:128] + dq_first[cols], dq[:, 128:T]], 1) * SCALE
+        later = [
+            jnp.concatenate([jnp.zeros((SEL3, 128), F32), top[SEL3:SEL2], rest[SEL2:T]], 0)
+            for top, rest in ((dk_top, dk), (dv_top, dv))
+        ]
+        both = jnp.concatenate(later + [dq_t.T], 1).astype(BF)
         even = dot(put_mat(pos[0] * NH + 2 * p, T), both)
         odd = dot(put_mat(pos[0] * NH + 2 * p + 1, T), both)
         natural = jnp.where((iota(even.shape, 1) & 127) < HD, even, odd)
@@ -371,17 +409,15 @@
         dq_out[:, cols] = natural[:, 256:384].astype(BF)
 
 
-def last_kernel(pos, own, b1, b2, b3, dk_head, dv_head, dk_part, dv_part, mix_own, mix_got,
-                dk_out, dv_out, w_out, mixed_out):
+def last_kernel(pos, own, b1, b2, b3, dk_head, dv_head, dk_part, dv_part, dk_out, dv_out, w_out):
     total = own[...] + b1[...].astype(F32) + b2[...].astype(F32) + b3[...].astype(F32)
-    ks = (total[0:128] + dk_head[...]).astype(BF)
-    vs = (total[128:256] + dv_head[...]).astype(BF)
-    w_out[...] = total[256:272].T
-    mats = [put_mat(pos[0] * NH + m, SEL2) for m in range(NH)]
+    ks = (total[0:SEL3] + dk_head[...]).astype(BF)
+    vs = (total[SEL3:2 * SEL3] + dv_head[...]).astype(BF)
+    w_out[...] = total[64:80]
+    mats = [put_mat(pos[0] * NH + m, SEL3) for m in range(NH)]
     ks, vs = per_head_rows(mats, [ks, vs])
     dk_out[...] = (ks + dk_part[...].astype(F32)).astype(BF)
     dv_out[...] = (vs + dv_part[...].astype(F32)).astype(BF)
-    mixed_out[...] = (mix_own[...] + mix_got[...].astype(F32)).astype(BF)
 
 
 def call(kernel, outs, *args, us=5, scratch=()):
@@ -394,9 +430,9 @@
         in_specs=[spec(a) for a in args],
         out_specs=[pl.BlockSpec(memory_space=pltpu.VMEM)] * len(outs),
         scratch_shapes=scratch,
-        compiler_params=pltpu.CompilerParams(vmem_limit_bytes=40 * 2 ** 20),
+        compiler_params=pltpu.CompilerParams(vmem_limit_bytes=24 * 2 ** 20),
         cost_estimate=pl.CostEstimate(flops=us * 500_000_000, bytes_accessed=us * 1_000_000, transcendentals=0),
-        name=kernel.__name__,
+        name=getattr(kernel, "func", kernel).__name__,
     )(*args)
 
 
@@ -416,6 +452,14 @@
     return [blocks[0]] + [lax.ppermute(blocks[d], "seq", step(stride, -d)) for d in (1, 2, 3)]
 
 
+def swap_z(block, mask):
+    return lax.ppermute(block, "seq", [(s, s ^ (4 * mask)) for s in range(64)])
+
+
+def swap_y(block, mask):
+    return lax.ppermute(block, "seq", [(s, s ^ mask) for s in range(64)])
+
+
 def swap(block, mask):
     return lax.ppermute(block, "head", [(s, s ^ mask) for s in range(4)])
 
@@ -426,74 +470,86 @@
     pos = jnp.stack([head, seq // 16, seq // 4 % 4, seq % 4]).astype(jnp.int32)
     wide, tall, stat = (T, F), (F, T), (8, T)
 
-    (p1,) = call(pack1_kernel, [((256, F), BF)], pos, key_act, value_act, us=2)
-    kv2 = spread(p1, 1)
-    cot_z = swap(cotangent, 2)
-    cot_c = swap(cotangent, 1)
+    (mine3,) = call(pick3_kernel, [((64, F), BF)], pos, key_act, value_act, us=1)
+    pair_a = swap_z(mine3, 1)
+    (mine2,) = call(pick2_kernel, [((256, F), BF)], pos, key_act, value_act, mine3, us=1)
+    got2 = swap_y(mine2, 1)
+    q, q_t, k, k_t, v, v_t = call(
+        order_kernel, [(wide, BF), (tall, BF)] * 3, pos, query_act, key_act, value_act, mine2, us=3,
+    )
+    (both,) = call(pair_kernel, [((128, F), BF)], mine3, pair_a, q, us=1)
+    pair_b = swap_z(both, 3)
+    (half2,) = call(pair_kernel, [((512, F), BF)], mine2, got2, both, us=1)
+    kv2 = [half2, swap_y(half2, 3)]
+    pair_out = [(stat, F32), (stat, F32), ((128, T), F32)]
+    m1a, l1a, o1a = call(functools.partial(first_kernel, 0), pair_out, q_t, k, v_t, half2, us=2)
+    all3, cot = call(pack3_kernel, [((256, F), BF), (wide, BF)], mine3, pair_a, pair_b, cotangent, m1a, us=1)
+    kv3 = spread(all3, 1)
+    cot_z = swap(cot, 2)
+    cot_c = swap(cot, 1)
     cot_zc = swap(cot_z, 1)
-    cots = [cotangent, cot_c, cot_z, cot_zc]
-
-    q, q_t, k, k_t, v, m1, l1, o1 = call(
-        first_kernel,
-        [(wide, BF), (tall, BF), (wide, BF), (tall, BF), (wide, BF), (stat, F32), (stat, F32), (tall, F32)],
-        pos, query_act, key_act, value_act, p1, us=10,
-    )
-    (p2,) = call(pack2_kernel, [((256, F), BF)], *kv2, us=1)
-    kv3 = spread(p2, 4)
+    cots = [cot, cot_c, cot_z, cot_zc]
+    m1b, l1b, o1b = call(functools.partial(first_kernel, 1), pair_out, q_t, k, v_t, all3, us=2)
     m2, l2, o2 = call(
-        second_kernel, [(stat, F32), (stat, F32), ((F, 128), F32)], *kv2, q, p2, us=6
-    )
-    (p3,) = call(pack3_kernel, [((256, F), BF)], *kv3, us=1)
-    kv4 = spread(p3, 16)
+        second_kernel, [(stat, F32), (stat, F32), ((F, 128), F32)], *kv2, q, us=6
+    )
+    (mine4,) = call(pack4_kernel, [((256, F), BF)], *kv3, m2, m1b, us=1)
+    kv4 = spread(mine4, 16)
     m, l, o, g, g_t, lse, delta, att_part = call(
         third_kernel,
         [((8, 128), F32), ((8, 128), F32), ((F, 128), F32), (wide, BF), (tall, BF), (stat, F32), (stat, F32),
          (tall, F32)],
-        pos, *kv3, q, m1, l1, o1, m2, l2, o2, *cots, out_weight, p3, us=8,
-    )
-    lse, delta, att, dq4, *sent = call(
+        pos, *kv3, q, m1a, l1a, o1a, m1b, l1b, o1b, m2, l2, o2, *cots, out_weight, mine4, us=8,
+    )
+    lse, delta, att, dq_first, *sent = call(
         fourth_kernel,
         [(stat, F32), (stat, F32), (tall, BF), ((F, 128), F32), ((512, F), F32)] + [((512, F), BF)] * 3,
         pos, *kv4, q, m, l, o, g, g_t, lse, delta, att_part, *cots, us=6,
         scratch=[pltpu.VMEM((4, T, F), BF)],
     )
+    own2, sent2, dq_first = call(
+        second_back_kernel, [((512, F), F32), ((512, F), BF), ((F, 128), F32)],
+        *kv2, q, g, lse, delta, dq_first, us=2,
+    )
+    sent = lax.optimization_barrier((*sent, sent2))[:4]
     r4 = bring(sent, 16)
+    got2 = swap_y(sent2, 3)
     send_c, keep_a, keep_b = call(
-        project_kernel, [((2 * T, F), BF), (wide, F32), (wide, F32)], pos, att, out_weight, us=2
-    )
-    got_c = swap(send_c, 1)
+        project_kernel, [((2 * T, F), BF), (wide, F32), (wide, F32)], pos, att, out_weight, sent2, us=2
+    )
     dk3, dv3, dq_first, dk_a, dv_a, dq_a = call(
-        fifth_kernel,
+        third_back_kernel,
         [(wide, F32), (wide, F32), ((F, 128), F32), ((T, 128), F32), ((T, 128), F32), ((128, T), F32)],
-        *kv3, q, q_t, k, k_t, v, g, g_t, lse, delta, dq4, us=10,
-    )
-    *sent, _ = call(
-        reduce_z_kernel, [((320, F), F32)] + [((320, F), BF)] * 3 + [((512, F), F32)],
-        pos, *r4, dk3, dv3, us=1,
-    )
-    r3 = bring(sent, 4)
+        *kv3, q, q_t, k, k_t, v, g, g_t, lse, delta, dq_first, us=6,
+    )
+    own2, sent2 = call(fold_kernel, [((256, F), F32), ((256, F), BF)], own2, got2, us=1)
+    got2 = swap_y(sent2, 1)
+    sent = call(
+        reduce_y_kernel, [((320, F), F32)] + [((320, F), BF)] * 3, pos, *r4, dk3, dv3, got2, us=1,
+        scratch=[pltpu.VMEM((512, F), F32)],
+    )
+    r3 = bring(sent, 1)
+    got_c = swap(lax.optimization_barrier((send_c, sent[0]))[0], 1)
     mix_own, mix_send = call(mix_kernel, [(wide, F32), (wide, BF)], keep_a, keep_b, got_c, us=1)
     mix_got = swap(mix_send, 2)
-    dk2, dv2, dq_first = call(
-        sixth_kernel, [(wide, F32), (wide, F32), ((F, 128), F32)],
-        *kv2, q, g, lse, delta, dq_first, sent[1], us=7,
-    )
-    *sent, _ = call(
-        reduce_y_kernel, [((272, F), F32)] + [((272, F), BF)] * 3 + [((320, F), F32)],
-        pos, *r3, dk2, dv2, us=1,
-    )
-    r2 = bring(sent, 1)
-    query_grad, dk_part, dv_part, dk_head, dv_head, *_ = call(
-        seventh_kernel,
-        [(wide, BF), (wide, BF), (wide, BF), ((SEL2, F), F32), ((SEL2, F), F32),
-         ((T, 128), F32), ((T, 128), F32), ((128, T), F32)],
-        pos, q, q_t, k, k_t, v, g, g_t, lse, delta, dq_first, dk_a, dv_a, dq_a, sent[1], us=9,
-    )
-    key_grad, value_grad, weight_grad, mixed_out = call(
-        last_kernel, [(wide, BF), (wide, BF), ((F, 16), F32), (wide, BF)],
-        pos, *r2, dk_head, dv_head, dk_part, dv_part, mix_own, mix_got, us=2,
-    )
-    return mixed_out, query_grad, key_grad, value_grad, weight_grad
+    dk_b, dv_b, dq_b = call(
+        pair_back_kernel, [((T, 128), F32), ((T, 128), F32), ((128, T), F32)],
+        q, q_t, k, k_t, v, g, g_t, lse, delta, sent[1], us=6,
+    )
+    sent = call(
+        reduce_z_kernel, [((80, F), F32)] + [((80, F), BF)] * 3, pos, *r3, us=1,
+        scratch=[pltpu.VMEM((320, F), F32)],
+    )
+    rz = [sent[0]] + [swap_z(sent[n], n) for n in (1, 2, 3)]
+    query_grad, dk_part, dv_part, dk_head, dv_head, mixed_out = call(
+        natural_kernel, [(wide, BF), (wide, BF), (wide, BF), ((SEL3, F), F32), ((SEL3, F), F32), (wide, BF)],
+        pos, dq_first, dk_a, dv_a, dq_a, dk_b, dv_b, dq_b, own2, got2, mix_own, mix_got, sent[1], us=6,
+    )
+    key_grad, value_grad, weight_grad = call(
+        last_kernel, [(wide, BF), (wide, BF), ((16, F), F32)],
+        pos, *rz, dk_head, dv_head, dk_part, dv_part, us=2,
+    )
+    return mixed_out, query_grad, key_grad, value_grad, weight_grad.T
 
 
 def solution(mesh):

time: 103 us -> 87.2 us (0.85)
  waiting for transfers between devices: 37 us -> 22.3 us
    ppermute x0 -> x9, starting transfers between devices: none -> 21.4 us  [the longest x5 13.6 us: swap_z(): return lax.ppermute(block, 'seq', [(s, s ^ 4 * mask) for s in range(64)])]
    ppermute x9 -> x6, starting transfers between devices: 18.5 us -> 7.32 us  [spread(): lax.ppermute(block, 'seq', step(stride, d))]
    ppermute x9 -> x6, waiting for transfers between devices: 16 us -> 4.9 us  [spread(): lax.ppermute(block, 'seq', step(stride, d))]
    ppermute x9 -> x6, starting transfers between devices: 16.7 us -> 5.64 us  [bring(): lax.ppermute(blocks[d], 'seq', step(stride, -d))]
    ppermute x9 -> x6, waiting for transfers between devices: 18.7 us -> 10.9 us  [bring(): lax.ppermute(blocks[d], 'seq', step(stride, -d))]
    ppermute x0 -> x9, waiting for transfers between devices: none -> 6.52 us  [the longest x4 5.8 us: swap_y(): return lax.ppermute(block, 'seq', [(s, s ^ mask) for s in range(64)])]
    ppermute x5, waiting for transfers between devices: 2.38 us -> 0.01 us  [swap(): return lax.ppermute(block, 'head', [(s, s ^ mask) for s in range(4)])]
    ppermute x5, starting transfers between devices: 1.5 us -> 2.81 us  [swap(): return lax.ppermute(block, 'head', [(s, s ^ mask) for s in range(4)])]
  transfers between devices with their start and end apart: 23 -> 26, of which waited for: 15 -> 11; matrix products, arithmetic and copies ran while one was open for 0% -> 0% of each run, Pallas kernels for 19% -> 21%
where the time goes in v2:
time: 87.2 us; the launch traced here: 86.8 us
  starting transfers between devices  37.1 us (43%)
  Pallas kernels  24.5 us (28%)
  waiting for transfers between devices  22.3 us (26%)
  local copies, waits for them, and re-layouts  1.93 us (2%)
  between operations  0.89 us (1%)
    pallas_call x22, Pallas kernels, call(): pl.pallas_call(kernel, out_shape=[jax.ShapeDtypeStruct(shape, dtype) for...  24.5 us
    ppermute x5, starting transfers between devices, swap_z(): return lax.ppermute(block, 'seq', [(s, s ^ 4 * mask) for s in range(64)])  13.6 us
    ppermute x6, waiting for transfers between devices, bring(): lax.ppermute(blocks[d], 'seq', step(stride, -d))  10.9 us
    ppermute x4, starting transfers between devices, swap_y(): return lax.ppermute(block, 'seq', [(s, s ^ mask) for s in range(64)])  7.76 us
    ppermute x6, starting transfers between devices, spread(): lax.ppermute(block, 'seq', step(stride, d))  7.32 us
    ppermute x4, waiting for transfers between devices, swap_y(): return lax.ppermute(block, 'seq', [(s, s ^ mask) for s in range(64)])  5.8 us
    ppermute x6, starting transfers between devices, bring(): lax.ppermute(blocks[d], 'seq', step(stride, -d))  5.64 us
    ppermute x6, waiting for transfers between devices, spread(): lax.ppermute(block, 'seq', step(stride, d))  4.9 us
  transfers between devices with their start and end apart: 26, of which 11 were waited for; matrix products, arithmetic and copies ran while one was open for 0% of the time, Pallas kernels for 21%

profile of v2, /device:TPU:32, one launch (start us, length us, event | category | flops | bytes accessed | tf_op | source)
XLA Modules:
  0.0 86.8 jit_solution(3461602506625041227)
XLA Ops:
  3.5 3.4 %collective-permute-start = (bf16[64,256]{1,0:T(8,128)(2,1)S(1)}, bf16[64,256]{1,0:T(8,128)(2,1)S(1)}, u32[]{:S(2)}, u32[]{:S(2)}) collective-permute-start(bf16[64,256]{1,0:T(8,128)(2,1)S(1)} %pick3_kernel.1._p3.a), channel_id=1, source_target_pairs={{0,16},{4,20},{8,24},{12,28},{16,0},{20,4},{24,8},{28,12},{32,48},... | collective-permute-start | bytes 98312 | tf_op jit(solution)/shard_map/ppermute | solution.py:456
  7.7 1.7 %collective-permute-start.2 = (bf16[256,256]{1,0:T(8,128)(2,1)S(1)}, bf16[256,256]{1,0:T(8,128)(2,1)S(1)}, u32[]{:S(2)}, u32[]{:S(2)}) collective-permute-start(bf16[256,256]{1,0:T(8,128)(2,1)S(1)} %pick2_kernel.1._s.a), channel_id=1, source_target_pairs={{0,4},{4,0},{8,12},{12,8},{16,20},{20,16},{24,28},{28,24},{32,36},... | collective-permute-start | bytes 393224 | tf_op jit(solution)/shard_map/ppermute | solution.py:460
  9.4 2.0 %order_kernel.1 = (bf16[512,256]{1,0:T(8,128)(2,1)S(1)}, bf16[256,512]{1,0:T(8,128)(2,1)S(1)}, bf16[512,256]{1,0:T(8,128)(2,1)S(1)}, bf16[256,512]{1,0:T(8,128)(...) custom-call(s32[4]{0:T(128)S(1)} %pad_add_fusion.pos, bf16[512,256]{1,0:T(8,128)(2,1)S(1)} %copy-done.3, ...), custom_call_target="tpu_custom_call" | custom-call | flops 1500000000 | bytes 3000000 | tf_op jit(solution)/shard_map/order_kernel/pallas_call | solution.py:427
  11.4 3.7 %collective-permute-start.1 = (bf16[128,256]{1,0:T(8,128)(2,1)S(1)}, bf16[128,256]{1,0:T(8,128)(2,1)S(1)}, u32[]{:S(2)}, u32[]{:S(2)}) collective-permute-start(bf16[128,256]{1,0:T(8,128)(2,1)S(1)} %pair_kernel.2._s), channel_id=1, source_target_pairs={{0,48},{4,52},{8,56},{12,60},{16,32},{20,36},{24,40},{28,44},{32,1... | collective-permute-start | bytes 196616 | tf_op jit(solution)/shard_map/ppermute | solution.py:456
  15.1 2.3 %collective-permute-start.6 = (bf16[512,256]{1,0:T(8,128)(2,1)S(1)}, bf16[512,256]{1,0:T(8,128)(2,1)S(1)}, u32[]{:S(2)}, u32[]{:S(2)}) collective-permute-start(bf16[512,256]{1,0:T(8,128)(2,1)S(1)} %pair_kernel.3._s.a), channel_id=1, source_target_pairs={{0,12},{4,8},{8,4},{12,0},{16,28},{20,24},{24,20},{28,16},{32,44},... | collective-permute-start | bytes 786440 | tf_op jit(solution)/shard_map/ppermute | solution.py:460
  17.4 1.7 %first_kernel.2 = (f32[8,512]{1,0:T(8,128)S(1)}, f32[8,512]{1,0:T(8,128)S(1)}, f32[128,512]{1,0:T(8,128)S(1)}) custom-call(bf16[256,512]{1,0:T(8,128)(2,1)S(1)} %get-tuple-element.80.q_t, bf16[512,256]{1,0:T(8,128)(2,1)S(1)} %get-tuple-element.81.k, bf16[256,512]{1,0:T(8,128)(2,1)S(1)} %get-tuple-element.82.v_t, bf16[512,256]{1,0:T(8,128)(2,1)S(1)} %pair_kernel.3._s.a), custom_call_target="tpu_custom_call" | custom-call | flops 1000000000 | bytes 2000000 | tf_op jit(solution)/shard_map/first_kernel/pallas_call | solution.py:427
  19.2 1.1 %collective-permute-start.8 = (bf16[512,256]{1,0:T(8,128)(2,1)S(1)}, bf16[512,256]{1,0:T(8,128)(2,1)S(1)}, u32[]{:S(2)}, u32[]{:S(2)}) collective-permute-start(bf16[512,256]{1,0:T(8,128)(2,1)S(1)} %get-tuple-element.95.c0), channel_id=1, source_target_pairs={{0,2},{1,3},{2,0},{3,1},{4,6},{5,7},{6,4},{7,5},{8,10},{9,11},{10,... | collective-permute-start | bytes 786440 | tf_op jit(solution)/shard_map/ppermute | solution.py:464
  21.3 1.7 %collective-permute-start.4 = (bf16[256,256]{1,0:T(8,128)(2,1)S(1)}, bf16[256,256]{1,0:T(8,128)(2,1)S(1)}, u32[]{:S(2)}, u32[]{:S(2)}) collective-permute-start(bf16[256,256]{1,0:T(8,128)(2,1)S(1)} %get-tuple-element.84._s.a0), channel_id=1, source_target_pairs={{0,8},{4,12},{8,0},{12,4},{16,24},{20,28},{24,16},{28,20},{32,40},... | collective-permute-start | bytes 393224 | tf_op jit(solution)/shard_map/ppermute | solution.py:448
  23.1 1.7 %first_kernel.3 = (f32[8,512]{1,0:T(8,128)S(1)}, f32[8,512]{1,0:T(8,128)S(1)}, f32[128,512]{1,0:T(8,128)S(1)}) custom-call(bf16[256,512]{1,0:T(8,128)(2,1)S(1)} %get-tuple-element.80.q_t, bf16[512,256]{1,0:T(8,128)(2,1)S(1)} %get-tuple-element.81.k, bf16[256,512]{1,0:T(8,128)(2,1)S(1)} %get-tuple-element.82.v_t, bf16[256,256]{1,0:T(8,128)(2,1)S(1)} %get-tuple-element.84._s.a0), custom_call_target="tpu_custom_call" | custom-call | flops 1000000000 | bytes 2000000 | tf_op jit(solution)/shard_map/first_kernel/pallas_call | solution.py:427
  24.8 1.6 %collective-permute-done.6.b = bf16[512,256]{1,0:T(8,128)(2,1)S(1)} collective-permute-done((bf16[512,256]{1,0:T(8,128)(2,1)S(1)}, bf16[512,256]{1,0:T(8,128)(2,1)S(1)}, u32[]{:S(2)}, u32[]{:S(2)}) %collective-permute-start.6) | collective-permute-done | bytes 262176 | tf_op jit(solution)/shard_map/ppermute | solution.py:460
  27.8 1.4 %collective-permute-done.3.a1 = bf16[256,256]{1,0:T(8,128)(2,1)S(1)} collective-permute-done((bf16[256,256]{1,0:T(8,128)(2,1)S(1)}, bf16[256,256]{1,0:T(8,128)(2,1)S(1)}, u32[]{:S(2)}, u32[]{:S(2)}) %collective-permute-start.3) | collective-permute-done | bytes 131104 | tf_op jit(solution)/shard_map/ppermute | solution.py:448
  29.3 2.8 %collective-permute-start.12 = (bf16[256,256]{1,0:T(8,128)(2,1)S(1)}, bf16[256,256]{1,0:T(8,128)(2,1)S(1)}, u32[]{:S(2)}, u32[]{:S(2)}) collective-permute-start(bf16[256,256]{1,0:T(8,128)(2,1)S(1)} %pack4_kernel.1._p3.a0), channel_id=1, source_target_pairs={{0,192},{4,196},{8,200},{12,204},{16,208},{20,212},{24,216},{28,22... | collective-permute-start | bytes 393224 | tf_op jit(solution)/shard_map/ppermute | solution.py:448
  33.8 2.9 %third_kernel.1 = (f32[8,128]{1,0:T(8,128)S(1)}, f32[8,128]{1,0:T(8,128)S(1)}, f32[256,128]{1,0:T(8,128)S(1)}, bf16[512,256]{1,0:T(8,128)(2,1)S(1)}, bf16[256,51...) custom-call(s32[4]{0:T(128)S(1)} %pad_add_fusion.pos, ...), custom_call_target="tpu_custom_call" | custom-call | flops 4000000000 | bytes 8000000 | tf_op jit(solution)/shard_map/third_kernel/pallas_call | solution.py:427
  36.7 2.1 %collective-permute-done.11.a2 = bf16[256,256]{1,0:T(8,128)(2,1)S(1)} collective-permute-done((bf16[256,256]{1,0:T(8,128)(2,1)S(1)}, bf16[256,256]{1,0:T(8,128)(2,1)S(1)}, u32[]{:S(2)}, u32[]{:S(2)}) %collective-permute-start.11) | collective-permute-done | bytes 131104 | tf_op jit(solution)/shard_map/ppermute | solution.py:448
  38.8 1.3 %collective-permute-done.10.a1 = bf16[256,256]{1,0:T(8,128)(2,1)S(1)} collective-permute-done((bf16[256,256]{1,0:T(8,128)(2,1)S(1)}, bf16[256,256]{1,0:T(8,128)(2,1)S(1)}, u32[]{:S(2)}, u32[]{:S(2)}) %collective-permute-start.10) | collective-permute-done | bytes 131104 | tf_op jit(solution)/shard_map/ppermute | solution.py:448
  40.1 2.2 %fourth_kernel.1 = (f32[8,512]{1,0:T(8,128)S(1)}, f32[8,512]{1,0:T(8,128)S(1)}, bf16[256,512]{1,0:T(8,128)(2,1)S(1)}, f32[256,128]{1,0:T(8,128)S(1)}, f32[512,25...) custom-call(s32[4]{0:T(128)S(1)} %pad_add_fusion.pos, ...), custom_call_target="tpu_custom_call" | custom-call | flops 3000000000 | bytes 6000000 | tf_op jit(solution)/shard_map/fourth_kernel/pallas_call | solution.py:427
  43.3 3.7 %collective-permute-start.16 = (bf16[512,256]{1,0:T(8,128)(2,1)S(1)}, bf16[512,256]{1,0:T(8,128)(2,1)S(1)}, u32[]{:S(2)}, u32[]{:S(2)}) collective-permute-start(bf16[512,256]{1,0:T(8,128)(2,1)S(1)} %get-tuple-element.116._s), channel_id=1, source_target_pairs={{0,12},{4,8},{8,4},{12,0},{16,28},{20,24},{24,20},{28,16},{32,44},... | collective-permute-start | bytes 786440 | tf_op jit(solution)/shard_map/ppermute | solution.py:460
  49.3 4.2 %collective-permute-done.16.got = bf16[512,256]{1,0:T(8,128)(2,1)S(1)} collective-permute-done((bf16[512,256]{1,0:T(8,128)(2,1)S(1)}, bf16[512,256]{1,0:T(8,128)(2,1)S(1)}, u32[]{:S(2)}, u32[]{:S(2)}) %collective-permute-start.16) | collective-permute-done | bytes 262176 | tf_op jit(solution)/shard_map/ppermute | solution.py:460
  53.7 1.8 %third_back_kernel.1 = (f32[512,256]{1,0:T(8,128)S(1)}, f32[512,256]{1,0:T(8,128)S(1)}, f32[256,128]{1,0:T(8,128)S(1)}, f32[512,128]{1,0:T(8,128)S(1)}, f32[512,128]{1,0:T(8,128)S(1)}, /*index=5*/f32[128,512]{1,0:T(8,128)S(1)}) custom-call(bf16[256,256]{1,0:T(8,128)(2,1)S(1)} %get-tuple-element.84._s.a0, bf16[256,256]{1,0:T(8,128)(2,1)S(1)} %collective-permute-done.3.a1, ...), custom_call_target="tpu_custom_call" | custom-call | flops 3000000000 | bytes 6000000 | tf_op jit(solution)/shard_map/third_back_kernel/pallas_call | solution.py:427
  56.6 1.8 %collective-permute-done.14.b2 = bf16[512,256]{1,0:T(8,128)(2,1)S(1)} collective-permute-done((bf16[512,256]{1,0:T(8,128)(2,1)S(1)}, bf16[512,256]{1,0:T(8,128)(2,1)S(1)}, u32[]{:S(2)}, u32[]{:S(2)}) %collective-permute-start.14) | collective-permute-done | bytes 262176 | tf_op jit(solution)/shard_map/ppermute | solution.py:452
  58.4 3.7 %collective-permute-done.15.b3 = bf16[512,256]{1,0:T(8,128)(2,1)S(1)} collective-permute-done((bf16[512,256]{1,0:T(8,128)(2,1)S(1)}, bf16[512,256]{1,0:T(8,128)(2,1)S(1)}, u32[]{:S(2)}, u32[]{:S(2)}) %collective-permute-start.15) | collective-permute-done | bytes 262176 | tf_op jit(solution)/shard_map/ppermute | solution.py:452
  63.1 1.3 %collective-permute-start.22 = (bf16[320,256]{1,0:T(8,128)(2,1)S(1)}, bf16[320,256]{1,0:T(8,128)(2,1)S(1)}, u32[]{:S(2)}, u32[]{:S(2)}) collective-permute-start(bf16[320,256]{1,0:T(8,128)(2,1)S(1)} %get-tuple-element.139), channel_id=1, source_target_pairs={{0,4},{4,8},{8,12},{12,0},{16,20},{20,24},{24,28},{28,16},{32,36},... | collective-permute-start | bytes 491528 | tf_op jit(solution)/shard_map/ppermute | solution.py:452
  64.4 2.0 %collective-permute-start.20 = (bf16[320,256]{1,0:T(8,128)(2,1)S(1)}, bf16[320,256]{1,0:T(8,128)(2,1)S(1)}, u32[]{:S(2)}, u32[]{:S(2)}) collective-permute-start(bf16[320,256]{1,0:T(8,128)(2,1)S(1)} %get-tuple-element.125._s), channel_id=1, source_target_pairs={{0,12},{4,0},{8,4},{12,8},{16,28},{20,16},{24,20},{28,24},{32,44},... | collective-permute-start | bytes 491528 | tf_op jit(solution)/shard_map/ppermute | solution.py:452
  66.5 1.1 %collective-permute-start.19 = (bf16[512,256]{1,0:T(8,128)(2,1)S(1)}, bf16[512,256]{1,0:T(8,128)(2,1)S(1)}, u32[]{:S(2)}, u32[]{:S(2)}) collective-permute-start(bf16[512,256]{1,0:T(8,128)(2,1)S(1)} %get-tuple-element.137), channel_id=1, source_target_pairs={{0,2},{1,3},{2,0},{3,1},{4,6},{5,7},{6,4},{7,5},{8,10},{9,11},{10,... | collective-permute-start | bytes 786440 | tf_op jit(solution)/shard_map/ppermute | solution.py:464
  67.6 1.4 %pair_back_kernel.1 = (f32[512,128]{1,0:T(8,128)S(1)}, f32[512,128]{1,0:T(8,128)S(1)}, f32[128,512]{1,0:T(8,128)S(1)}) custom-call(bf16[512,256]{1,0:T(8,128)(2,1)S(1)} %get-tuple-element.79._s.q, bf16[256,512]{1,0:T(8,128)(2,1)S(1)} %get-tuple-element.80.q_t, bf16[512,256]{1,0:T(8,128)(2,1)S(1)} %get-tuple-element.81.k, ...), custom_call_target="tpu_custom_call" | custom-call | flops 3000000000 | bytes 6000000 | tf_op jit(solution)/shard_map/pair_back_kernel/pallas_call | solution.py:427
  69.0 2.6 %collective-permute-done.21.b2 = bf16[320,256]{1,0:T(8,128)(2,1)S(1)} collective-permute-done((bf16[320,256]{1,0:T(8,128)(2,1)S(1)}, bf16[320,256]{1,0:T(8,128)(2,1)S(1)}, u32[]{:S(2)}, u32[]{:S(2)}) %collective-permute-start.21) | collective-permute-done | bytes 163872 | tf_op jit(solution)/shard_map/ppermute | solution.py:452
  71.7 2.7 %collective-permute-done.22.b3 = bf16[320,256]{1,0:T(8,128)(2,1)S(1)} collective-permute-done((bf16[320,256]{1,0:T(8,128)(2,1)S(1)}, bf16[320,256]{1,0:T(8,128)(2,1)S(1)}, u32[]{:S(2)}, u32[]{:S(2)}) %collective-permute-start.22) | collective-permute-done | bytes 163872 | tf_op jit(solution)/shard_map/ppermute | solution.py:452
  75.0 1.1 %collective-permute-start.24 = (bf16[80,256]{1,0:T(8,128)(2,1)S(1)}, bf16[80,256]{1,0:T(8,128)(2,1)S(1)}, u32[]{:S(2)}, u32[]{:S(2)}) collective-permute-start(bf16[80,256]{1,0:T(8,128)(2,1)S(1)} %get-tuple-element.144), channel_id=1, source_target_pairs={{0,32},{4,36},{8,40},{12,44},{16,48},{20,52},{24,56},{28,60},{32,0... | collective-permute-start | bytes 122888 | tf_op jit(solution)/shard_map/ppermute | solution.py:456
  76.1 4.1 %collective-permute-start.25 = (bf16[80,256]{1,0:T(8,128)(2,1)S(1)}, bf16[80,256]{1,0:T(8,128)(2,1)S(1)}, u32[]{:S(2)}, u32[]{:S(2)}) collective-permute-start(bf16[80,256]{1,0:T(8,128)(2,1)S(1)} %get-tuple-element.145), channel_id=1, source_target_pairs={{0,48},{4,52},{8,56},{12,60},{16,32},{20,36},{24,40},{28,44},{32,1... | collective-permute-start | bytes 122888 | tf_op jit(solution)/shard_map/ppermute | solution.py:456
  80.2 1.4 %collective-permute-start.23 = (bf16[80,256]{1,0:T(8,128)(2,1)S(1)}, bf16[80,256]{1,0:T(8,128)(2,1)S(1)}, u32[]{:S(2)}, u32[]{:S(2)}) collective-permute-start(bf16[80,256]{1,0:T(8,128)(2,1)S(1)} %get-tuple-element.140._s), channel_id=1, source_target_pairs={{0,16},{4,20},{8,24},{12,28},{16,0},{20,4},{24,8},{28,12},{32,48},... | collective-permute-start | bytes 122888 | tf_op jit(solution)/shard_map/ppermute | solution.py:456
  81.6 2.8 %natural_kernel.1 = (bf16[512,256]{1,0:T(8,128)(2,1)}, bf16[512,256]{1,0:T(8,128)(2,1)S(1)}, bf16[512,256]{1,0:T(8,128)(2,1)S(1)}, f32[32,256]{1,0:T(8,128)S(1)}...) custom-call(s32[4]{0:T(128)S(1)} %pad_add_fusion.pos, f32[256,128]{1,0:T(8,128)S(1)} %get-tuple-element.108.dq_first, ...), custom_call_target="tpu_custom_call" | custom-call | flops 3000000000 | bytes 6000000 | tf_op jit(solution)/shard_map/natural_kernel/pallas_call | solution.py:427
  85.1 1.8 %last_kernel.1 = (bf16[512,256]{1,0:T(8,128)(2,1)}, bf16[512,256]{1,0:T(8,128)(2,1)}, f32[16,256]{1,0:T(8,128)}) custom-call(s32[4]{0:T(128)S(1)} %pad_add_fusion.pos, f32[80,256]{1,0:T(8,128)S(1)} %get-tuple-element.143.own, bf16[80,256]{1,0:T(8,128)(2,1)S(1)} %collective-permute-done.23.b1, bf16[80,256]{1,0:T(8,128)(2,1)S(1)} %collective-permute-done.24.b2, ...), custom_call_target="tpu_custom_call" | custom-call | flops 1000000000 | bytes 2000000 | tf_op jit(solution)/shard_map/last_kernel/pallas_call | solution.py:427
  (53 shorter events, 14.9 us)
Async XLA Ops:
  0.8 1.0 %copy-start.1 = (bf16[512,256]{1,0:T(8,128)(2,1)S(1)}, bf16[512,256]{1,0:T(8,128)(2,1)}, u32[]{:S(2)}) copy-start(bf16[512,256]{1,0:T(8,128)(2,1)} %k.5) | copy-start | bytes 786436
  1.7 0.9 %copy-start.2 = (bf16[512,256]{1,0:T(8,128)(2,1)S(1)}, bf16[512,256]{1,0:T(8,128)(2,1)}, u32[]{:S(2)}) copy-start(bf16[512,256]{1,0:T(8,128)(2,1)} %v.5) | copy-start | bytes 786436
  3.5 5.9 %copy-start.3 = (bf16[512,256]{1,0:T(8,128)(2,1)S(1)}, bf16[512,256]{1,0:T(8,128)(2,1)}, u32[]{:S(2)}) copy-start(bf16[512,256]{1,0:T(8,128)(2,1)} %q.1) | copy-start | bytes 786436
  3.5 7.9 %collective-permute-start = (bf16[64,256]{1,0:T(8,128)(2,1)S(1)}, bf16[64,256]{1,0:T(8,128)(2,1)S(1)}, u32[]{:S(2)}, u32[]{:S(2)}) collective-permute-start(bf16[64,256]{1,0:T(8,128)(2,1)S(1)} %pick3_kernel.1._p3.a), channel_id=1, source_target_pairs={{0,16},{4,20},{8,24},{12,28},{16,0},{20,4},{24,8},{28,12},{32,48},... | collective-permute-start | bytes 98312 | tf_op jit(solution)/shard_map/ppermute | solution.py:456
  7.7 7.3 %collective-permute-start.2 = (bf16[256,256]{1,0:T(8,128)(2,1)S(1)}, bf16[256,256]{1,0:T(8,128)(2,1)S(1)}, u32[]{:S(2)}, u32[]{:S(2)}) collective-permute-start(bf16[256,256]{1,0:T(8,128)(2,1)S(1)} %pick2_kernel.1._s.a), channel_id=1, source_target_pairs={{0,4},{4,0},{8,12},{12,8},{16,20},{20,16},{24,28},{28,24},{32,36},... | collective-permute-start | bytes 393224 | tf_op jit(solution)/shard_map/ppermute | solution.py:460
  11.4 7.7 %collective-permute-start.1 = (bf16[128,256]{1,0:T(8,128)(2,1)S(1)}, bf16[128,256]{1,0:T(8,128)(2,1)S(1)}, u32[]{:S(2)}, u32[]{:S(2)}) collective-permute-start(bf16[128,256]{1,0:T(8,128)(2,1)S(1)} %pair_kernel.2._s), channel_id=1, source_target_pairs={{0,48},{4,52},{8,56},{12,60},{16,32},{20,36},{24,40},{28,44},{32,1... | collective-permute-start | bytes 196616 | tf_op jit(solution)/shard_map/ppermute | solution.py:456
  15.1 11.2 %collective-permute-start.6 = (bf16[512,256]{1,0:T(8,128)(2,1)S(1)}, bf16[512,256]{1,0:T(8,128)(2,1)S(1)}, u32[]{:S(2)}, u32[]{:S(2)}) collective-permute-start(bf16[512,256]{1,0:T(8,128)(2,1)S(1)} %pair_kernel.3._s.a), channel_id=1, source_target_pairs={{0,12},{4,8},{8,4},{12,0},{16,28},{20,24},{24,20},{28,16},{32,44},... | collective-permute-start | bytes 786440 | tf_op jit(solution)/shard_map/ppermute | solution.py:460
  17.4 1.7 %copy-start.4 = (bf16[512,256]{1,0:T(8,128)(2,1)S(1)}, bf16[512,256]{1,0:T(8,128)(2,1)}, u32[]{:S(2)}) copy-start(bf16[512,256]{1,0:T(8,128)(2,1)} %cot.1) | copy-start | bytes 786436
  19.2 7.2 %collective-permute-start.8 = (bf16[512,256]{1,0:T(8,128)(2,1)S(1)}, bf16[512,256]{1,0:T(8,128)(2,1)S(1)}, u32[]{:S(2)}, u32[]{:S(2)}) collective-permute-start(bf16[512,256]{1,0:T(8,128)(2,1)S(1)} %get-tuple-element.95.c0), channel_id=1, source_target_pairs={{0,2},{1,3},{2,0},{3,1},{4,6},{5,7},{6,4},{7,5},{8,10},{9,11},{10,... | collective-permute-start | bytes 786440 | tf_op jit(solution)/shard_map/ppermute | solution.py:464
  20.3 7.5 %collective-permute-start.5 = (bf16[256,256]{1,0:T(8,128)(2,1)S(1)}, bf16[256,256]{1,0:T(8,128)(2,1)S(1)}, u32[]{:S(2)}, u32[]{:S(2)}) collective-permute-start(bf16[256,256]{1,0:T(8,128)(2,1)S(1)} %get-tuple-element.84._s.a0), channel_id=1, source_target_pairs={{0,12},{4,0},{8,4},{12,8},{16,28},{20,16},{24,20},{28,24},{32,44},... | collective-permute-start | bytes 393224 | tf_op jit(solution)/shard_map/ppermute | solution.py:448
  21.3 6.5 %collective-permute-start.4 = (bf16[256,256]{1,0:T(8,128)(2,1)S(1)}, bf16[256,256]{1,0:T(8,128)(2,1)S(1)}, u32[]{:S(2)}, u32[]{:S(2)}) collective-permute-start(bf16[256,256]{1,0:T(8,128)(2,1)S(1)} %get-tuple-element.84._s.a0), channel_id=1, source_target_pairs={{0,8},{4,12},{8,0},{12,4},{16,24},{20,28},{24,16},{28,20},{32,40},... | collective-permute-start | bytes 393224 | tf_op jit(solution)/shard_map/ppermute | solution.py:448
  23.0 6.2 %collective-permute-start.3 = (bf16[256,256]{1,0:T(8,128)(2,1)S(1)}, bf16[256,256]{1,0:T(8,128)(2,1)S(1)}, u32[]{:S(2)}, u32[]{:S(2)}) collective-permute-start(bf16[256,256]{1,0:T(8,128)(2,1)S(1)} %get-tuple-element.84._s.a0), channel_id=1, source_target_pairs={{0,4},{4,8},{8,12},{12,0},{16,20},{20,24},{24,28},{28,16},{32,36},... | collective-permute-start | bytes 393224 | tf_op jit(solution)/shard_map/ppermute | solution.py:448
  26.4 7.4 %collective-permute-start.7 = (bf16[512,256]{1,0:T(8,128)(2,1)S(1)}, bf16[512,256]{1,0:T(8,128)(2,1)S(1)}, u32[]{:S(2)}, u32[]{:S(2)}) collective-permute-start(bf16[512,256]{1,0:T(8,128)(2,1)S(1)} %get-tuple-element.95.c0), channel_id=1, source_target_pairs={{0,1},{1,0},{2,3},{3,2},{4,5},{5,4},{6,7},{7,6},{8,9},{9,8},{10,11... | collective-permute-start | bytes 786440 | tf_op jit(solution)/shard_map/ppermute | solution.py:464
  26.4 7.4 %collective-permute-start.9 = (bf16[512,256]{1,0:T(8,128)(2,1)S(1)}, bf16[512,256]{1,0:T(8,128)(2,1)S(1)}, u32[]{:S(2)}, u32[]{:S(2)}) collective-permute-start(bf16[512,256]{1,0:T(8,128)(2,1)S(1)} %collective-permute-done.8.c2), channel_id=1, source_target_pairs={{0,1},{1,0},{2,3},{3,2},{4,5},{5,4},{6,7},{7,6},{8,9},{9,8},{10,11... | collective-permute-start | bytes 786440 | tf_op jit(solution)/shard_map/ppermute | solution.py:464
  29.2 4.6 %copy-start = (bf16[256,1024]{1,0:T(8,128)(2,1)S(1)}, bf16[256,1024]{1,0:T(8,128)(2,1)}, u32[]{:S(2)}) copy-start(bf16[256,1024]{1,0:T(8,128)(2,1)} %w.3) | copy-start | bytes 1572868
  29.3 7.4 %collective-permute-start.12 = (bf16[256,256]{1,0:T(8,128)(2,1)S(1)}, bf16[256,256]{1,0:T(8,128)(2,1)S(1)}, u32[]{:S(2)}, u32[]{:S(2)}) collective-permute-start(bf16[256,256]{1,0:T(8,128)(2,1)S(1)} %pack4_kernel.1._p3.a0), channel_id=1, source_target_pairs={{0,192},{4,196},{8,200},{12,204},{16,208},{20,212},{24,216},{28,22... | collective-permute-start | bytes 393224 | tf_op jit(solution)/shard_map/ppermute | solution.py:448
  32.1 6.7 %collective-permute-start.11 = (bf16[256,256]{1,0:T(8,128)(2,1)S(1)}, bf16[256,256]{1,0:T(8,128)(2,1)S(1)}, u32[]{:S(2)}, u32[]{:S(2)}) collective-permute-start(bf16[256,256]{1,0:T(8,128)(2,1)S(1)} %pack4_kernel.1._p3.a0), channel_id=1, source_target_pairs={{0,128},{4,132},{8,136},{12,140},{16,144},{20,148},{24,152},{28,15... | collective-permute-start | bytes 393224 | tf_op jit(solution)/shard_map/ppermute | solution.py:448
  32.9 7.2 %collective-permute-start.10 = (bf16[256,256]{1,0:T(8,128)(2,1)S(1)}, bf16[256,256]{1,0:T(8,128)(2,1)S(1)}, u32[]{:S(2)}, u32[]{:S(2)}) collective-permute-start(bf16[256,256]{1,0:T(8,128)(2,1)S(1)} %pack4_kernel.1._p3.a0), channel_id=1, source_target_pairs={{0,64},{4,68},{8,72},{12,76},{16,80},{20,84},{24,88},{28,92},{32,9... | collective-permute-start | bytes 393224 | tf_op jit(solution)/shard_map/ppermute | solution.py:448
  43.3 10.2 %collective-permute-start.16 = (bf16[512,256]{1,0:T(8,128)(2,1)S(1)}, bf16[512,256]{1,0:T(8,128)(2,1)S(1)}, u32[]{:S(2)}, u32[]{:S(2)}) collective-permute-start(bf16[512,256]{1,0:T(8,128)(2,1)S(1)} %get-tuple-element.116._s), channel_id=1, source_target_pairs={{0,12},{4,8},{8,4},{12,0},{16,28},{20,24},{24,20},{28,16},{32,44},... | collective-permute-start | bytes 786440 | tf_op jit(solution)/shard_map/ppermute | solution.py:460
  47.0 9.5 %collective-permute-start.13 = (bf16[512,256]{1,0:T(8,128)(2,1)S(1)}, bf16[512,256]{1,0:T(8,128)(2,1)S(1)}, u32[]{:S(2)}, u32[]{:S(2)}) collective-permute-start(bf16[512,256]{1,0:T(8,128)(2,1)S(1)} %get-tuple-element.118), channel_id=1, source_target_pairs={{0,192},{4,196},{8,200},{12,204},{16,208},{20,212},{24,216},{28,22... | collective-permute-start | bytes 786440 | tf_op jit(solution)/shard_map/ppermute | solution.py:452
  47.6 10.8 %collective-permute-start.14 = (bf16[512,256]{1,0:T(8,128)(2,1)S(1)}, bf16[512,256]{1,0:T(8,128)(2,1)S(1)}, u32[]{:S(2)}, u32[]{:S(2)}) collective-permute-start(bf16[512,256]{1,0:T(8,128)(2,1)S(1)} %get-tuple-element.119), channel_id=1, source_target_pairs={{0,128},{4,132},{8,136},{12,140},{16,144},{20,148},{24,152},{28,15... | collective-permute-start | bytes 786440 | tf_op jit(solution)/shard_map/ppermute | solution.py:452
  48.4 13.7 %collective-permute-start.15 = (bf16[512,256]{1,0:T(8,128)(2,1)S(1)}, bf16[512,256]{1,0:T(8,128)(2,1)S(1)}, u32[]{:S(2)}, u32[]{:S(2)}) collective-permute-start(bf16[512,256]{1,0:T(8,128)(2,1)S(1)} %get-tuple-element.120), channel_id=1, source_target_pairs={{0,64},{4,68},{8,72},{12,76},{16,80},{20,84},{24,88},{28,92},{32,9... | collective-permute-start | bytes 786440 | tf_op jit(solution)/shard_map/ppermute | solution.py:452
  53.6 8.5 %collective-permute-start.17 = (bf16[256,256]{1,0:T(8,128)(2,1)S(1)}, bf16[256,256]{1,0:T(8,128)(2,1)S(1)}, u32[]{:S(2)}, u32[]{:S(2)}) collective-permute-start(bf16[256,256]{1,0:T(8,128)(2,1)S(1)} %get-tuple-element.124), channel_id=1, source_target_pairs={{0,4},{4,0},{8,12},{12,8},{16,20},{20,16},{24,28},{28,24},{32,36},... | collective-permute-start | bytes 393224 | tf_op jit(solution)/shard_map/ppermute | solution.py:460
  62.9 3.5 %collective-permute-start.18 = (bf16[1024,256]{1,0:T(8,128)(2,1)S(1)}, bf16[1024,256]{1,0:T(8,128)(2,1)S(1)}, u32[]{:S(2)}, u32[]{:S(2)}) collective-permute-start(bf16[1024,256]{1,0:T(8,128)(2,1)S(1)} %get-tuple-element.135), channel_id=1, source_target_pairs={{0,1},{1,0},{2,3},{3,2},{4,5},{5,4},{6,7},{7,6},{8,9},{9,8},{10,11... | collective-permute-start | bytes 1572872 | tf_op jit(solution)/shard_map/ppermute | solution.py:464
  63.0 8.6 %collective-permute-start.21 = (bf16[320,256]{1,0:T(8,128)(2,1)S(1)}, bf16[320,256]{1,0:T(8,128)(2,1)S(1)}, u32[]{:S(2)}, u32[]{:S(2)}) collective-permute-start(bf16[320,256]{1,0:T(8,128)(2,1)S(1)} %get-tuple-element.138), channel_id=1, source_target_pairs={{0,8},{4,12},{8,0},{12,4},{16,24},{20,28},{24,16},{28,20},{32,40},... | collective-permute-start | bytes 491528 | tf_op jit(solution)/shard_map/ppermute | solution.py:452
  63.1 11.2 %collective-permute-start.22 = (bf16[320,256]{1,0:T(8,128)(2,1)S(1)}, bf16[320,256]{1,0:T(8,128)(2,1)S(1)}, u32[]{:S(2)}, u32[]{:S(2)}) collective-permute-start(bf16[320,256]{1,0:T(8,128)(2,1)S(1)} %get-tuple-element.139), channel_id=1, source_target_pairs={{0,4},{4,8},{8,12},{12,0},{16,20},{20,24},{24,28},{28,16},{32,36},... | collective-permute-start | bytes 491528 | tf_op jit(solution)/shard_map/ppermute | solution.py:452
  64.4 9.9 %collective-permute-start.20 = (bf16[320,256]{1,0:T(8,128)(2,1)S(1)}, bf16[320,256]{1,0:T(8,128)(2,1)S(1)}, u32[]{:S(2)}, u32[]{:S(2)}) collective-permute-start(bf16[320,256]{1,0:T(8,128)(2,1)S(1)} %get-tuple-element.125._s), channel_id=1, source_target_pairs={{0,12},{4,0},{8,4},{12,8},{16,28},{20,16},{24,20},{28,24},{32,44},... | collective-permute-start | bytes 491528 | tf_op jit(solution)/shard_map/ppermute | solution.py:452
  66.5 15.1 %collective-permute-start.19 = (bf16[512,256]{1,0:T(8,128)(2,1)S(1)}, bf16[512,256]{1,0:T(8,128)(2,1)S(1)}, u32[]{:S(2)}, u32[]{:S(2)}) collective-permute-start(bf16[512,256]{1,0:T(8,128)(2,1)S(1)} %get-tuple-element.137), channel_id=1, source_target_pairs={{0,2},{1,3},{2,0},{3,1},{4,6},{5,7},{6,4},{7,5},{8,10},{9,11},{10,... | collective-permute-start | bytes 786440 | tf_op jit(solution)/shard_map/ppermute | solution.py:464
  75.0 9.3 %collective-permute-start.24 = (bf16[80,256]{1,0:T(8,128)(2,1)S(1)}, bf16[80,256]{1,0:T(8,128)(2,1)S(1)}, u32[]{:S(2)}, u32[]{:S(2)}) collective-permute-start(bf16[80,256]{1,0:T(8,128)(2,1)S(1)} %get-tuple-element.144), channel_id=1, source_target_pairs={{0,32},{4,36},{8,40},{12,44},{16,48},{20,52},{24,56},{28,60},{32,0... | collective-permute-start | bytes 122888 | tf_op jit(solution)/shard_map/ppermute | solution.py:456
  76.1 8.3 %collective-permute-start.25 = (bf16[80,256]{1,0:T(8,128)(2,1)S(1)}, bf16[80,256]{1,0:T(8,128)(2,1)S(1)}, u32[]{:S(2)}, u32[]{:S(2)}) collective-permute-start(bf16[80,256]{1,0:T(8,128)(2,1)S(1)} %get-tuple-element.145), channel_id=1, source_target_pairs={{0,48},{4,52},{8,56},{12,60},{16,32},{20,36},{24,40},{28,44},{32,1... | collective-permute-start | bytes 122888 | tf_op jit(solution)/shard_map/ppermute | solution.py:456
  80.2 4.9 %collective-permute-start.23 = (bf16[80,256]{1,0:T(8,128)(2,1)S(1)}, bf16[80,256]{1,0:T(8,128)(2,1)S(1)}, u32[]{:S(2)}, u32[]{:S(2)}) collective-permute-start(bf16[80,256]{1,0:T(8,128)(2,1)S(1)} %get-tuple-element.140._s), channel_id=1, source_target_pairs={{0,16},{4,20},{8,24},{12,28},{16,0},{20,4},{24,8},{28,12},{32,48},... | collective-permute-start | bytes 122888 | tf_op jit(solution)/shard_map/ppermute | solution.py:456

commit v3 on v2

--- a/solution.py
+++ b/solution.py
@@ -140,6 +140,32 @@
                 dk_ref[...] += dk
 
 
+def blocks4(rows):
+    full = jnp.concatenate([head_blocks(r.astype(F32), SEL4) for r in rows], 0)
+    return full.astype(BF), full.T.astype(BF)
+
+
+def fold_heads(wide):
+    total = None
+    for h in range(NH):
+        part = wide[HD * h:HD * h + HD]
+        part = jnp.where(((iota(part.shape, 1) >> 3) & 3) == h, part, 0.0)
+        total = part if total is None else total + part
+    return total
+
+
+def first_lanes(rows, d):
+    return pltpu.roll(rows, 128 - 32 * d, 1) if d else rows
+
+
+def three(rows):
+    high = rows.astype(BF)
+    rest = rows - high.astype(F32)
+    middle = rest.astype(BF)
+    low = (rest - middle.astype(F32)).astype(BF)
+    return [high.astype(F32), middle.astype(F32), low.astype(F32)]
+
+
 def pick3_kernel(pos, k, v, out):
     mats = [pick_mat(pos[0] * NH + m, SEL3) for m in range(NH)]
     ks, vs = per_head_rows(mats, [k[...], v[...]])
@@ -154,11 +180,12 @@
     out[SEL2:2 * SEL2] = vs.astype(BF)
 
 
-def order_kernel(pos, q, k, v, _s, q_out, q_t_out, k_out, k_t_out, v_out, v_t_out):
+def order_kernel(pos, q, k, v, _s, q_out, q_t_out, k_out, k_t_out, v_out, v_t_out, q4_out):
     mats = [pick_mat(pos[0] * NH + m, T) for m in range(NH)]
     qs, ks, vs = per_head_rows(mats, [q[...], k[...], v[...]])
     qs = qs * SCALE
     q_out[...] = qs.astype(BF)
+    q4_out[...] = qs[0:16].astype(BF)
     q_t_out[...] = qs.T.astype(BF)
     k_out[...] = ks.astype(BF)
     k_t_out[...] = ks.T.astype(BF)
@@ -187,29 +214,47 @@
     out[rows:2 * rows] = b[...]
 
 
-def pack3_kernel(a, b, c, cot, _s, out, cot_out):
+def pack3_kernel(b, c, cot, _s, _t, out, cot_out):
     cot_out[...] = cot[...]
     for half in range(2):
         base = SEL3 * half
-        rows = [a[base:base + SEL3], b[base:base + SEL3], c[64 + base:64 + base + SEL3], c[base:base + SEL3]]
-        for n, part in enumerate(rows):
-            out[128 * half + SEL3 * n:128 * half + SEL3 * n + SEL3] = part
-
-
-def pack4_kernel(a0, a1, a2, a3, _s, _t, out):
-    for base in (0, 128):
+        for n, part in enumerate((b[base:base + SEL3], c[64 + base:64 + base + SEL3], c[base:base + SEL3])):
+            out[96 * half + SEL3 * n:96 * half + SEL3 * n + SEL3] = part
+
+
+def level2_places(a, b):
+    return a.at[0:256], a.at[256:512], b.at[256:512], b.at[0:256]
+
+
+def part4_kernel(a, b, c0, c1, c2, c3, qa, qb, _s, _t, out, part):
+    for half in range(2):
         parts = []
-        for a in (a0, a1, a2, a3):
-            for n in range(4):
-                start = base + SEL3 * n
-                parts.append(a[start:start + 16].astype(F32)[:SEL4])
-        out[base:base + 128] = jnp.concatenate(parts, 0).astype(BF)
+        for here, others in zip(level2_places(a, b), (c0, c1, c2, c3)):
+            parts.append(here[128 * half:128 * half + 16].astype(F32)[:SEL4])
+            for n in range(3):
+                start = 96 * half + SEL3 * n
+                parts.append(others[start:start + 16].astype(F32)[:SEL4])
+        out[128 * half:128 * half + 128] = jnp.concatenate(parts, 0).astype(BF)
+    _, q_t = blocks4([qa[0:16], qa[16:32], qb[16:32], qb[0:16]])
+    peak, total, weights = soft(dot(out[0:128], q_t))
+    part[0:HD] = fold_heads(dot(out[128:256], weights, ((0,), (0,))))
+    part[HD:HD + 8] = jnp.concatenate(
+        [peak, total, jnp.zeros((6, 128), F32)], 0
+    )
 
 
 def stack_kv(refs):
     keys = jnp.concatenate([a[0:128] for a in refs], 0)
     values = jnp.concatenate([a[128:256] for a in refs], 0)
     return keys, values
+
+
+def stack_kv3(a, b, others):
+    keys, values = [], []
+    for here, other in zip(level2_places(a, b), others):
+        keys += [here[0:SEL3], other[0:96]]
+        values += [here[128:128 + SEL3], other[96:192]]
+    return jnp.concatenate(keys, 0), jnp.concatenate(values, 0)
 
 
 def second_kernel(a, b, q, m_out, l_out, o_out):
@@ -223,7 +268,7 @@
     )
 
 
-def third_kernel(pos, a0, a1, a2, a3, q, m1a, l1a, o1a, m1b, l1b, o1b, m2, l2, o2, c0, c1, c2, c3, w, _p3,
+def third_kernel(pos, a, b, a0, a1, a2, a3, q, m1a, l1a, o1a, m1b, l1b, o1b, m2, l2, o2, c0, c1, c2, c3, w, _p3,
                  m_out, l_out, o_out, g_out, g_t_out, lse_out, delta_out, att_out):
     here = pos[0]
     grad = None
@@ -237,7 +282,7 @@
     g_out[...] = gs.astype(BF)
     g_t_out[...] = g_t.astype(BF)
 
-    keys, values = stack_kv((a0, a1, a2, a3))
+    keys, values = stack_kv3(a, b, (a0, a1, a2, a3))
     _, q_t = blocks_both(q[0:SEL3].astype(F32), SEL3)
     m3, l3, wide = forward(keys, values, q_t)
     m3 = jnp.broadcast_to(m3, (8, 128))
@@ -267,14 +312,17 @@
         att_out[rows] = dot(out.astype(BF), mats[h][128:T])
 
 
-def fourth_kernel(pos, a0, a1, a2, a3, q, m, l, o, g, g_t, lse_in, delta_in, att_in, c0, c1, c2, c3,
-                  lse_out, delta_out, att_out, dq_out, s0, s1, s2, s3, blocks):
+def fourth_kernel(pos, r0, r1, r2, r3, m, l, o, g, g_t, lse_in, delta_in, att_in, c0, c1, c2, c3,
+                  lse_out, delta_out, att_out, s0, s1, s2, s3, blocks):
     here, x_pos = pos[0], pos[1]
-    keys, values = stack_kv((a0, a1, a2, a3))
-    q4, q4_t = blocks_both(q[0:16].astype(F32), SEL4)
-    g4, g4_t = blocks_both(g[0:16].astype(F32), SEL4)
-    peak, total, weights = soft(dot(keys, q4_t))
-    wide = dot(values, weights, ((0,), (0,)))
+    parts = [first_lanes(r[...], d) for d, r in enumerate((r0, r1, r2, r3))]
+    peaks = [r[HD:HD + 8] for r in parts]
+    peak = jnp.maximum(jnp.maximum(peaks[0], peaks[1]), jnp.maximum(peaks[2], peaks[3]))[0:1]
+    total, weighted = 0.0, 0.0
+    for r in parts:
+        factor = jnp.exp(r[HD:HD + 1] - peak)
+        total = total + factor * r[HD + 1:HD + 2]
+        weighted = weighted + factor * r[0:HD]
     peak = jnp.broadcast_to(peak, (8, 128))
     total = jnp.broadcast_to(total, (8, 128))
     lse_out[...] = lse_in[...]
@@ -285,7 +333,7 @@
         ma, la, oa = m[h:h + 1], l[h:h + 1], o[rows]
         mb = from_lanes(peak, h, SEL4, NEG)[0:1]
         lb = from_lanes(total, h, SEL4, 0.0)[0:1]
-        ob = from_lanes(wide[rows], h, SEL4, 0.0)
+        ob = from_lanes(weighted, h, SEL4, 0.0)
         top = jnp.maximum(ma, mb)
         fa, fb = jnp.exp(ma - top), jnp.exp(mb - top)
         denominator = fa * la + fb * lb
@@ -298,17 +346,32 @@
         delta_rows.append(delta)
         att = att_in[rows] + dot(out.astype(BF), pick_mat(here * NH + h, SEL2))
         att_out[rows] = att.astype(BF)
-    d_keys, d_values, dq = backward(
-        keys, values, q4, q4_t, g4, g4_t, to_lanes(lse_rows, SEL4), to_lanes(delta_rows, SEL4)
-    )
-    dq_out[...] = diag_lanes(dq, SEL4)
+    stats = three(to_lanes(lse_rows, SEL4)) + three(to_lanes(delta_rows, SEL4)) + [jnp.zeros((2, 128), F32)]
+    stats = jnp.concatenate(stats, 0)
+    stats = jnp.concatenate([g[0:16].astype(F32)[0:SEL4], jnp.concatenate([stats, stats], 1)], 0).astype(BF)
     for r, c in enumerate((c0, c1, c2, c3)):
         blocks[here ^ r] = c[...]
     for d, s in enumerate((s0, s1, s2, s3)):
-        s[0:128] = d_keys[128 * d:128 * d + 128].astype(s.dtype)
-        s[128:256] = d_values[128 * d:128 * d + 128].astype(s.dtype)
-        term = dot(att_out[...], blocks[(x_pos - d) & 3])
-        s[256:512] = term.T.astype(s.dtype)
+        term = dot(att_out[...], blocks[x_pos ^ d])
+        s[0:256] = term.T.astype(s.dtype)
+        s[256:272] = stats.astype(s.dtype)
+
+
+def fourth_back_kernel(kv, qa, qb, b0, b1, b2, b3, d_keys, d_values, dq):
+    q, q_t = blocks4([qa[0:16], qa[16:32], qb[16:32], qb[0:16]])
+    news = [b[256:272].astype(F32) for b in (b0, b1, b2, b3)]
+    g, g_t = blocks4(news)
+    lse, delta = 0.0, 0.0
+    for d, new in enumerate(news):
+        for start in range(3):
+            row_l = jnp.where(iota((1, 128), 1) < 32, new[8 + start:9 + start, 0:128], 0.0)
+            row_d = jnp.where(iota((1, 128), 1) < 32, new[11 + start:12 + start, 0:128], 0.0)
+            both = jnp.concatenate([row_l, row_d, jnp.zeros((6, 128), F32)], 0)
+            both = pltpu.roll(both, 32 * d, 1) if d else both
+            lse = lse + both[0:1]
+            delta = delta + both[1:2]
+    d_keys[...], d_values[...], wide = backward(kv[0:128], kv[128:256], q, q_t, g, g_t, lse, delta)
+    dq[...] = fold_heads(wide)
 
 
 def project_kernel(pos, att, w, _s, send, keep_a, keep_b):
@@ -318,7 +381,7 @@
         ref[...] = dot(att[...], w[:, pl.ds(at, F)], ((0,), (0,))).astype(ref.dtype)
 
 
-def second_back_kernel(a, b, q, g, lse, delta, dq_in, own, send, dq_first):
+def second_back_kernel(a, b, q, g, lse, delta, own, send, dq_first):
     keys, values = stack_kv((a.at[0:256], a.at[256:512], b.at[0:256], b.at[256:512]))
     q2, q2_t = blocks_both(q[0:SEL2].astype(F32), SEL2)
     g2, g2_t = blocks_both(g[0:SEL2].astype(F32), SEL2)
@@ -326,20 +389,20 @@
     delta2 = jnp.concatenate([delta[h:h + 1, 0:128] for h in range(NH)], 1)
     d_keys, d_values, wide = backward(keys, values, q2, q2_t, g2, g2_t, lse2, delta2)
     diag = [wide[HD * h:HD * h + HD, 128 * h:128 * h + 128] for h in range(NH)]
-    dq_first[...] = dq_in[...] + jnp.concatenate(diag, 0)
+    dq_first[...] = jnp.concatenate(diag, 0)
     for n, (out, at) in enumerate(((own, 0), (own, 256), (send, 0), (send, 256))):
         out[at:at + 128] = d_keys[128 * n:128 * n + 128].astype(out.dtype)
         out[at + 128:at + 256] = d_values[128 * n:128 * n + 128].astype(out.dtype)
 
 
-def fold_kernel(own, got, keep, send):
+def fold_kernel(own, got, _s, keep, send):
     keep[...] = own[0:256] + got[0:256].astype(F32)
     send[...] = (own[256:512] + got[256:512].astype(F32)).astype(BF)
 
 
-def third_back_kernel(a0, a1, a2, a3, q, q_t, k, k_t, v, g, g_t, lse, delta, dq_in,
+def third_back_kernel(a, b, a0, a1, a2, a3, q, q_t, k, k_t, v, g, g_t, lse, delta, dq_in,
                       dk3, dv3, dq_first, dk, dv, dq):
-    keys, values = stack_kv((a0, a1, a2, a3))
+    keys, values = stack_kv3(a, b, (a0, a1, a2, a3))
     q3, q3_t = blocks_both(q[0:SEL3].astype(F32), SEL3)
     g3, g3_t = blocks_both(g[0:SEL3].astype(F32), SEL3)
     lse3 = to_lanes([lse[h:h + 1, 0:128] for h in range(NH)], SEL3)
@@ -353,20 +416,20 @@
     level1_backward(1, q, q_t, k, k_t, v, g, g_t, lse, delta, dk, dv, dq)
 
 
-def reduce_y_kernel(pos, own, b1, b2, b3, dk3, dv3, _s, s0, s1, s2, s3, total):
+def reduce_y_kernel(pos, own, b1, b2, b3, dk4, dv4, dk3, dv3, _s, s0, s1, s2, s3, total):
     y_pos = pos[3]
-    total[...] = own[...] + b1[...].astype(F32) + b2[...].astype(F32) + b3[...].astype(F32)
+    total[...] = own[0:256] + b1[0:256].astype(F32) + b2[0:256].astype(F32) + b3[0:256].astype(F32)
     for d, s in enumerate((s0, s1, s2, s3)):
-        for base, level in ((0, dk3), (128, dv3)):
+        for base, level, fourth in ((0, dk3, dk4), (128, dv3, dv4)):
             parts = []
             for n in range(4):
                 at = 128 * d + SEL3 * n
-                start = base + SEL3 * d + SEL4 * n
-                parts.append(level[at:at + SEL4] + total[start:start + SEL4])
+                start = SEL3 * d + SEL4 * n
+                parts.append(level[at:at + SEL4] + fourth[start:start + SEL4])
                 parts.append(level[at + SEL4:at + SEL3])
             s[base:base + 128] = jnp.concatenate(parts, 0).astype(s.dtype)
         for n in range(4):
-            start = pl.multiple_of(256 + 64 * n + 16 * ((y_pos - d) & 3), 16)
+            start = pl.multiple_of(64 * n + 16 * (y_pos ^ d), 16)
             s[256 + 16 * n:272 + 16 * n] = total[pl.ds(start, 16)].astype(s.dtype)
 
 
@@ -380,22 +443,29 @@
         s[64:80] = total[pl.ds(start, 16)].astype(s.dtype)
 
 
+def fold4_kernel(own, got, keep, send):
+    keep[...] = own[...] + first_lanes(got[...], 3)
+    send[...] = first_lanes(own[...], 1) + first_lanes(got[...], 2)
+
+
 def mix_kernel(keep_a, keep_b, got, own, send):
     own[...] = keep_a[...] + got[0:T].astype(F32)
     send[...] = (keep_b[...] + got[T:2 * T].astype(F32)).astype(BF)
 
 
-def natural_kernel(pos, dq_first, dk_a, dv_a, dq_a, dk_b, dv_b, dq_b, own2, got2, mix_own, mix_got, _s,
+def natural_kernel(pos, e0, e1, dq_first, dk_a, dv_a, dq_a, dk_b, dv_b, dq_b, own2, got2, mix_own, mix_got, _s,
                    dq_out, dk_part, dv_part, dk_head, dv_head, mixed_out):
+    mixed_out[...] = (mix_own[...] + mix_got[...].astype(F32)).astype(BF)
     level2 = own2[...] + got2[...].astype(F32)
-    mixed_out[...] = (mix_own[...] + mix_got[...].astype(F32)).astype(BF)
+    dq4 = e0[...] + e1[...]
     for p, (dk, dv, dq) in enumerate(((dk_a, dv_a, dq_a), (dk_b, dv_b, dq_b))):
         cols = slice(128 * p, 128 * p + 128)
         dk_top = dk[0:SEL2] + level2[0:SEL2, cols]
         dv_top = dv[0:SEL2] + level2[SEL2:2 * SEL2, cols]
         dk_head[:, cols] = dk_top[0:SEL3]
         dv_head[:, cols] = dv_top[0:SEL3]
-        dq_t = jnp.concatenate([dq[:, 0:128] + dq_first[cols], dq[:, 128:T]], 1) * SCALE
+        dq4_pair = jnp.concatenate([from_lanes(dq4, h, SEL4, 0.0) for h in (2 * p, 2 * p + 1)], 0)
+        dq_t = jnp.concatenate([dq[:, 0:128] + dq_first[cols] + dq4_pair, dq[:, 128:T]], 1) * SCALE
         later = [
             jnp.concatenate([jnp.zeros((SEL3, 128), F32), top[SEL3:SEL2], rest[SEL2:T]], 0)
             for top, rest in ((dk_top, dk), (dv_top, dv))
@@ -436,20 +506,8 @@
     )(*args)
 
 
-def step(stride, shift):
-    pairs = []
-    for s in range(64):
-        at = s // stride % 4
-        pairs.append((s, s + ((at + shift) % 4 - at) * stride))
-    return pairs
-
-
-def spread(block, stride):
-    return [block] + [lax.ppermute(block, "seq", step(stride, d)) for d in (1, 2, 3)]
-
-
-def bring(blocks, stride):
-    return [blocks[0]] + [lax.ppermute(blocks[d], "seq", step(stride, -d)) for d in (1, 2, 3)]
+def swap_x(block, mask):
+    return lax.ppermute(block, "seq", [(s, s ^ (16 * mask)) for s in range(64)])
 
 
 def swap_z(block, mask):
@@ -474,17 +532,19 @@
     pair_a = swap_z(mine3, 1)
     (mine2,) = call(pick2_kernel, [((256, F), BF)], pos, key_act, value_act, mine3, us=1)
     got2 = swap_y(mine2, 1)
-    q, q_t, k, k_t, v, v_t = call(
-        order_kernel, [(wide, BF), (tall, BF)] * 3, pos, query_act, key_act, value_act, mine2, us=3,
+    q, q_t, k, k_t, v, v_t, q4 = call(
+        order_kernel, [(wide, BF), (tall, BF)] * 3 + [((16, F), BF)], pos, query_act, key_act, value_act, mine2, us=3,
     )
     (both,) = call(pair_kernel, [((128, F), BF)], mine3, pair_a, q, us=1)
     pair_b = swap_z(both, 3)
     (half2,) = call(pair_kernel, [((512, F), BF)], mine2, got2, both, us=1)
     kv2 = [half2, swap_y(half2, 3)]
+    (q4_both,) = call(pair_kernel, [((32, F), BF)], q4, swap_x(q4, 1), both, us=1)
+    q4 = [q4_both, swap_x(q4_both, 3)]
     pair_out = [(stat, F32), (stat, F32), ((128, T), F32)]
     m1a, l1a, o1a = call(functools.partial(first_kernel, 0), pair_out, q_t, k, v_t, half2, us=2)
-    all3, cot = call(pack3_kernel, [((256, F), BF), (wide, BF)], mine3, pair_a, pair_b, cotangent, m1a, us=1)
-    kv3 = spread(all3, 1)
+    all3, cot = call(pack3_kernel, [((192, F), BF), (wide, BF)], pair_a, pair_b, cotangent, m1a, q4[1], us=1)
+    kv3 = [*kv2, all3] + [swap_y(all3, n) for n in (1, 2, 3)]
     cot_z = swap(cot, 2)
     cot_c = swap(cot, 1)
     cot_zc = swap(cot_z, 1)
@@ -493,26 +553,25 @@
     m2, l2, o2 = call(
         second_kernel, [(stat, F32), (stat, F32), ((F, 128), F32)], *kv2, q, us=6
     )
-    (mine4,) = call(pack4_kernel, [((256, F), BF)], *kv3, m2, m1b, us=1)
-    kv4 = spread(mine4, 16)
+    kv4, mine4 = call(part4_kernel, [((256, F), BF), ((HD + 8, 128), F32)], *kv3, *q4, m2, m1b, us=1)
+    parts = [mine4] + [swap_x(mine4, n) for n in (1, 2, 3)]
     m, l, o, g, g_t, lse, delta, att_part = call(
         third_kernel,
         [((8, 128), F32), ((8, 128), F32), ((F, 128), F32), (wide, BF), (tall, BF), (stat, F32), (stat, F32),
          (tall, F32)],
         pos, *kv3, q, m1a, l1a, o1a, m1b, l1b, o1b, m2, l2, o2, *cots, out_weight, mine4, us=8,
     )
-    lse, delta, att, dq_first, *sent = call(
+    lse, delta, att, *sent = call(
         fourth_kernel,
-        [(stat, F32), (stat, F32), (tall, BF), ((F, 128), F32), ((512, F), F32)] + [((512, F), BF)] * 3,
-        pos, *kv4, q, m, l, o, g, g_t, lse, delta, att_part, *cots, us=6,
+        [(stat, F32), (stat, F32), (tall, BF), ((272, F), F32)] + [((272, F), BF)] * 3,
+        pos, *parts, m, l, o, g, g_t, lse, delta, att_part, *cots, us=6,
         scratch=[pltpu.VMEM((4, T, F), BF)],
     )
     own2, sent2, dq_first = call(
         second_back_kernel, [((512, F), F32), ((512, F), BF), ((F, 128), F32)],
-        *kv2, q, g, lse, delta, dq_first, us=2,
-    )
-    sent = lax.optimization_barrier((*sent, sent2))[:4]
-    r4 = bring(sent, 16)
+        *kv2, q, g, lse, delta, us=2,
+    )
+    r4 = [sent[0]] + [swap_x(sent[n], n) for n in (1, 2, 3)]
     got2 = swap_y(sent2, 3)
     send_c, keep_a, keep_b = call(
         project_kernel, [((2 * T, F), BF), (wide, F32), (wide, F32)], pos, att, out_weight, sent2, us=2
@@ -522,13 +581,19 @@
         [(wide, F32), (wide, F32), ((F, 128), F32), ((T, 128), F32), ((T, 128), F32), ((128, T), F32)],
         *kv3, q, q_t, k, k_t, v, g, g_t, lse, delta, dq_first, us=6,
     )
-    own2, sent2 = call(fold_kernel, [((256, F), F32), ((256, F), BF)], own2, got2, us=1)
+    own2, sent2 = call(fold_kernel, [((256, F), F32), ((256, F), BF)], own2, got2, r4[3], us=1)
     got2 = swap_y(sent2, 1)
+    dk4, dv4, dq4 = call(
+        fourth_back_kernel, [((128, F), F32), ((128, F), F32), ((HD, 128), F32)], kv4, *q4, *r4, us=1,
+    )
     sent = call(
-        reduce_y_kernel, [((320, F), F32)] + [((320, F), BF)] * 3, pos, *r4, dk3, dv3, got2, us=1,
-        scratch=[pltpu.VMEM((512, F), F32)],
-    )
-    r3 = bring(sent, 1)
+        reduce_y_kernel, [((320, F), F32)] + [((320, F), BF)] * 3, pos, *r4, dk4, dv4, dk3, dv3, sent2, us=1,
+        scratch=[pltpu.VMEM((256, F), F32)],
+    )
+    got4 = swap_x(lax.optimization_barrier((dq4, sent[0]))[0], 3)
+    dq4, dq4_send = call(fold4_kernel, [((HD, 128), F32)] * 2, dq4, got4, us=1)
+    got4 = swap_x(dq4_send, 1)
+    r3 = [sent[0]] + [swap_y(sent[n], n) for n in (1, 2, 3)]
     got_c = swap(lax.optimization_barrier((send_c, sent[0]))[0], 1)
     mix_own, mix_send = call(mix_kernel, [(wide, F32), (wide, BF)], keep_a, keep_b, got_c, us=1)
     mix_got = swap(mix_send, 2)
@@ -543,7 +608,7 @@
     rz = [sent[0]] + [swap_z(sent[n], n) for n in (1, 2, 3)]
     query_grad, dk_part, dv_part, dk_head, dv_head, mixed_out = call(
         natural_kernel, [(wide, BF), (wide, BF), (wide, BF), ((SEL3, F), F32), ((SEL3, F), F32), (wide, BF)],
-        pos, dq_first, dk_a, dv_a, dq_a, dk_b, dv_b, dq_b, own2, got2, mix_own, mix_got, sent[1], us=6,
+        pos, dq4, got4, dq_first, dk_a, dv_a, dq_a, dk_b, dv_b, dq_b, own2, got2, mix_own, mix_got, sent[1], us=6,
     )
     key_grad, value_grad, weight_grad = call(
         last_kernel, [(wide, BF), (wide, BF), ((16, F), F32)],

time: 87.2 us -> 83.1 us (0.953)
  waiting for transfers between devices: 22.3 us -> 9.82 us
  starting transfers between devices: 37.1 us -> 45.6 us
    ppermute x12 -> x10, waiting for transfers between devices: 15.8 us -> 6.25 us  [swap_x(): return lax.ppermute(block, 'seq', [(s, s ^ 16 * mask) for s in range(64)])]
    ppermute x4 -> x10, starting transfers between devices: 7.76 us -> 15.8 us  [swap_y(): return lax.ppermute(block, 'seq', [(s, s ^ mask) for s in range(64)])]
    ppermute x4 -> x10, waiting for transfers between devices: 5.8 us -> 1.23 us  [swap_y(): return lax.ppermute(block, 'seq', [(s, s ^ mask) for s in range(64)])]
    ppermute x5, waiting for transfers between devices: 0.72 us -> 2.33 us  [swap_z(): return lax.ppermute(block, 'seq', [(s, s ^ 4 * mask) for s in range(64)])]
    ppermute x12 -> x10, starting transfers between devices: 13 us -> 13.4 us  [swap_x(): return lax.ppermute(block, 'seq', [(s, s ^ 16 * mask) for s in range(64)])]
    pallas_call x22 -> x25, Pallas kernels: 24.5 us -> 24.6 us  [call(): pl.pallas_call(kernel, out_shape=[jax.ShapeDtypeStruct(shape, dtype) for...]
  transfers between devices with their start and end apart: 26 -> 30, of which waited for: 11 -> 8; matrix products, arithmetic and copies ran while one was open for 0% -> 0% of each run, Pallas kernels for 21% -> 23%
where the time goes in v3:
time: 83.1 us; the launch traced here: 83 us
  starting transfers between devices  45.6 us (55%)
  Pallas kernels  24.6 us (30%)
  waiting for transfers between devices  9.82 us (12%)
  local copies, waits for them, and re-layouts  1.93 us (2%)
  between operations  0.97 us (1%)
    pallas_call x25, Pallas kernels, call(): pl.pallas_call(kernel, out_shape=[jax.ShapeDtypeStruct(shape, dtype) for...  24.6 us
    ppermute x10, starting transfers between devices, swap_y(): return lax.ppermute(block, 'seq', [(s, s ^ mask) for s in range(64)])  15.8 us
    ppermute x5, starting transfers between devices, swap_z(): return lax.ppermute(block, 'seq', [(s, s ^ 4 * mask) for s in range(64)])  13.6 us
    ppermute x10, starting transfers between devices, swap_x(): return lax.ppermute(block, 'seq', [(s, s ^ 16 * mask) for s in range(64)])  13.4 us
    ppermute x10, waiting for transfers between devices, swap_x(): return lax.ppermute(block, 'seq', [(s, s ^ 16 * mask) for s in range(64)])  6.25 us
    ppermute x5, starting transfers between devices, swap(): return lax.ppermute(block, 'head', [(s, s ^ mask) for s in range(4)])  2.79 us
    ppermute x5, waiting for transfers between devices, swap_z(): return lax.ppermute(block, 'seq', [(s, s ^ 4 * mask) for s in range(64)])  2.33 us
    unnamed x10, local copies, waits for them, and re-layouts  1.93 us
  transfers between devices with their start and end apart: 30, of which 8 were waited for; matrix products, arithmetic and copies ran while one was open for 0% of the time, Pallas kernels for 23%

profile of v3, /device:TPU:32, one launch (start us, length us, event | category | flops | bytes accessed | tf_op | source)
XLA Modules:
  0.0 83.0 jit_solution(9727742132097861375)
XLA Ops:
  3.5 3.4 %collective-permute-start.1 = (bf16[64,256]{1,0:T(8,128)(2,1)S(1)}, bf16[64,256]{1,0:T(8,128)(2,1)S(1)}, u32[]{:S(2)}, u32[]{:S(2)}) collective-permute-start(bf16[64,256]{1,0:T(8,128)(2,1)S(1)} %pick3_kernel.1._p3.a), channel_id=1, source_target_pairs={{0,16},{4,20},{8,24},{12,28},{16,0},{20,4},{24,8},{28,12},{32,48},... | collective-permute-start | bytes 98312 | tf_op jit(solution)/shard_map/ppermute | solution.py:514
  7.7 1.7 %collective-permute-start = (bf16[256,256]{1,0:T(8,128)(2,1)S(1)}, bf16[256,256]{1,0:T(8,128)(2,1)S(1)}, u32[]{:S(2)}, u32[]{:S(2)}) collective-permute-start(bf16[256,256]{1,0:T(8,128)(2,1)S(1)} %pick2_kernel.1._s.a), channel_id=1, source_target_pairs={{0,4},{4,0},{8,12},{12,8},{16,20},{20,16},{24,28},{28,24},{32,36},... | collective-permute-start | bytes 393224 | tf_op jit(solution)/shard_map/ppermute | solution.py:518
  9.4 2.0 %order_kernel.1 = (bf16[512,256]{1,0:T(8,128)(2,1)S(1)}, bf16[256,512]{1,0:T(8,128)(2,1)S(1)}, bf16[512,256]{1,0:T(8,128)(2,1)S(1)}, bf16[256,512]{1,0:T(8,128)(...) custom-call(s32[4]{0:T(128)S(1)} %pad_add_fusion.pos, ...), custom_call_target="tpu_custom_call" | custom-call | flops 1500000000 | bytes 3000000 | tf_op jit(solution)/shard_map/order_kernel/pallas_call | solution.py:497
  11.4 1.6 %collective-permute-start.4 = (bf16[16,256]{1,0:T(8,128)(2,1)S(1)}, bf16[16,256]{1,0:T(8,128)(2,1)S(1)}, u32[]{:S(2)}, u32[]{:S(2)}) collective-permute-start(bf16[16,256]{1,0:T(8,128)(2,1)S(1)} %get-tuple-element.88.a), channel_id=1, source_target_pairs={{0,64},{4,68},{8,72},{12,76},{16,80},{20,84},{24,88},{28,92},{32,9... | collective-permute-start | bytes 24584 | tf_op jit(solution)/shard_map/ppermute | solution.py:510
  13.0 3.7 %collective-permute-start.3 = (bf16[128,256]{1,0:T(8,128)(2,1)S(1)}, bf16[128,256]{1,0:T(8,128)(2,1)S(1)}, u32[]{:S(2)}, u32[]{:S(2)}) collective-permute-start(bf16[128,256]{1,0:T(8,128)(2,1)S(1)} %pair_kernel.3._s), channel_id=1, source_target_pairs={{0,48},{4,52},{8,56},{12,60},{16,32},{20,36},{24,40},{28,44},{32,1... | collective-permute-start | bytes 196616 | tf_op jit(solution)/shard_map/ppermute | solution.py:514
  16.7 2.1 %collective-permute-start.5 = (bf16[32,256]{1,0:T(8,128)(2,1)S(1)}, bf16[32,256]{1,0:T(8,128)(2,1)S(1)}, u32[]{:S(2)}, u32[]{:S(2)}) collective-permute-start(bf16[32,256]{1,0:T(8,128)(2,1)S(1)} %pair_kernel.5.qa), channel_id=1, source_target_pairs={{0,192},{4,196},{8,200},{12,204},{16,208},{20,212},{24,216},{28,22... | collective-permute-start | bytes 49160 | tf_op jit(solution)/shard_map/ppermute | solution.py:510
  18.8 2.3 %collective-permute-start.2 = (bf16[512,256]{1,0:T(8,128)(2,1)S(1)}, bf16[512,256]{1,0:T(8,128)(2,1)S(1)}, u32[]{:S(2)}, u32[]{:S(2)}) collective-permute-start(bf16[512,256]{1,0:T(8,128)(2,1)S(1)} %pair_kernel.4._s.a), channel_id=1, source_target_pairs={{0,12},{4,8},{8,4},{12,0},{16,28},{20,24},{24,20},{28,16},{32,44},... | collective-permute-start | bytes 786440 | tf_op jit(solution)/shard_map/ppermute | solution.py:518
  21.1 1.7 %first_kernel.2 = (f32[8,512]{1,0:T(8,128)S(1)}, f32[8,512]{1,0:T(8,128)S(1)}, f32[128,512]{1,0:T(8,128)S(1)}) custom-call(bf16[256,512]{1,0:T(8,128)(2,1)S(1)} %get-tuple-element.84.q_t, bf16[512,256]{1,0:T(8,128)(2,1)S(1)} %get-tuple-element.85.k, bf16[256,512]{1,0:T(8,128)(2,1)S(1)} %get-tuple-element.86.v_t, bf16[512,256]{1,0:T(8,128)(2,1)S(1)} %pair_kernel.4._s.a), custom_call_target="tpu_custom_call" | custom-call | flops 1000000000 | bytes 2000000 | tf_op jit(solution)/shard_map/first_kernel/pallas_call | solution.py:497
  22.8 1.1 %collective-permute-start.13 = (bf16[512,256]{1,0:T(8,128)(2,1)S(1)}, bf16[512,256]{1,0:T(8,128)(2,1)S(1)}, u32[]{:S(2)}, u32[]{:S(2)}) collective-permute-start(bf16[512,256]{1,0:T(8,128)(2,1)S(1)} %get-tuple-element.100.c0), channel_id=1, source_target_pairs={{0,2},{1,3},{2,0},{3,1},{4,6},{5,7},{6,4},{7,5},{8,10},{9,11},{10,... | collective-permute-start | bytes 786440 | tf_op jit(solution)/shard_map/ppermute | solution.py:522
  24.6 1.8 %collective-permute-start.7 = (bf16[192,256]{1,0:T(8,128)(2,1)S(1)}, bf16[192,256]{1,0:T(8,128)(2,1)S(1)}, u32[]{:S(2)}, u32[]{:S(2)}) collective-permute-start(bf16[192,256]{1,0:T(8,128)(2,1)S(1)} %get-tuple-element.89._s.c0.a0), channel_id=1, source_target_pairs={{0,8},{4,12},{8,0},{12,4},{16,24},{20,28},{24,16},{28,20},{32,40},... | collective-permute-start | bytes 294920 | tf_op jit(solution)/shard_map/ppermute | solution.py:518
  26.5 2.2 %collective-permute-start.8 = (bf16[192,256]{1,0:T(8,128)(2,1)S(1)}, bf16[192,256]{1,0:T(8,128)(2,1)S(1)}, u32[]{:S(2)}, u32[]{:S(2)}) collective-permute-start(bf16[192,256]{1,0:T(8,128)(2,1)S(1)} %get-tuple-element.89._s.c0.a0), channel_id=1, source_target_pairs={{0,12},{4,8},{8,4},{12,0},{16,28},{20,24},{24,20},{28,16},{32,44},... | collective-permute-start | bytes 294920 | tf_op jit(solution)/shard_map/ppermute | solution.py:518
  28.6 1.7 %first_kernel.3 = (f32[8,512]{1,0:T(8,128)S(1)}, f32[8,512]{1,0:T(8,128)S(1)}, f32[128,512]{1,0:T(8,128)S(1)}) custom-call(bf16[256,512]{1,0:T(8,128)(2,1)S(1)} %get-tuple-element.84.q_t, bf16[512,256]{1,0:T(8,128)(2,1)S(1)} %get-tuple-element.85.k, bf16[256,512]{1,0:T(8,128)(2,1)S(1)} %get-tuple-element.86.v_t, bf16[192,256]{1,0:T(8,128)(2,1)S(1)} %get-tuple-element.89._s.c0.a0), custom_call_target="tpu_custom_call" | custom-call | flops 1000000000 | bytes 2000000 | tf_op jit(solution)/shard_map/first_kernel/pallas_call | solution.py:497
  32.7 1.7 %collective-permute-start.10 = (f32[72,128]{1,0:T(8,128)S(1)}, f32[72,128]{1,0:T(8,128)S(1)}, u32[]{:S(2)}, u32[]{:S(2)}) collective-permute-start(f32[72,128]{1,0:T(8,128)S(1)} %get-tuple-element.93._p3.r0), channel_id=1, source_target_pairs={{0,128},{4,132},{8,136},{12,140},{16,144},{20,148},{24,152},{28,15... | collective-permute-start | bytes 110600 | tf_op jit(solution)/shard_map/ppermute | solution.py:510
  34.4 1.8 %collective-permute-start.11 = (f32[72,128]{1,0:T(8,128)S(1)}, f32[72,128]{1,0:T(8,128)S(1)}, u32[]{:S(2)}, u32[]{:S(2)}) collective-permute-start(f32[72,128]{1,0:T(8,128)S(1)} %get-tuple-element.93._p3.r0), channel_id=1, source_target_pairs={{0,192},{4,196},{8,200},{12,204},{16,208},{20,212},{24,216},{28,22... | collective-permute-start | bytes 110600 | tf_op jit(solution)/shard_map/ppermute | solution.py:510
  36.5 2.9 %third_kernel.1 = (f32[8,128]{1,0:T(8,128)S(1)}, f32[8,128]{1,0:T(8,128)S(1)}, f32[256,128]{1,0:T(8,128)S(1)}, bf16[512,256]{1,0:T(8,128)(2,1)S(1)}, bf16[256,51...) custom-call(s32[4]{0:T(128)S(1)} %pad_add_fusion.pos, ...), custom_call_target="tpu_custom_call" | custom-call | flops 4000000000 | bytes 8000000 | tf_op jit(solution)/shard_map/third_kernel/pallas_call | solution.py:497
  40.2 1.4 %fourth_kernel.1 = (f32[8,512]{1,0:T(8,128)S(1)}, f32[8,512]{1,0:T(8,128)S(1)}, bf16[256,512]{1,0:T(8,128)(2,1)S(1)}, f32[272,256]{1,0:T(8,128)S(1)}, bf16[272,2...) custom-call(s32[4]{0:T(128)S(1)} %pad_add_fusion.pos, ...), custom_call_target="tpu_custom_call" | custom-call | flops 3000000000 | bytes 6000000 | tf_op jit(solution)/shard_map/fourth_kernel/pallas_call | solution.py:497
  42.6 2.3 %collective-permute-start.18 = (bf16[512,256]{1,0:T(8,128)(2,1)S(1)}, bf16[512,256]{1,0:T(8,128)(2,1)S(1)}, u32[]{:S(2)}, u32[]{:S(2)}) collective-permute-start(bf16[512,256]{1,0:T(8,128)(2,1)S(1)} %get-tuple-element.124._s), channel_id=1, source_target_pairs={{0,12},{4,8},{8,4},{12,0},{16,28},{20,24},{24,20},{28,16},{32,44},... | collective-permute-start | bytes 786440 | tf_op jit(solution)/shard_map/ppermute | solution.py:518
  44.9 1.2 %collective-permute-start.17 = (bf16[272,256]{1,0:T(8,128)(2,1)S(1)}, bf16[272,256]{1,0:T(8,128)(2,1)S(1)}, u32[]{:S(2)}, u32[]{:S(2)}) collective-permute-start(bf16[272,256]{1,0:T(8,128)(2,1)S(1)} %get-tuple-element.112), channel_id=1, source_target_pairs={{0,192},{4,196},{8,200},{12,204},{16,208},{20,212},{24,216},{28,22... | collective-permute-start | bytes 417800 | tf_op jit(solution)/shard_map/ppermute | solution.py:510
  46.1 3.5 %collective-permute-start.16 = (bf16[272,256]{1,0:T(8,128)(2,1)S(1)}, bf16[272,256]{1,0:T(8,128)(2,1)S(1)}, u32[]{:S(2)}, u32[]{:S(2)}) collective-permute-start(bf16[272,256]{1,0:T(8,128)(2,1)S(1)} %get-tuple-element.111), channel_id=1, source_target_pairs={{0,128},{4,132},{8,136},{12,140},{16,144},{20,148},{24,152},{28,15... | collective-permute-start | bytes 417800 | tf_op jit(solution)/shard_map/ppermute | solution.py:510
  49.6 1.8 %third_back_kernel.1 = (f32[512,256]{1,0:T(8,128)S(1)}, f32[512,256]{1,0:T(8,128)S(1)}, f32[256,128]{1,0:T(8,128)S(1)}, f32[512,128]{1,0:T(8,128)S(1)}, f32[512,128]{1,0:T(8,128)S(1)}, /*index=5*/f32[128,512]{1,0:T(8,128)S(1)}) custom-call(bf16[512,256]{1,0:T(8,128)(2,1)S(1)} %pair_kernel.4._s.a, bf16[512,256]{1,0:T(8,128)(2,1)S(1)} %collective-permute-done.2.b, ...), custom_call_target="tpu_custom_call" | custom-call | flops 3000000000 | bytes 6000000 | tf_op jit(solution)/shard_map/third_back_kernel/pallas_call | solution.py:497
  52.5 1.6 %collective-permute-done.16.b2 = bf16[272,256]{1,0:T(8,128)(2,1)S(1)} collective-permute-done((bf16[272,256]{1,0:T(8,128)(2,1)S(1)}, bf16[272,256]{1,0:T(8,128)(2,1)S(1)}, u32[]{:S(2)}, u32[]{:S(2)}) %collective-permute-start.16) | collective-permute-done | bytes 139296 | tf_op jit(solution)/shard_map/ppermute | solution.py:510
  55.5 2.0 %collective-permute-start.24 = (bf16[320,256]{1,0:T(8,128)(2,1)S(1)}, bf16[320,256]{1,0:T(8,128)(2,1)S(1)}, u32[]{:S(2)}, u32[]{:S(2)}) collective-permute-start(bf16[320,256]{1,0:T(8,128)(2,1)S(1)} %get-tuple-element.134._s), channel_id=1, source_target_pairs={{0,4},{4,0},{8,12},{12,8},{16,20},{20,16},{24,28},{28,24},{32,36},... | collective-permute-start | bytes 491528 | tf_op jit(solution)/shard_map/ppermute | solution.py:518
  58.1 2.2 %collective-permute-start.26 = (bf16[320,256]{1,0:T(8,128)(2,1)S(1)}, bf16[320,256]{1,0:T(8,128)(2,1)S(1)}, u32[]{:S(2)}, u32[]{:S(2)}) collective-permute-start(bf16[320,256]{1,0:T(8,128)(2,1)S(1)} %get-tuple-element.147), channel_id=1, source_target_pairs={{0,12},{4,8},{8,4},{12,0},{16,28},{20,24},{24,20},{28,16},{32,44},... | collective-permute-start | bytes 491528 | tf_op jit(solution)/shard_map/ppermute | solution.py:518
  60.3 1.2 %collective-permute-start.19 = (f32[64,128]{1,0:T(8,128)S(1)}, f32[64,128]{1,0:T(8,128)S(1)}, u32[]{:S(2)}, u32[]{:S(2)}) collective-permute-start(f32[64,128]{1,0:T(8,128)S(1)} %get-tuple-element.127.own), channel_id=1, source_target_pairs={{0,192},{4,196},{8,200},{12,204},{16,208},{20,212},{24,216},{28,22... | collective-permute-start | bytes 98312 | tf_op jit(solution)/shard_map/ppermute | solution.py:510
  61.6 3.8 %collective-permute-done.19.got = f32[64,128]{1,0:T(8,128)S(1)} collective-permute-done((f32[64,128]{1,0:T(8,128)S(1)}, f32[64,128]{1,0:T(8,128)S(1)}, u32[]{:S(2)}, u32[]{:S(2)}) %collective-permute-start.19) | collective-permute-done | bytes 32800 | tf_op jit(solution)/shard_map/ppermute | solution.py:510
  66.5 1.4 %pair_back_kernel.1 = (f32[512,128]{1,0:T(8,128)S(1)}, f32[512,128]{1,0:T(8,128)S(1)}, f32[128,512]{1,0:T(8,128)S(1)}) custom-call(bf16[512,256]{1,0:T(8,128)(2,1)S(1)} %get-tuple-element.83._s.q, bf16[256,512]{1,0:T(8,128)(2,1)S(1)} %get-tuple-element.84.q_t, bf16[512,256]{1,0:T(8,128)(2,1)S(1)} %get-tuple-element.85.k, ...), custom_call_target="tpu_custom_call" | custom-call | flops 3000000000 | bytes 6000000 | tf_op jit(solution)/shard_map/pair_back_kernel/pallas_call | solution.py:497
  69.5 1.6 %collective-permute-start.27 = (bf16[80,256]{1,0:T(8,128)(2,1)S(1)}, bf16[80,256]{1,0:T(8,128)(2,1)S(1)}, u32[]{:S(2)}, u32[]{:S(2)}) collective-permute-start(bf16[80,256]{1,0:T(8,128)(2,1)S(1)} %get-tuple-element.148._s), channel_id=1, source_target_pairs={{0,16},{4,20},{8,24},{12,28},{16,0},{20,4},{24,8},{28,12},{32,48},... | collective-permute-start | bytes 122888 | tf_op jit(solution)/shard_map/ppermute | solution.py:514
  71.1 3.6 %collective-permute-start.28 = (bf16[80,256]{1,0:T(8,128)(2,1)S(1)}, bf16[80,256]{1,0:T(8,128)(2,1)S(1)}, u32[]{:S(2)}, u32[]{:S(2)}) collective-permute-start(bf16[80,256]{1,0:T(8,128)(2,1)S(1)} %get-tuple-element.152), channel_id=1, source_target_pairs={{0,32},{4,36},{8,40},{12,44},{16,48},{20,52},{24,56},{28,60},{32,0... | collective-permute-start | bytes 122888 | tf_op jit(solution)/shard_map/ppermute | solution.py:514
  74.7 1.4 %collective-permute-start.29 = (bf16[80,256]{1,0:T(8,128)(2,1)S(1)}, bf16[80,256]{1,0:T(8,128)(2,1)S(1)}, u32[]{:S(2)}, u32[]{:S(2)}) collective-permute-start(bf16[80,256]{1,0:T(8,128)(2,1)S(1)} %get-tuple-element.153), channel_id=1, source_target_pairs={{0,48},{4,52},{8,56},{12,60},{16,32},{20,36},{24,40},{28,44},{32,1... | collective-permute-start | bytes 122888 | tf_op jit(solution)/shard_map/ppermute | solution.py:514
  76.1 2.8 %natural_kernel.1 = (bf16[512,256]{1,0:T(8,128)(2,1)}, bf16[512,256]{1,0:T(8,128)(2,1)S(1)}, bf16[512,256]{1,0:T(8,128)(2,1)S(1)}, f32[32,256]{1,0:T(8,128)S(1)}...) custom-call(s32[4]{0:T(128)S(1)} %pad_add_fusion.pos, f32[64,128]{1,0:T(8,128)S(1)} %get-tuple-element.128.e0, ...), custom_call_target="tpu_custom_call" | custom-call | flops 3000000000 | bytes 6000000 | tf_op jit(solution)/shard_map/natural_kernel/pallas_call | solution.py:497
  79.0 2.3 %collective-permute-done.29.b3 = bf16[80,256]{1,0:T(8,128)(2,1)S(1)} collective-permute-done((bf16[80,256]{1,0:T(8,128)(2,1)S(1)}, bf16[80,256]{1,0:T(8,128)(2,1)S(1)}, u32[]{:S(2)}, u32[]{:S(2)}) %collective-permute-start.29) | collective-permute-done | bytes 40992 | tf_op jit(solution)/shard_map/ppermute | solution.py:514
  81.2 1.8 %last_kernel.1 = (bf16[512,256]{1,0:T(8,128)(2,1)}, bf16[512,256]{1,0:T(8,128)(2,1)}, f32[16,256]{1,0:T(8,128)}) custom-call(s32[4]{0:T(128)S(1)} %pad_add_fusion.pos, f32[80,256]{1,0:T(8,128)S(1)} %get-tuple-element.151.own, bf16[80,256]{1,0:T(8,128)(2,1)S(1)} %collective-permute-done.27.b1, bf16[80,256]{1,0:T(8,128)(2,1)S(1)} %collective-permute-done.28.b2, ...), custom_call_target="tpu_custom_call" | custom-call | flops 1000000000 | bytes 2000000 | tf_op jit(solution)/shard_map/last_kernel/pallas_call | solution.py:497
  (64 shorter events, 14.7 us)
Async XLA Ops:
  3.5 5.9 %copy-start.3 = (bf16[512,256]{1,0:T(8,128)(2,1)S(1)}, bf16[512,256]{1,0:T(8,128)(2,1)}, u32[]{:S(2)}) copy-start(bf16[512,256]{1,0:T(8,128)(2,1)} %q.1) | copy-start | bytes 786436
  3.5 9.5 %collective-permute-start.1 = (bf16[64,256]{1,0:T(8,128)(2,1)S(1)}, bf16[64,256]{1,0:T(8,128)(2,1)S(1)}, u32[]{:S(2)}, u32[]{:S(2)}) collective-permute-start(bf16[64,256]{1,0:T(8,128)(2,1)S(1)} %pick3_kernel.1._p3.a), channel_id=1, source_target_pairs={{0,16},{4,20},{8,24},{12,28},{16,0},{20,4},{24,8},{28,12},{32,48},... | collective-permute-start | bytes 98312 | tf_op jit(solution)/shard_map/ppermute | solution.py:514
  7.7 11.0 %collective-permute-start = (bf16[256,256]{1,0:T(8,128)(2,1)S(1)}, bf16[256,256]{1,0:T(8,128)(2,1)S(1)}, u32[]{:S(2)}, u32[]{:S(2)}) collective-permute-start(bf16[256,256]{1,0:T(8,128)(2,1)S(1)} %pick2_kernel.1._s.a), channel_id=1, source_target_pairs={{0,4},{4,0},{8,12},{12,8},{16,20},{20,16},{24,28},{28,24},{32,36},... | collective-permute-start | bytes 393224 | tf_op jit(solution)/shard_map/ppermute | solution.py:518
  11.4 5.3 %collective-permute-start.4 = (bf16[16,256]{1,0:T(8,128)(2,1)S(1)}, bf16[16,256]{1,0:T(8,128)(2,1)S(1)}, u32[]{:S(2)}, u32[]{:S(2)}) collective-permute-start(bf16[16,256]{1,0:T(8,128)(2,1)S(1)} %get-tuple-element.88.a), channel_id=1, source_target_pairs={{0,64},{4,68},{8,72},{12,76},{16,80},{20,84},{24,88},{28,92},{32,9... | collective-permute-start | bytes 24584 | tf_op jit(solution)/shard_map/ppermute | solution.py:510
  13.0 9.8 %collective-permute-start.3 = (bf16[128,256]{1,0:T(8,128)(2,1)S(1)}, bf16[128,256]{1,0:T(8,128)(2,1)S(1)}, u32[]{:S(2)}, u32[]{:S(2)}) collective-permute-start(bf16[128,256]{1,0:T(8,128)(2,1)S(1)} %pair_kernel.3._s), channel_id=1, source_target_pairs={{0,48},{4,52},{8,56},{12,60},{16,32},{20,36},{24,40},{28,44},{32,1... | collective-permute-start | bytes 196616 | tf_op jit(solution)/shard_map/ppermute | solution.py:514
  16.7 6.1 %collective-permute-start.5 = (bf16[32,256]{1,0:T(8,128)(2,1)S(1)}, bf16[32,256]{1,0:T(8,128)(2,1)S(1)}, u32[]{:S(2)}, u32[]{:S(2)}) collective-permute-start(bf16[32,256]{1,0:T(8,128)(2,1)S(1)} %pair_kernel.5.qa), channel_id=1, source_target_pairs={{0,192},{4,196},{8,200},{12,204},{16,208},{20,212},{24,216},{28,22... | collective-permute-start | bytes 49160 | tf_op jit(solution)/shard_map/ppermute | solution.py:510
  18.8 11.6 %collective-permute-start.2 = (bf16[512,256]{1,0:T(8,128)(2,1)S(1)}, bf16[512,256]{1,0:T(8,128)(2,1)S(1)}, u32[]{:S(2)}, u32[]{:S(2)}) collective-permute-start(bf16[512,256]{1,0:T(8,128)(2,1)S(1)} %pair_kernel.4._s.a), channel_id=1, source_target_pairs={{0,12},{4,8},{8,4},{12,0},{16,28},{20,24},{24,20},{28,16},{32,44},... | collective-permute-start | bytes 786440 | tf_op jit(solution)/shard_map/ppermute | solution.py:518
  22.8 7.6 %collective-permute-start.13 = (bf16[512,256]{1,0:T(8,128)(2,1)S(1)}, bf16[512,256]{1,0:T(8,128)(2,1)S(1)}, u32[]{:S(2)}, u32[]{:S(2)}) collective-permute-start(bf16[512,256]{1,0:T(8,128)(2,1)S(1)} %get-tuple-element.100.c0), channel_id=1, source_target_pairs={{0,2},{1,3},{2,0},{3,1},{4,6},{5,7},{6,4},{7,5},{8,10},{9,11},{10,... | collective-permute-start | bytes 786440 | tf_op jit(solution)/shard_map/ppermute | solution.py:522
  23.9 7.9 %collective-permute-start.6 = (bf16[192,256]{1,0:T(8,128)(2,1)S(1)}, bf16[192,256]{1,0:T(8,128)(2,1)S(1)}, u32[]{:S(2)}, u32[]{:S(2)}) collective-permute-start(bf16[192,256]{1,0:T(8,128)(2,1)S(1)} %get-tuple-element.89._s.c0.a0), channel_id=1, source_target_pairs={{0,4},{4,0},{8,12},{12,8},{16,20},{20,16},{24,28},{28,24},{32,36},... | collective-permute-start | bytes 294920 | tf_op jit(solution)/shard_map/ppermute | solution.py:518
  24.6 7.3 %collective-permute-start.7 = (bf16[192,256]{1,0:T(8,128)(2,1)S(1)}, bf16[192,256]{1,0:T(8,128)(2,1)S(1)}, u32[]{:S(2)}, u32[]{:S(2)}) collective-permute-start(bf16[192,256]{1,0:T(8,128)(2,1)S(1)} %get-tuple-element.89._s.c0.a0), channel_id=1, source_target_pairs={{0,8},{4,12},{8,0},{12,4},{16,24},{20,28},{24,16},{28,20},{32,40},... | collective-permute-start | bytes 294920 | tf_op jit(solution)/shard_map/ppermute | solution.py:518
  26.5 5.8 %collective-permute-start.8 = (bf16[192,256]{1,0:T(8,128)(2,1)S(1)}, bf16[192,256]{1,0:T(8,128)(2,1)S(1)}, u32[]{:S(2)}, u32[]{:S(2)}) collective-permute-start(bf16[192,256]{1,0:T(8,128)(2,1)S(1)} %get-tuple-element.89._s.c0.a0), channel_id=1, source_target_pairs={{0,12},{4,8},{8,4},{12,0},{16,28},{20,24},{24,20},{28,16},{32,44},... | collective-permute-start | bytes 294920 | tf_op jit(solution)/shard_map/ppermute | solution.py:518
  30.4 6.1 %collective-permute-start.12 = (bf16[512,256]{1,0:T(8,128)(2,1)S(1)}, bf16[512,256]{1,0:T(8,128)(2,1)S(1)}, u32[]{:S(2)}, u32[]{:S(2)}) collective-permute-start(bf16[512,256]{1,0:T(8,128)(2,1)S(1)} %get-tuple-element.100.c0), channel_id=1, source_target_pairs={{0,1},{1,0},{2,3},{3,2},{4,5},{5,4},{6,7},{7,6},{8,9},{9,8},{10,11... | collective-permute-start | bytes 786440 | tf_op jit(solution)/shard_map/ppermute | solution.py:522
  30.5 6.0 %collective-permute-start.14 = (bf16[512,256]{1,0:T(8,128)(2,1)S(1)}, bf16[512,256]{1,0:T(8,128)(2,1)S(1)}, u32[]{:S(2)}, u32[]{:S(2)}) collective-permute-start(bf16[512,256]{1,0:T(8,128)(2,1)S(1)} %collective-permute-done.13.c2), channel_id=1, source_target_pairs={{0,1},{1,0},{2,3},{3,2},{4,5},{5,4},{6,7},{7,6},{8,9},{9,8},{10,11... | collective-permute-start | bytes 786440 | tf_op jit(solution)/shard_map/ppermute | solution.py:522
  32.3 4.2 %copy-start = (bf16[256,1024]{1,0:T(8,128)(2,1)S(1)}, bf16[256,1024]{1,0:T(8,128)(2,1)}, u32[]{:S(2)}) copy-start(bf16[256,1024]{1,0:T(8,128)(2,1)} %w.3) | copy-start | bytes 1572868
  32.7 6.7 %collective-permute-start.10 = (f32[72,128]{1,0:T(8,128)S(1)}, f32[72,128]{1,0:T(8,128)S(1)}, u32[]{:S(2)}, u32[]{:S(2)}) collective-permute-start(f32[72,128]{1,0:T(8,128)S(1)} %get-tuple-element.93._p3.r0), channel_id=1, source_target_pairs={{0,128},{4,132},{8,136},{12,140},{16,144},{20,148},{24,152},{28,15... | collective-permute-start | bytes 110600 | tf_op jit(solution)/shard_map/ppermute | solution.py:510
  34.4 5.2 %collective-permute-start.11 = (f32[72,128]{1,0:T(8,128)S(1)}, f32[72,128]{1,0:T(8,128)S(1)}, u32[]{:S(2)}, u32[]{:S(2)}) collective-permute-start(f32[72,128]{1,0:T(8,128)S(1)} %get-tuple-element.93._p3.r0), channel_id=1, source_target_pairs={{0,192},{4,196},{8,200},{12,204},{16,208},{20,212},{24,216},{28,22... | collective-permute-start | bytes 110600 | tf_op jit(solution)/shard_map/ppermute | solution.py:510
  36.3 4.0 %collective-permute-start.9 = (f32[72,128]{1,0:T(8,128)S(1)}, f32[72,128]{1,0:T(8,128)S(1)}, u32[]{:S(2)}, u32[]{:S(2)}) collective-permute-start(f32[72,128]{1,0:T(8,128)S(1)} %get-tuple-element.93._p3.r0), channel_id=1, source_target_pairs={{0,64},{4,68},{8,72},{12,76},{16,80},{20,84},{24,88},{28,92},{32,9... | collective-permute-start | bytes 110600 | tf_op jit(solution)/shard_map/ppermute | solution.py:510
  42.6 11.9 %collective-permute-start.18 = (bf16[512,256]{1,0:T(8,128)(2,1)S(1)}, bf16[512,256]{1,0:T(8,128)(2,1)S(1)}, u32[]{:S(2)}, u32[]{:S(2)}) collective-permute-start(bf16[512,256]{1,0:T(8,128)(2,1)S(1)} %get-tuple-element.124._s), channel_id=1, source_target_pairs={{0,12},{4,8},{8,4},{12,0},{16,28},{20,24},{24,20},{28,16},{32,44},... | collective-permute-start | bytes 786440 | tf_op jit(solution)/shard_map/ppermute | solution.py:518
  44.9 7.6 %collective-permute-start.17 = (bf16[272,256]{1,0:T(8,128)(2,1)S(1)}, bf16[272,256]{1,0:T(8,128)(2,1)S(1)}, u32[]{:S(2)}, u32[]{:S(2)}) collective-permute-start(bf16[272,256]{1,0:T(8,128)(2,1)S(1)} %get-tuple-element.112), channel_id=1, source_target_pairs={{0,192},{4,196},{8,200},{12,204},{16,208},{20,212},{24,216},{28,22... | collective-permute-start | bytes 417800 | tf_op jit(solution)/shard_map/ppermute | solution.py:510
  46.1 6.4 %collective-permute-start.15 = (bf16[272,256]{1,0:T(8,128)(2,1)S(1)}, bf16[272,256]{1,0:T(8,128)(2,1)S(1)}, u32[]{:S(2)}, u32[]{:S(2)}) collective-permute-start(bf16[272,256]{1,0:T(8,128)(2,1)S(1)} %get-tuple-element.110), channel_id=1, source_target_pairs={{0,64},{4,68},{8,72},{12,76},{16,80},{20,84},{24,88},{28,92},{32,9... | collective-permute-start | bytes 417800 | tf_op jit(solution)/shard_map/ppermute | solution.py:510
  46.1 8.0 %collective-permute-start.16 = (bf16[272,256]{1,0:T(8,128)(2,1)S(1)}, bf16[272,256]{1,0:T(8,128)(2,1)S(1)}, u32[]{:S(2)}, u32[]{:S(2)}) collective-permute-start(bf16[272,256]{1,0:T(8,128)(2,1)S(1)} %get-tuple-element.111), channel_id=1, source_target_pairs={{0,128},{4,132},{8,136},{12,140},{16,144},{20,148},{24,152},{28,15... | collective-permute-start | bytes 417800 | tf_op jit(solution)/shard_map/ppermute | solution.py:510
  55.3 5.0 %collective-permute-start.22 = (bf16[1024,256]{1,0:T(8,128)(2,1)S(1)}, bf16[1024,256]{1,0:T(8,128)(2,1)S(1)}, u32[]{:S(2)}, u32[]{:S(2)}) collective-permute-start(bf16[1024,256]{1,0:T(8,128)(2,1)S(1)} %get-tuple-element.143), channel_id=1, source_target_pairs={{0,1},{1,0},{2,3},{3,2},{4,5},{5,4},{6,7},{7,6},{8,9},{9,8},{10,11... | collective-permute-start | bytes 1572872 | tf_op jit(solution)/shard_map/ppermute | solution.py:522
  55.4 20.7 %collective-permute-start.21 = (bf16[256,256]{1,0:T(8,128)(2,1)S(1)}, bf16[256,256]{1,0:T(8,128)(2,1)S(1)}, u32[]{:S(2)}, u32[]{:S(2)}) collective-permute-start(bf16[256,256]{1,0:T(8,128)(2,1)S(1)} %get-tuple-element.125._s), channel_id=1, source_target_pairs={{0,4},{4,0},{8,12},{12,8},{16,20},{20,16},{24,28},{28,24},{32,36},... | collective-permute-start | bytes 393224 | tf_op jit(solution)/shard_map/ppermute | solution.py:518
  55.5 12.4 %collective-permute-start.24 = (bf16[320,256]{1,0:T(8,128)(2,1)S(1)}, bf16[320,256]{1,0:T(8,128)(2,1)S(1)}, u32[]{:S(2)}, u32[]{:S(2)}) collective-permute-start(bf16[320,256]{1,0:T(8,128)(2,1)S(1)} %get-tuple-element.134._s), channel_id=1, source_target_pairs={{0,4},{4,0},{8,12},{12,8},{16,20},{20,16},{24,28},{28,24},{32,36},... | collective-permute-start | bytes 491528 | tf_op jit(solution)/shard_map/ppermute | solution.py:518
  57.5 11.3 %collective-permute-start.25 = (bf16[320,256]{1,0:T(8,128)(2,1)S(1)}, bf16[320,256]{1,0:T(8,128)(2,1)S(1)}, u32[]{:S(2)}, u32[]{:S(2)}) collective-permute-start(bf16[320,256]{1,0:T(8,128)(2,1)S(1)} %get-tuple-element.146), channel_id=1, source_target_pairs={{0,8},{4,12},{8,0},{12,4},{16,24},{20,28},{24,16},{28,20},{32,40},... | collective-permute-start | bytes 491528 | tf_op jit(solution)/shard_map/ppermute | solution.py:518
  58.1 10.7 %collective-permute-start.26 = (bf16[320,256]{1,0:T(8,128)(2,1)S(1)}, bf16[320,256]{1,0:T(8,128)(2,1)S(1)}, u32[]{:S(2)}, u32[]{:S(2)}) collective-permute-start(bf16[320,256]{1,0:T(8,128)(2,1)S(1)} %get-tuple-element.147), channel_id=1, source_target_pairs={{0,12},{4,8},{8,4},{12,0},{16,28},{20,24},{24,20},{28,16},{32,44},... | collective-permute-start | bytes 491528 | tf_op jit(solution)/shard_map/ppermute | solution.py:518
  60.3 5.1 %collective-permute-start.19 = (f32[64,128]{1,0:T(8,128)S(1)}, f32[64,128]{1,0:T(8,128)S(1)}, u32[]{:S(2)}, u32[]{:S(2)}) collective-permute-start(f32[64,128]{1,0:T(8,128)S(1)} %get-tuple-element.127.own), channel_id=1, source_target_pairs={{0,192},{4,196},{8,200},{12,204},{16,208},{20,212},{24,216},{28,22... | collective-permute-start | bytes 98312 | tf_op jit(solution)/shard_map/ppermute | solution.py:510
  65.4 10.7 %collective-permute-start.23 = (bf16[512,256]{1,0:T(8,128)(2,1)S(1)}, bf16[512,256]{1,0:T(8,128)(2,1)S(1)}, u32[]{:S(2)}, u32[]{:S(2)}) collective-permute-start(bf16[512,256]{1,0:T(8,128)(2,1)S(1)} %get-tuple-element.145), channel_id=1, source_target_pairs={{0,2},{1,3},{2,0},{3,1},{4,6},{5,7},{6,4},{7,5},{8,10},{9,11},{10,... | collective-permute-start | bytes 786440 | tf_op jit(solution)/shard_map/ppermute | solution.py:522
  67.9 6.7 %collective-permute-start.20 = (f32[64,128]{1,0:T(8,128)S(1)}, f32[64,128]{1,0:T(8,128)S(1)}, u32[]{:S(2)}, u32[]{:S(2)}) collective-permute-start(f32[64,128]{1,0:T(8,128)S(1)} %get-tuple-element.129), channel_id=1, source_target_pairs={{0,64},{4,68},{8,72},{12,76},{16,80},{20,84},{24,88},{28,92},{32,9... | collective-permute-start | bytes 98312 | tf_op jit(solution)/shard_map/ppermute | solution.py:510
  69.5 9.4 %collective-permute-start.27 = (bf16[80,256]{1,0:T(8,128)(2,1)S(1)}, bf16[80,256]{1,0:T(8,128)(2,1)S(1)}, u32[]{:S(2)}, u32[]{:S(2)}) collective-permute-start(bf16[80,256]{1,0:T(8,128)(2,1)S(1)} %get-tuple-element.148._s), channel_id=1, source_target_pairs={{0,16},{4,20},{8,24},{12,28},{16,0},{20,4},{24,8},{28,12},{32,48},... | collective-permute-start | bytes 122888 | tf_op jit(solution)/shard_map/ppermute | solution.py:514
  71.1 7.9 %collective-permute-start.28 = (bf16[80,256]{1,0:T(8,128)(2,1)S(1)}, bf16[80,256]{1,0:T(8,128)(2,1)S(1)}, u32[]{:S(2)}, u32[]{:S(2)}) collective-permute-start(bf16[80,256]{1,0:T(8,128)(2,1)S(1)} %get-tuple-element.152), channel_id=1, source_target_pairs={{0,32},{4,36},{8,40},{12,44},{16,48},{20,52},{24,56},{28,60},{32,0... | collective-permute-start | bytes 122888 | tf_op jit(solution)/shard_map/ppermute | solution.py:514
  74.7 6.6 %collective-permute-start.29 = (bf16[80,256]{1,0:T(8,128)(2,1)S(1)}, bf16[80,256]{1,0:T(8,128)(2,1)S(1)}, u32[]{:S(2)}, u32[]{:S(2)}) collective-permute-start(bf16[80,256]{1,0:T(8,128)(2,1)S(1)} %get-tuple-element.153), channel_id=1, source_target_pairs={{0,48},{4,52},{8,56},{12,60},{16,32},{20,36},{24,40},{28,44},{32,1... | collective-permute-start | bytes 122888 | tf_op jit(solution)/shard_map/ppermute | solution.py:514
  (3 other events, 3.6 us)

commit v4 on v3

--- a/solution.py
+++ b/solution.py
@@ -582,7 +582,6 @@
         *kv3, q, q_t, k, k_t, v, g, g_t, lse, delta, dq_first, us=6,
     )
     own2, sent2 = call(fold_kernel, [((256, F), F32), ((256, F), BF)], own2, got2, r4[3], us=1)
-    got2 = swap_y(sent2, 1)
     dk4, dv4, dq4 = call(
         fourth_back_kernel, [((128, F), F32), ((128, F), F32), ((HD, 128), F32)], kv4, *q4, *r4, us=1,
     )
@@ -597,6 +596,7 @@
     got_c = swap(lax.optimization_barrier((send_c, sent[0]))[0], 1)
     mix_own, mix_send = call(mix_kernel, [(wide, F32), (wide, BF)], keep_a, keep_b, got_c, us=1)
     mix_got = swap(mix_send, 2)
+    got2 = swap_y(lax.optimization_barrier((sent2, r3[1]))[0], 1)
     dk_b, dv_b, dq_b = call(
         pair_back_kernel, [((T, 128), F32), ((T, 128), F32), ((128, T), F32)],
         q, q_t, k, k_t, v, g, g_t, lse, delta, sent[1], us=6,

time: 83.1 us -> 83 us (level)
    ppermute x10, waiting for transfers between devices: 6.25 us -> 2.59 us  [swap_x(): return lax.ppermute(block, 'seq', [(s, s ^ 16 * mask) for s in range(64)])]
    ppermute x10, waiting for transfers between devices: 1.23 us -> 4.26 us  [swap_y(): return lax.ppermute(block, 'seq', [(s, s ^ mask) for s in range(64)])]
  transfers between devices with their start and end apart: 30 -> 30, of which waited for: 8 -> 10; matrix products, arithmetic and copies ran while one was open for 0% -> 0% of each run, Pallas kernels for 23% -> 23%
where the time goes in v4:
time: 83 us; the launch traced here: 82.9 us
  starting transfers between devices  46.1 us (56%)
  Pallas kernels  24.6 us (30%)
  waiting for transfers between devices  9.19 us (11%)
  local copies, waits for them, and re-layouts  1.93 us (2%)
  between operations  0.96 us (1%)
    pallas_call x25, Pallas kernels, call(): pl.pallas_call(kernel, out_shape=[jax.ShapeDtypeStruct(shape, dtype) for...  24.6 us
    ppermute x10, starting transfers between devices, swap_y(): return lax.ppermute(block, 'seq', [(s, s ^ mask) for s in range(64)])  15.7 us
    ppermute x10, starting transfers between devices, swap_x(): return lax.ppermute(block, 'seq', [(s, s ^ 16 * mask) for s in range(64)])  13.9 us
    ppermute x5, starting transfers between devices, swap_z(): return lax.ppermute(block, 'seq', [(s, s ^ 4 * mask) for s in range(64)])  13.6 us
    ppermute x10, waiting for transfers between devices, swap_y(): return lax.ppermute(block, 'seq', [(s, s ^ mask) for s in range(64)])  4.26 us
    ppermute x5, starting transfers between devices, swap(): return lax.ppermute(block, 'head', [(s, s ^ mask) for s in range(4)])  2.88 us
    ppermute x10, waiting for transfers between devices, swap_x(): return lax.ppermute(block, 'seq', [(s, s ^ 16 * mask) for s in range(64)])  2.59 us
    ppermute x5, waiting for transfers between devices, swap_z(): return lax.ppermute(block, 'seq', [(s, s ^ 4 * mask) for s in range(64)])  2.33 us
  transfers between devices with their start and end apart: 30, of which 10 were waited for; matrix products, arithmetic and copies ran while one was open for 0% of the time, Pallas kernels for 23%

profile of v4, /device:TPU:32, one launch (start us, length us, event | category | flops | bytes accessed | tf_op | source)
XLA Modules:
  0.0 82.9 jit_solution(6412988735373485157)
XLA Ops:
  3.5 3.4 %collective-permute-start.1 = (bf16[64,256]{1,0:T(8,128)(2,1)S(1)}, bf16[64,256]{1,0:T(8,128)(2,1)S(1)}, u32[]{:S(2)}, u32[]{:S(2)}) collective-permute-start(bf16[64,256]{1,0:T(8,128)(2,1)S(1)} %pick3_kernel.1._p3.a), channel_id=1, source_target_pairs={{0,16},{4,20},{8,24},{12,28},{16,0},{20,4},{24,8},{28,12},{32,48},... | collective-permute-start | bytes 98312 | tf_op jit(solution)/shard_map/ppermute | solution.py:514
  7.7 1.7 %collective-permute-start = (bf16[256,256]{1,0:T(8,128)(2,1)S(1)}, bf16[256,256]{1,0:T(8,128)(2,1)S(1)}, u32[]{:S(2)}, u32[]{:S(2)}) collective-permute-start(bf16[256,256]{1,0:T(8,128)(2,1)S(1)} %pick2_kernel.1._s.a), channel_id=1, source_target_pairs={{0,4},{4,0},{8,12},{12,8},{16,20},{20,16},{24,28},{28,24},{32,36},... | collective-permute-start | bytes 393224 | tf_op jit(solution)/shard_map/ppermute | solution.py:518
  9.4 2.0 %order_kernel.1 = (bf16[512,256]{1,0:T(8,128)(2,1)S(1)}, bf16[256,512]{1,0:T(8,128)(2,1)S(1)}, bf16[512,256]{1,0:T(8,128)(2,1)S(1)}, bf16[256,512]{1,0:T(8,128)(...) custom-call(s32[4]{0:T(128)S(1)} %pad_add_fusion.pos, ...), custom_call_target="tpu_custom_call" | custom-call | flops 1500000000 | bytes 3000000 | tf_op jit(solution)/shard_map/order_kernel/pallas_call | solution.py:497
  11.4 1.6 %collective-permute-start.4 = (bf16[16,256]{1,0:T(8,128)(2,1)S(1)}, bf16[16,256]{1,0:T(8,128)(2,1)S(1)}, u32[]{:S(2)}, u32[]{:S(2)}) collective-permute-start(bf16[16,256]{1,0:T(8,128)(2,1)S(1)} %get-tuple-element.89.a), channel_id=1, source_target_pairs={{0,64},{4,68},{8,72},{12,76},{16,80},{20,84},{24,88},{28,92},{32,9... | collective-permute-start | bytes 24584 | tf_op jit(solution)/shard_map/ppermute | solution.py:510
  13.0 3.7 %collective-permute-start.3 = (bf16[128,256]{1,0:T(8,128)(2,1)S(1)}, bf16[128,256]{1,0:T(8,128)(2,1)S(1)}, u32[]{:S(2)}, u32[]{:S(2)}) collective-permute-start(bf16[128,256]{1,0:T(8,128)(2,1)S(1)} %pair_kernel.3._s), channel_id=1, source_target_pairs={{0,48},{4,52},{8,56},{12,60},{16,32},{20,36},{24,40},{28,44},{32,1... | collective-permute-start | bytes 196616 | tf_op jit(solution)/shard_map/ppermute | solution.py:514
  16.7 2.1 %collective-permute-start.5 = (bf16[32,256]{1,0:T(8,128)(2,1)S(1)}, bf16[32,256]{1,0:T(8,128)(2,1)S(1)}, u32[]{:S(2)}, u32[]{:S(2)}) collective-permute-start(bf16[32,256]{1,0:T(8,128)(2,1)S(1)} %pair_kernel.5.qa), channel_id=1, source_target_pairs={{0,192},{4,196},{8,200},{12,204},{16,208},{20,212},{24,216},{28,22... | collective-permute-start | bytes 49160 | tf_op jit(solution)/shard_map/ppermute | solution.py:510
  18.8 2.3 %collective-permute-start.2 = (bf16[512,256]{1,0:T(8,128)(2,1)S(1)}, bf16[512,256]{1,0:T(8,128)(2,1)S(1)}, u32[]{:S(2)}, u32[]{:S(2)}) collective-permute-start(bf16[512,256]{1,0:T(8,128)(2,1)S(1)} %pair_kernel.4._s.a), channel_id=1, source_target_pairs={{0,12},{4,8},{8,4},{12,0},{16,28},{20,24},{24,20},{28,16},{32,44},... | collective-permute-start | bytes 786440 | tf_op jit(solution)/shard_map/ppermute | solution.py:518
  21.1 1.7 %first_kernel.2 = (f32[8,512]{1,0:T(8,128)S(1)}, f32[8,512]{1,0:T(8,128)S(1)}, f32[128,512]{1,0:T(8,128)S(1)}) custom-call(bf16[256,512]{1,0:T(8,128)(2,1)S(1)} %get-tuple-element.85.q_t, bf16[512,256]{1,0:T(8,128)(2,1)S(1)} %get-tuple-element.86.k, bf16[256,512]{1,0:T(8,128)(2,1)S(1)} %get-tuple-element.87.v_t, bf16[512,256]{1,0:T(8,128)(2,1)S(1)} %pair_kernel.4._s.a), custom_call_target="tpu_custom_call" | custom-call | flops 1000000000 | bytes 2000000 | tf_op jit(solution)/shard_map/first_kernel/pallas_call | solution.py:497
  24.6 1.8 %collective-permute-start.7 = (bf16[192,256]{1,0:T(8,128)(2,1)S(1)}, bf16[192,256]{1,0:T(8,128)(2,1)S(1)}, u32[]{:S(2)}, u32[]{:S(2)}) collective-permute-start(bf16[192,256]{1,0:T(8,128)(2,1)S(1)} %get-tuple-element.90._s.c0.a0), channel_id=1, source_target_pairs={{0,8},{4,12},{8,0},{12,4},{16,24},{20,28},{24,16},{28,20},{32,40},... | collective-permute-start | bytes 294920 | tf_op jit(solution)/shard_map/ppermute | solution.py:518
  26.5 2.2 %collective-permute-start.8 = (bf16[192,256]{1,0:T(8,128)(2,1)S(1)}, bf16[192,256]{1,0:T(8,128)(2,1)S(1)}, u32[]{:S(2)}, u32[]{:S(2)}) collective-permute-start(bf16[192,256]{1,0:T(8,128)(2,1)S(1)} %get-tuple-element.90._s.c0.a0), channel_id=1, source_target_pairs={{0,12},{4,8},{8,4},{12,0},{16,28},{20,24},{24,20},{28,16},{32,44},... | collective-permute-start | bytes 294920 | tf_op jit(solution)/shard_map/ppermute | solution.py:518
  28.6 1.7 %first_kernel.3 = (f32[8,512]{1,0:T(8,128)S(1)}, f32[8,512]{1,0:T(8,128)S(1)}, f32[128,512]{1,0:T(8,128)S(1)}) custom-call(bf16[256,512]{1,0:T(8,128)(2,1)S(1)} %get-tuple-element.85.q_t, bf16[512,256]{1,0:T(8,128)(2,1)S(1)} %get-tuple-element.86.k, bf16[256,512]{1,0:T(8,128)(2,1)S(1)} %get-tuple-element.87.v_t, bf16[192,256]{1,0:T(8,128)(2,1)S(1)} %get-tuple-element.90._s.c0.a0), custom_call_target="tpu_custom_call" | custom-call | flops 1000000000 | bytes 2000000 | tf_op jit(solution)/shard_map/first_kernel/pallas_call | solution.py:497
  32.7 1.7 %collective-permute-start.10 = (f32[72,128]{1,0:T(8,128)S(1)}, f32[72,128]{1,0:T(8,128)S(1)}, u32[]{:S(2)}, u32[]{:S(2)}) collective-permute-start(f32[72,128]{1,0:T(8,128)S(1)} %get-tuple-element.94._p3.r0), channel_id=1, source_target_pairs={{0,128},{4,132},{8,136},{12,140},{16,144},{20,148},{24,152},{28,15... | collective-permute-start | bytes 110600 | tf_op jit(solution)/shard_map/ppermute | solution.py:510
  34.4 1.8 %collective-permute-start.11 = (f32[72,128]{1,0:T(8,128)S(1)}, f32[72,128]{1,0:T(8,128)S(1)}, u32[]{:S(2)}, u32[]{:S(2)}) collective-permute-start(f32[72,128]{1,0:T(8,128)S(1)} %get-tuple-element.94._p3.r0), channel_id=1, source_target_pairs={{0,192},{4,196},{8,200},{12,204},{16,208},{20,212},{24,216},{28,22... | collective-permute-start | bytes 110600 | tf_op jit(solution)/shard_map/ppermute | solution.py:510
  36.5 2.9 %third_kernel.1 = (f32[8,128]{1,0:T(8,128)S(1)}, f32[8,128]{1,0:T(8,128)S(1)}, f32[256,128]{1,0:T(8,128)S(1)}, bf16[512,256]{1,0:T(8,128)(2,1)S(1)}, bf16[256,51...) custom-call(s32[4]{0:T(128)S(1)} %pad_add_fusion.pos, ...), custom_call_target="tpu_custom_call" | custom-call | flops 4000000000 | bytes 8000000 | tf_op jit(solution)/shard_map/third_kernel/pallas_call | solution.py:497
  40.2 1.4 %fourth_kernel.1 = (f32[8,512]{1,0:T(8,128)S(1)}, f32[8,512]{1,0:T(8,128)S(1)}, bf16[256,512]{1,0:T(8,128)(2,1)S(1)}, f32[272,256]{1,0:T(8,128)S(1)}, bf16[272,2...) custom-call(s32[4]{0:T(128)S(1)} %pad_add_fusion.pos, ...), custom_call_target="tpu_custom_call" | custom-call | flops 3000000000 | bytes 6000000 | tf_op jit(solution)/shard_map/fourth_kernel/pallas_call | solution.py:497
  42.6 2.3 %collective-permute-start.18 = (bf16[512,256]{1,0:T(8,128)(2,1)S(1)}, bf16[512,256]{1,0:T(8,128)(2,1)S(1)}, u32[]{:S(2)}, u32[]{:S(2)}) collective-permute-start(bf16[512,256]{1,0:T(8,128)(2,1)S(1)} %get-tuple-element.125._s), channel_id=1, source_target_pairs={{0,12},{4,8},{8,4},{12,0},{16,28},{20,24},{24,20},{28,16},{32,44},... | collective-permute-start | bytes 786440 | tf_op jit(solution)/shard_map/ppermute | solution.py:518
  44.9 1.2 %collective-permute-start.17 = (bf16[272,256]{1,0:T(8,128)(2,1)S(1)}, bf16[272,256]{1,0:T(8,128)(2,1)S(1)}, u32[]{:S(2)}, u32[]{:S(2)}) collective-permute-start(bf16[272,256]{1,0:T(8,128)(2,1)S(1)} %get-tuple-element.113), channel_id=1, source_target_pairs={{0,192},{4,196},{8,200},{12,204},{16,208},{20,212},{24,216},{28,22... | collective-permute-start | bytes 417800 | tf_op jit(solution)/shard_map/ppermute | solution.py:510
  46.1 3.5 %collective-permute-start.16 = (bf16[272,256]{1,0:T(8,128)(2,1)S(1)}, bf16[272,256]{1,0:T(8,128)(2,1)S(1)}, u32[]{:S(2)}, u32[]{:S(2)}) collective-permute-start(bf16[272,256]{1,0:T(8,128)(2,1)S(1)} %get-tuple-element.112), channel_id=1, source_target_pairs={{0,128},{4,132},{8,136},{12,140},{16,144},{20,148},{24,152},{28,15... | collective-permute-start | bytes 417800 | tf_op jit(solution)/shard_map/ppermute | solution.py:510
  49.6 1.8 %third_back_kernel.1 = (f32[512,256]{1,0:T(8,128)S(1)}, f32[512,256]{1,0:T(8,128)S(1)}, f32[256,128]{1,0:T(8,128)S(1)}, f32[512,128]{1,0:T(8,128)S(1)}, f32[512,128]{1,0:T(8,128)S(1)}, /*index=5*/f32[128,512]{1,0:T(8,128)S(1)}) custom-call(bf16[512,256]{1,0:T(8,128)(2,1)S(1)} %pair_kernel.4._s.a, bf16[512,256]{1,0:T(8,128)(2,1)S(1)} %collective-permute-done.2.b, ...), custom_call_target="tpu_custom_call" | custom-call | flops 3000000000 | bytes 6000000 | tf_op jit(solution)/shard_map/third_back_kernel/pallas_call | solution.py:497
  52.5 1.6 %collective-permute-done.16.b2 = bf16[272,256]{1,0:T(8,128)(2,1)S(1)} collective-permute-done((bf16[272,256]{1,0:T(8,128)(2,1)S(1)}, bf16[272,256]{1,0:T(8,128)(2,1)S(1)}, u32[]{:S(2)}, u32[]{:S(2)}) %collective-permute-start.16) | collective-permute-done | bytes 139296 | tf_op jit(solution)/shard_map/ppermute | solution.py:510
  55.5 2.5 %collective-permute-start.25 = (bf16[320,256]{1,0:T(8,128)(2,1)S(1)}, bf16[320,256]{1,0:T(8,128)(2,1)S(1)}, u32[]{:S(2)}, u32[]{:S(2)}) collective-permute-start(bf16[320,256]{1,0:T(8,128)(2,1)S(1)} %get-tuple-element.148), channel_id=1, source_target_pairs={{0,8},{4,12},{8,0},{12,4},{16,24},{20,28},{24,16},{28,20},{32,40},... | collective-permute-start | bytes 491528 | tf_op jit(solution)/shard_map/ppermute | solution.py:518
  58.0 2.2 %collective-permute-start.26 = (bf16[320,256]{1,0:T(8,128)(2,1)S(1)}, bf16[320,256]{1,0:T(8,128)(2,1)S(1)}, u32[]{:S(2)}, u32[]{:S(2)}) collective-permute-start(bf16[320,256]{1,0:T(8,128)(2,1)S(1)} %get-tuple-element.149), channel_id=1, source_target_pairs={{0,12},{4,8},{8,4},{12,0},{16,28},{20,24},{24,20},{28,16},{32,44},... | collective-permute-start | bytes 491528 | tf_op jit(solution)/shard_map/ppermute | solution.py:518
  60.2 1.2 %collective-permute-start.19 = (f32[64,128]{1,0:T(8,128)S(1)}, f32[64,128]{1,0:T(8,128)S(1)}, u32[]{:S(2)}, u32[]{:S(2)}) collective-permute-start(f32[64,128]{1,0:T(8,128)S(1)} %get-tuple-element.128.own), channel_id=1, source_target_pairs={{0,192},{4,196},{8,200},{12,204},{16,208},{20,212},{24,216},{28,22... | collective-permute-start | bytes 98312 | tf_op jit(solution)/shard_map/ppermute | solution.py:510
  62.7 1.1 %collective-permute-start.24 = (bf16[512,256]{1,0:T(8,128)(2,1)S(1)}, bf16[512,256]{1,0:T(8,128)(2,1)S(1)}, u32[]{:S(2)}, u32[]{:S(2)}) collective-permute-start(bf16[512,256]{1,0:T(8,128)(2,1)S(1)} %get-tuple-element.147), channel_id=1, source_target_pairs={{0,2},{1,3},{2,0},{3,1},{4,6},{5,7},{6,4},{7,5},{8,10},{9,11},{10,... | collective-permute-start | bytes 786440 | tf_op jit(solution)/shard_map/ppermute | solution.py:522
  63.8 1.4 %pair_back_kernel.1 = (f32[512,128]{1,0:T(8,128)S(1)}, f32[512,128]{1,0:T(8,128)S(1)}, f32[128,512]{1,0:T(8,128)S(1)}) custom-call(bf16[512,256]{1,0:T(8,128)(2,1)S(1)} %get-tuple-element.84._s.q, bf16[256,512]{1,0:T(8,128)(2,1)S(1)} %get-tuple-element.85.q_t, bf16[512,256]{1,0:T(8,128)(2,1)S(1)} %get-tuple-element.86.k, ...), custom_call_target="tpu_custom_call" | custom-call | flops 3000000000 | bytes 6000000 | tf_op jit(solution)/shard_map/pair_back_kernel/pallas_call | solution.py:497
  66.6 2.2 %collective-permute-done.26.b3 = bf16[320,256]{1,0:T(8,128)(2,1)S(1)} collective-permute-done((bf16[320,256]{1,0:T(8,128)(2,1)S(1)}, bf16[320,256]{1,0:T(8,128)(2,1)S(1)}, u32[]{:S(2)}, u32[]{:S(2)}) %collective-permute-start.26) | collective-permute-done | bytes 163872 | tf_op jit(solution)/shard_map/ppermute | solution.py:518
  69.4 1.6 %collective-permute-start.27 = (bf16[80,256]{1,0:T(8,128)(2,1)S(1)}, bf16[80,256]{1,0:T(8,128)(2,1)S(1)}, u32[]{:S(2)}, u32[]{:S(2)}) collective-permute-start(bf16[80,256]{1,0:T(8,128)(2,1)S(1)} %get-tuple-element.150._s), channel_id=1, source_target_pairs={{0,16},{4,20},{8,24},{12,28},{16,0},{20,4},{24,8},{28,12},{32,48},... | collective-permute-start | bytes 122888 | tf_op jit(solution)/shard_map/ppermute | solution.py:514
  70.9 3.6 %collective-permute-start.28 = (bf16[80,256]{1,0:T(8,128)(2,1)S(1)}, bf16[80,256]{1,0:T(8,128)(2,1)S(1)}, u32[]{:S(2)}, u32[]{:S(2)}) collective-permute-start(bf16[80,256]{1,0:T(8,128)(2,1)S(1)} %get-tuple-element.154), channel_id=1, source_target_pairs={{0,32},{4,36},{8,40},{12,44},{16,48},{20,52},{24,56},{28,60},{32,0... | collective-permute-start | bytes 122888 | tf_op jit(solution)/shard_map/ppermute | solution.py:514
  74.6 1.4 %collective-permute-start.29 = (bf16[80,256]{1,0:T(8,128)(2,1)S(1)}, bf16[80,256]{1,0:T(8,128)(2,1)S(1)}, u32[]{:S(2)}, u32[]{:S(2)}) collective-permute-start(bf16[80,256]{1,0:T(8,128)(2,1)S(1)} %get-tuple-element.155), channel_id=1, source_target_pairs={{0,48},{4,52},{8,56},{12,60},{16,32},{20,36},{24,40},{28,44},{32,1... | collective-permute-start | bytes 122888 | tf_op jit(solution)/shard_map/ppermute | solution.py:514
  76.0 2.8 %natural_kernel.1 = (bf16[512,256]{1,0:T(8,128)(2,1)}, bf16[512,256]{1,0:T(8,128)(2,1)S(1)}, bf16[512,256]{1,0:T(8,128)(2,1)S(1)}, f32[32,256]{1,0:T(8,128)S(1)}...) custom-call(s32[4]{0:T(128)S(1)} %pad_add_fusion.pos, f32[64,128]{1,0:T(8,128)S(1)} %get-tuple-element.129.e0, ...), custom_call_target="tpu_custom_call" | custom-call | flops 3000000000 | bytes 6000000 | tf_op jit(solution)/shard_map/natural_kernel/pallas_call | solution.py:497
  79.2 1.9 %collective-permute-done.29.b3 = bf16[80,256]{1,0:T(8,128)(2,1)S(1)} collective-permute-done((bf16[80,256]{1,0:T(8,128)(2,1)S(1)}, bf16[80,256]{1,0:T(8,128)(2,1)S(1)}, u32[]{:S(2)}, u32[]{:S(2)}) %collective-permute-start.29) | collective-permute-done | bytes 40992 | tf_op jit(solution)/shard_map/ppermute | solution.py:514
  81.1 1.8 %last_kernel.1 = (bf16[512,256]{1,0:T(8,128)(2,1)}, bf16[512,256]{1,0:T(8,128)(2,1)}, f32[16,256]{1,0:T(8,128)}) custom-call(s32[4]{0:T(128)S(1)} %pad_add_fusion.pos, f32[80,256]{1,0:T(8,128)S(1)} %get-tuple-element.153.own, bf16[80,256]{1,0:T(8,128)(2,1)S(1)} %collective-permute-done.27.b1, bf16[80,256]{1,0:T(8,128)(2,1)S(1)} %collective-permute-done.28.b2, ...), custom_call_target="tpu_custom_call" | custom-call | flops 1000000000 | bytes 2000000 | tf_op jit(solution)/shard_map/last_kernel/pallas_call | solution.py:497
  (64 shorter events, 16.0 us)
Async XLA Ops:
  3.5 5.9 %copy-start.3 = (bf16[512,256]{1,0:T(8,128)(2,1)S(1)}, bf16[512,256]{1,0:T(8,128)(2,1)}, u32[]{:S(2)}) copy-start(bf16[512,256]{1,0:T(8,128)(2,1)} %q.1) | copy-start | bytes 786436
  3.5 9.5 %collective-permute-start.1 = (bf16[64,256]{1,0:T(8,128)(2,1)S(1)}, bf16[64,256]{1,0:T(8,128)(2,1)S(1)}, u32[]{:S(2)}, u32[]{:S(2)}) collective-permute-start(bf16[64,256]{1,0:T(8,128)(2,1)S(1)} %pick3_kernel.1._p3.a), channel_id=1, source_target_pairs={{0,16},{4,20},{8,24},{12,28},{16,0},{20,4},{24,8},{28,12},{32,48},... | collective-permute-start | bytes 98312 | tf_op jit(solution)/shard_map/ppermute | solution.py:514
  7.7 11.0 %collective-permute-start = (bf16[256,256]{1,0:T(8,128)(2,1)S(1)}, bf16[256,256]{1,0:T(8,128)(2,1)S(1)}, u32[]{:S(2)}, u32[]{:S(2)}) collective-permute-start(bf16[256,256]{1,0:T(8,128)(2,1)S(1)} %pick2_kernel.1._s.a), channel_id=1, source_target_pairs={{0,4},{4,0},{8,12},{12,8},{16,20},{20,16},{24,28},{28,24},{32,36},... | collective-permute-start | bytes 393224 | tf_op jit(solution)/shard_map/ppermute | solution.py:518
  11.4 5.3 %collective-permute-start.4 = (bf16[16,256]{1,0:T(8,128)(2,1)S(1)}, bf16[16,256]{1,0:T(8,128)(2,1)S(1)}, u32[]{:S(2)}, u32[]{:S(2)}) collective-permute-start(bf16[16,256]{1,0:T(8,128)(2,1)S(1)} %get-tuple-element.89.a), channel_id=1, source_target_pairs={{0,64},{4,68},{8,72},{12,76},{16,80},{20,84},{24,88},{28,92},{32,9... | collective-permute-start | bytes 24584 | tf_op jit(solution)/shard_map/ppermute | solution.py:510
  13.0 9.8 %collective-permute-start.3 = (bf16[128,256]{1,0:T(8,128)(2,1)S(1)}, bf16[128,256]{1,0:T(8,128)(2,1)S(1)}, u32[]{:S(2)}, u32[]{:S(2)}) collective-permute-start(bf16[128,256]{1,0:T(8,128)(2,1)S(1)} %pair_kernel.3._s), channel_id=1, source_target_pairs={{0,48},{4,52},{8,56},{12,60},{16,32},{20,36},{24,40},{28,44},{32,1... | collective-permute-start | bytes 196616 | tf_op jit(solution)/shard_map/ppermute | solution.py:514
  16.7 6.1 %collective-permute-start.5 = (bf16[32,256]{1,0:T(8,128)(2,1)S(1)}, bf16[32,256]{1,0:T(8,128)(2,1)S(1)}, u32[]{:S(2)}, u32[]{:S(2)}) collective-permute-start(bf16[32,256]{1,0:T(8,128)(2,1)S(1)} %pair_kernel.5.qa), channel_id=1, source_target_pairs={{0,192},{4,196},{8,200},{12,204},{16,208},{20,212},{24,216},{28,22... | collective-permute-start | bytes 49160 | tf_op jit(solution)/shard_map/ppermute | solution.py:510
  18.8 11.6 %collective-permute-start.2 = (bf16[512,256]{1,0:T(8,128)(2,1)S(1)}, bf16[512,256]{1,0:T(8,128)(2,1)S(1)}, u32[]{:S(2)}, u32[]{:S(2)}) collective-permute-start(bf16[512,256]{1,0:T(8,128)(2,1)S(1)} %pair_kernel.4._s.a), channel_id=1, source_target_pairs={{0,12},{4,8},{8,4},{12,0},{16,28},{20,24},{24,20},{28,16},{32,44},... | collective-permute-start | bytes 786440 | tf_op jit(solution)/shard_map/ppermute | solution.py:518
  22.8 7.6 %collective-permute-start.13 = (bf16[512,256]{1,0:T(8,128)(2,1)S(1)}, bf16[512,256]{1,0:T(8,128)(2,1)S(1)}, u32[]{:S(2)}, u32[]{:S(2)}) collective-permute-start(bf16[512,256]{1,0:T(8,128)(2,1)S(1)} %get-tuple-element.101.c0), channel_id=1, source_target_pairs={{0,2},{1,3},{2,0},{3,1},{4,6},{5,7},{6,4},{7,5},{8,10},{9,11},{10,... | collective-permute-start | bytes 786440 | tf_op jit(solution)/shard_map/ppermute | solution.py:522
  23.9 7.9 %collective-permute-start.6 = (bf16[192,256]{1,0:T(8,128)(2,1)S(1)}, bf16[192,256]{1,0:T(8,128)(2,1)S(1)}, u32[]{:S(2)}, u32[]{:S(2)}) collective-permute-start(bf16[192,256]{1,0:T(8,128)(2,1)S(1)} %get-tuple-element.90._s.c0.a0), channel_id=1, source_target_pairs={{0,4},{4,0},{8,12},{12,8},{16,20},{20,16},{24,28},{28,24},{32,36},... | collective-permute-start | bytes 294920 | tf_op jit(solution)/shard_map/ppermute | solution.py:518
  24.6 7.3 %collective-permute-start.7 = (bf16[192,256]{1,0:T(8,128)(2,1)S(1)}, bf16[192,256]{1,0:T(8,128)(2,1)S(1)}, u32[]{:S(2)}, u32[]{:S(2)}) collective-permute-start(bf16[192,256]{1,0:T(8,128)(2,1)S(1)} %get-tuple-element.90._s.c0.a0), channel_id=1, source_target_pairs={{0,8},{4,12},{8,0},{12,4},{16,24},{20,28},{24,16},{28,20},{32,40},... | collective-permute-start | bytes 294920 | tf_op jit(solution)/shard_map/ppermute | solution.py:518
  26.5 5.8 %collective-permute-start.8 = (bf16[192,256]{1,0:T(8,128)(2,1)S(1)}, bf16[192,256]{1,0:T(8,128)(2,1)S(1)}, u32[]{:S(2)}, u32[]{:S(2)}) collective-permute-start(bf16[192,256]{1,0:T(8,128)(2,1)S(1)} %get-tuple-element.90._s.c0.a0), channel_id=1, source_target_pairs={{0,12},{4,8},{8,4},{12,0},{16,28},{20,24},{24,20},{28,16},{32,44},... | collective-permute-start | bytes 294920 | tf_op jit(solution)/shard_map/ppermute | solution.py:518
  30.4 6.1 %collective-permute-start.12 = (bf16[512,256]{1,0:T(8,128)(2,1)S(1)}, bf16[512,256]{1,0:T(8,128)(2,1)S(1)}, u32[]{:S(2)}, u32[]{:S(2)}) collective-permute-start(bf16[512,256]{1,0:T(8,128)(2,1)S(1)} %get-tuple-element.101.c0), channel_id=1, source_target_pairs={{0,1},{1,0},{2,3},{3,2},{4,5},{5,4},{6,7},{7,6},{8,9},{9,8},{10,11... | collective-permute-start | bytes 786440 | tf_op jit(solution)/shard_map/ppermute | solution.py:522
  30.5 6.0 %collective-permute-start.14 = (bf16[512,256]{1,0:T(8,128)(2,1)S(1)}, bf16[512,256]{1,0:T(8,128)(2,1)S(1)}, u32[]{:S(2)}, u32[]{:S(2)}) collective-permute-start(bf16[512,256]{1,0:T(8,128)(2,1)S(1)} %collective-permute-done.13.c2), channel_id=1, source_target_pairs={{0,1},{1,0},{2,3},{3,2},{4,5},{5,4},{6,7},{7,6},{8,9},{9,8},{10,11... | collective-permute-start | bytes 786440 | tf_op jit(solution)/shard_map/ppermute | solution.py:522
  32.3 4.2 %copy-start = (bf16[256,1024]{1,0:T(8,128)(2,1)S(1)}, bf16[256,1024]{1,0:T(8,128)(2,1)}, u32[]{:S(2)}) copy-start(bf16[256,1024]{1,0:T(8,128)(2,1)} %w.3) | copy-start | bytes 1572868
  32.7 6.7 %collective-permute-start.10 = (f32[72,128]{1,0:T(8,128)S(1)}, f32[72,128]{1,0:T(8,128)S(1)}, u32[]{:S(2)}, u32[]{:S(2)}) collective-permute-start(f32[72,128]{1,0:T(8,128)S(1)} %get-tuple-element.94._p3.r0), channel_id=1, source_target_pairs={{0,128},{4,132},{8,136},{12,140},{16,144},{20,148},{24,152},{28,15... | collective-permute-start | bytes 110600 | tf_op jit(solution)/shard_map/ppermute | solution.py:510
  34.4 5.2 %collective-permute-start.11 = (f32[72,128]{1,0:T(8,128)S(1)}, f32[72,128]{1,0:T(8,128)S(1)}, u32[]{:S(2)}, u32[]{:S(2)}) collective-permute-start(f32[72,128]{1,0:T(8,128)S(1)} %get-tuple-element.94._p3.r0), channel_id=1, source_target_pairs={{0,192},{4,196},{8,200},{12,204},{16,208},{20,212},{24,216},{28,22... | collective-permute-start | bytes 110600 | tf_op jit(solution)/shard_map/ppermute | solution.py:510
  36.3 4.0 %collective-permute-start.9 = (f32[72,128]{1,0:T(8,128)S(1)}, f32[72,128]{1,0:T(8,128)S(1)}, u32[]{:S(2)}, u32[]{:S(2)}) collective-permute-start(f32[72,128]{1,0:T(8,128)S(1)} %get-tuple-element.94._p3.r0), channel_id=1, source_target_pairs={{0,64},{4,68},{8,72},{12,76},{16,80},{20,84},{24,88},{28,92},{32,9... | collective-permute-start | bytes 110600 | tf_op jit(solution)/shard_map/ppermute | solution.py:510
  42.6 11.9 %collective-permute-start.18 = (bf16[512,256]{1,0:T(8,128)(2,1)S(1)}, bf16[512,256]{1,0:T(8,128)(2,1)S(1)}, u32[]{:S(2)}, u32[]{:S(2)}) collective-permute-start(bf16[512,256]{1,0:T(8,128)(2,1)S(1)} %get-tuple-element.125._s), channel_id=1, source_target_pairs={{0,12},{4,8},{8,4},{12,0},{16,28},{20,24},{24,20},{28,16},{32,44},... | collective-permute-start | bytes 786440 | tf_op jit(solution)/shard_map/ppermute | solution.py:518
  44.9 7.6 %collective-permute-start.17 = (bf16[272,256]{1,0:T(8,128)(2,1)S(1)}, bf16[272,256]{1,0:T(8,128)(2,1)S(1)}, u32[]{:S(2)}, u32[]{:S(2)}) collective-permute-start(bf16[272,256]{1,0:T(8,128)(2,1)S(1)} %get-tuple-element.113), channel_id=1, source_target_pairs={{0,192},{4,196},{8,200},{12,204},{16,208},{20,212},{24,216},{28,22... | collective-permute-start | bytes 417800 | tf_op jit(solution)/shard_map/ppermute | solution.py:510
  46.1 6.4 %collective-permute-start.15 = (bf16[272,256]{1,0:T(8,128)(2,1)S(1)}, bf16[272,256]{1,0:T(8,128)(2,1)S(1)}, u32[]{:S(2)}, u32[]{:S(2)}) collective-permute-start(bf16[272,256]{1,0:T(8,128)(2,1)S(1)} %get-tuple-element.111), channel_id=1, source_target_pairs={{0,64},{4,68},{8,72},{12,76},{16,80},{20,84},{24,88},{28,92},{32,9... | collective-permute-start | bytes 417800 | tf_op jit(solution)/shard_map/ppermute | solution.py:510
  46.1 8.0 %collective-permute-start.16 = (bf16[272,256]{1,0:T(8,128)(2,1)S(1)}, bf16[272,256]{1,0:T(8,128)(2,1)S(1)}, u32[]{:S(2)}, u32[]{:S(2)}) collective-permute-start(bf16[272,256]{1,0:T(8,128)(2,1)S(1)} %get-tuple-element.112), channel_id=1, source_target_pairs={{0,128},{4,132},{8,136},{12,140},{16,144},{20,148},{24,152},{28,15... | collective-permute-start | bytes 417800 | tf_op jit(solution)/shard_map/ppermute | solution.py:510
  55.3 7.3 %collective-permute-start.23 = (bf16[1024,256]{1,0:T(8,128)(2,1)S(1)}, bf16[1024,256]{1,0:T(8,128)(2,1)S(1)}, u32[]{:S(2)}, u32[]{:S(2)}) collective-permute-start(bf16[1024,256]{1,0:T(8,128)(2,1)S(1)} %get-tuple-element.145), channel_id=1, source_target_pairs={{0,1},{1,0},{2,3},{3,2},{4,5},{5,4},{6,7},{7,6},{8,9},{9,8},{10,11... | collective-permute-start | bytes 1572872 | tf_op jit(solution)/shard_map/ppermute | solution.py:522
  55.4 7.1 %collective-permute-start.21 = (bf16[320,256]{1,0:T(8,128)(2,1)S(1)}, bf16[320,256]{1,0:T(8,128)(2,1)S(1)}, u32[]{:S(2)}, u32[]{:S(2)}) collective-permute-start(bf16[320,256]{1,0:T(8,128)(2,1)S(1)} %get-tuple-element.135._s), channel_id=1, source_target_pairs={{0,4},{4,0},{8,12},{12,8},{16,20},{20,16},{24,28},{28,24},{32,36},... | collective-permute-start | bytes 491528 | tf_op jit(solution)/shard_map/ppermute | solution.py:518
  55.5 11.0 %collective-permute-start.25 = (bf16[320,256]{1,0:T(8,128)(2,1)S(1)}, bf16[320,256]{1,0:T(8,128)(2,1)S(1)}, u32[]{:S(2)}, u32[]{:S(2)}) collective-permute-start(bf16[320,256]{1,0:T(8,128)(2,1)S(1)} %get-tuple-element.148), channel_id=1, source_target_pairs={{0,8},{4,12},{8,0},{12,4},{16,24},{20,28},{24,16},{28,20},{32,40},... | collective-permute-start | bytes 491528 | tf_op jit(solution)/shard_map/ppermute | solution.py:518
  58.0 10.7 %collective-permute-start.26 = (bf16[320,256]{1,0:T(8,128)(2,1)S(1)}, bf16[320,256]{1,0:T(8,128)(2,1)S(1)}, u32[]{:S(2)}, u32[]{:S(2)}) collective-permute-start(bf16[320,256]{1,0:T(8,128)(2,1)S(1)} %get-tuple-element.149), channel_id=1, source_target_pairs={{0,12},{4,8},{8,4},{12,0},{16,28},{20,24},{24,20},{28,16},{32,44},... | collective-permute-start | bytes 491528 | tf_op jit(solution)/shard_map/ppermute | solution.py:518
  60.2 5.1 %collective-permute-start.19 = (f32[64,128]{1,0:T(8,128)S(1)}, f32[64,128]{1,0:T(8,128)S(1)}, u32[]{:S(2)}, u32[]{:S(2)}) collective-permute-start(f32[64,128]{1,0:T(8,128)S(1)} %get-tuple-element.128.own), channel_id=1, source_target_pairs={{0,192},{4,196},{8,200},{12,204},{16,208},{20,212},{24,216},{28,22... | collective-permute-start | bytes 98312 | tf_op jit(solution)/shard_map/ppermute | solution.py:510
  62.5 13.5 %collective-permute-start.22 = (bf16[256,256]{1,0:T(8,128)(2,1)S(1)}, bf16[256,256]{1,0:T(8,128)(2,1)S(1)}, u32[]{:S(2)}, u32[]{:S(2)}) collective-permute-start(bf16[256,256]{1,0:T(8,128)(2,1)S(1)} %get-tuple-element.140._s), channel_id=1, source_target_pairs={{0,4},{4,0},{8,12},{12,8},{16,20},{20,16},{24,28},{28,24},{32,36},... | collective-permute-start | bytes 393224 | tf_op jit(solution)/shard_map/ppermute | solution.py:518
  62.7 13.3 %collective-permute-start.24 = (bf16[512,256]{1,0:T(8,128)(2,1)S(1)}, bf16[512,256]{1,0:T(8,128)(2,1)S(1)}, u32[]{:S(2)}, u32[]{:S(2)}) collective-permute-start(bf16[512,256]{1,0:T(8,128)(2,1)S(1)} %get-tuple-element.147), channel_id=1, source_target_pairs={{0,2},{1,3},{2,0},{3,1},{4,6},{5,7},{6,4},{7,5},{8,10},{9,11},{10,... | collective-permute-start | bytes 786440 | tf_op jit(solution)/shard_map/ppermute | solution.py:522
  65.4 9.1 %collective-permute-start.20 = (f32[64,128]{1,0:T(8,128)S(1)}, f32[64,128]{1,0:T(8,128)S(1)}, u32[]{:S(2)}, u32[]{:S(2)}) collective-permute-start(f32[64,128]{1,0:T(8,128)S(1)} %get-tuple-element.130), channel_id=1, source_target_pairs={{0,64},{4,68},{8,72},{12,76},{16,80},{20,84},{24,88},{28,92},{32,9... | collective-permute-start | bytes 98312 | tf_op jit(solution)/shard_map/ppermute | solution.py:510
  69.4 9.4 %collective-permute-start.27 = (bf16[80,256]{1,0:T(8,128)(2,1)S(1)}, bf16[80,256]{1,0:T(8,128)(2,1)S(1)}, u32[]{:S(2)}, u32[]{:S(2)}) collective-permute-start(bf16[80,256]{1,0:T(8,128)(2,1)S(1)} %get-tuple-element.150._s), channel_id=1, source_target_pairs={{0,16},{4,20},{8,24},{12,28},{16,0},{20,4},{24,8},{28,12},{32,48},... | collective-permute-start | bytes 122888 | tf_op jit(solution)/shard_map/ppermute | solution.py:514
  70.9 8.2 %collective-permute-start.28 = (bf16[80,256]{1,0:T(8,128)(2,1)S(1)}, bf16[80,256]{1,0:T(8,128)(2,1)S(1)}, u32[]{:S(2)}, u32[]{:S(2)}) collective-permute-start(bf16[80,256]{1,0:T(8,128)(2,1)S(1)} %get-tuple-element.154), channel_id=1, source_target_pairs={{0,32},{4,36},{8,40},{12,44},{16,48},{20,52},{24,56},{28,60},{32,0... | collective-permute-start | bytes 122888 | tf_op jit(solution)/shard_map/ppermute | solution.py:514
  74.6 6.6 %collective-permute-start.29 = (bf16[80,256]{1,0:T(8,128)(2,1)S(1)}, bf16[80,256]{1,0:T(8,128)(2,1)S(1)}, u32[]{:S(2)}, u32[]{:S(2)}) collective-permute-start(bf16[80,256]{1,0:T(8,128)(2,1)S(1)} %get-tuple-element.155), channel_id=1, source_target_pairs={{0,48},{4,52},{8,56},{12,60},{16,32},{20,36},{24,40},{28,44},{32,1... | collective-permute-start | bytes 122888 | tf_op jit(solution)/shard_map/ppermute | solution.py:514
  (3 other events, 3.6 us)

commit v5 on v4

--- a/solution.py
+++ b/solution.py
@@ -596,11 +596,11 @@
     got_c = swap(lax.optimization_barrier((send_c, sent[0]))[0], 1)
     mix_own, mix_send = call(mix_kernel, [(wide, F32), (wide, BF)], keep_a, keep_b, got_c, us=1)
     mix_got = swap(mix_send, 2)
-    got2 = swap_y(lax.optimization_barrier((sent2, r3[1]))[0], 1)
     dk_b, dv_b, dq_b = call(
         pair_back_kernel, [((T, 128), F32), ((T, 128), F32), ((128, T), F32)],
         q, q_t, k, k_t, v, g, g_t, lse, delta, sent[1], us=6,
     )
+    got2 = swap_y(lax.optimization_barrier((sent2, r3[1], dk_b))[0], 1)
     sent = call(
         reduce_z_kernel, [((80, F), F32)] + [((80, F), BF)] * 3, pos, *r3, us=1,
         scratch=[pltpu.VMEM((320, F), F32)],

time: 83 us -> 83.8 us (level)
    ppermute x10, waiting for transfers between devices: 2.59 us -> 6.36 us  [swap_x(): return lax.ppermute(block, 'seq', [(s, s ^ 16 * mask) for s in range(64)])]
    ppermute x10, waiting for transfers between devices: 4.26 us -> 0.59 us  [swap_y(): return lax.ppermute(block, 'seq', [(s, s ^ mask) for s in range(64)])]
  transfers between devices with their start and end apart: 30 -> 30, of which waited for: 10 -> 8; matrix products, arithmetic and copies ran while one was open for 0% -> 0% of each run, Pallas kernels for 23% -> 23%
where the time goes in v5:
time: 83.8 us; the launch traced here: 82.9 us
  starting transfers between devices  46 us (55%)
  Pallas kernels  24.6 us (29%)
  waiting for transfers between devices  9.28 us (11%)
  local copies, waits for them, and re-layouts  1.93 us (2%)
  between operations  0.99 us (1%)
    pallas_call x25, Pallas kernels, call(): pl.pallas_call(kernel, out_shape=[jax.ShapeDtypeStruct(shape, dtype) for...  24.6 us
    ppermute x10, starting transfers between devices, swap_y(): return lax.ppermute(block, 'seq', [(s, s ^ mask) for s in range(64)])  15.8 us
    ppermute x5, starting transfers between devices, swap_z(): return lax.ppermute(block, 'seq', [(s, s ^ 4 * mask) for s in range(64)])  13.6 us
    ppermute x10, starting transfers between devices, swap_x(): return lax.ppermute(block, 'seq', [(s, s ^ 16 * mask) for s in range(64)])  13.5 us
    ppermute x10, waiting for transfers between devices, swap_x(): return lax.ppermute(block, 'seq', [(s, s ^ 16 * mask) for s in range(64)])  6.36 us
    ppermute x5, starting transfers between devices, swap(): return lax.ppermute(block, 'head', [(s, s ^ mask) for s in range(4)])  3.1 us
    ppermute x5, waiting for transfers between devices, swap_z(): return lax.ppermute(block, 'seq', [(s, s ^ 4 * mask) for s in range(64)])  2.32 us
    unnamed x10, local copies, waits for them, and re-layouts  1.93 us
  transfers between devices with their start and end apart: 30, of which 8 were waited for; matrix products, arithmetic and copies ran while one was open for 0% of the time, Pallas kernels for 23%

profile of v5, /device:TPU:32, one launch (start us, length us, event | category | flops | bytes accessed | tf_op | source)
XLA Modules:
  0.0 82.9 jit_solution(715118601182262041)
XLA Ops:
  3.5 3.4 %collective-permute-start.1 = (bf16[64,256]{1,0:T(8,128)(2,1)S(1)}, bf16[64,256]{1,0:T(8,128)(2,1)S(1)}, u32[]{:S(2)}, u32[]{:S(2)}) collective-permute-start(bf16[64,256]{1,0:T(8,128)(2,1)S(1)} %pick3_kernel.1._p3.a), channel_id=1, source_target_pairs={{0,16},{4,20},{8,24},{12,28},{16,0},{20,4},{24,8},{28,12},{32,48},... | collective-permute-start | bytes 98312 | tf_op jit(solution)/shard_map/ppermute | solution.py:514
  7.7 1.7 %collective-permute-start = (bf16[256,256]{1,0:T(8,128)(2,1)S(1)}, bf16[256,256]{1,0:T(8,128)(2,1)S(1)}, u32[]{:S(2)}, u32[]{:S(2)}) collective-permute-start(bf16[256,256]{1,0:T(8,128)(2,1)S(1)} %pick2_kernel.1._s.a), channel_id=1, source_target_pairs={{0,4},{4,0},{8,12},{12,8},{16,20},{20,16},{24,28},{28,24},{32,36},... | collective-permute-start | bytes 393224 | tf_op jit(solution)/shard_map/ppermute | solution.py:518
  9.4 2.0 %order_kernel.1 = (bf16[512,256]{1,0:T(8,128)(2,1)S(1)}, bf16[256,512]{1,0:T(8,128)(2,1)S(1)}, bf16[512,256]{1,0:T(8,128)(2,1)S(1)}, bf16[256,512]{1,0:T(8,128)(...) custom-call(s32[4]{0:T(128)S(1)} %pad_add_fusion.pos, ...), custom_call_target="tpu_custom_call" | custom-call | flops 1500000000 | bytes 3000000 | tf_op jit(solution)/shard_map/order_kernel/pallas_call | solution.py:497
  11.4 1.6 %collective-permute-start.4 = (bf16[16,256]{1,0:T(8,128)(2,1)S(1)}, bf16[16,256]{1,0:T(8,128)(2,1)S(1)}, u32[]{:S(2)}, u32[]{:S(2)}) collective-permute-start(bf16[16,256]{1,0:T(8,128)(2,1)S(1)} %get-tuple-element.89.a), channel_id=1, source_target_pairs={{0,64},{4,68},{8,72},{12,76},{16,80},{20,84},{24,88},{28,92},{32,9... | collective-permute-start | bytes 24584 | tf_op jit(solution)/shard_map/ppermute | solution.py:510
  13.0 3.7 %collective-permute-start.3 = (bf16[128,256]{1,0:T(8,128)(2,1)S(1)}, bf16[128,256]{1,0:T(8,128)(2,1)S(1)}, u32[]{:S(2)}, u32[]{:S(2)}) collective-permute-start(bf16[128,256]{1,0:T(8,128)(2,1)S(1)} %pair_kernel.3._s), channel_id=1, source_target_pairs={{0,48},{4,52},{8,56},{12,60},{16,32},{20,36},{24,40},{28,44},{32,1... | collective-permute-start | bytes 196616 | tf_op jit(solution)/shard_map/ppermute | solution.py:514
  16.7 2.1 %collective-permute-start.5 = (bf16[32,256]{1,0:T(8,128)(2,1)S(1)}, bf16[32,256]{1,0:T(8,128)(2,1)S(1)}, u32[]{:S(2)}, u32[]{:S(2)}) collective-permute-start(bf16[32,256]{1,0:T(8,128)(2,1)S(1)} %pair_kernel.5.qa), channel_id=1, source_target_pairs={{0,192},{4,196},{8,200},{12,204},{16,208},{20,212},{24,216},{28,22... | collective-permute-start | bytes 49160 | tf_op jit(solution)/shard_map/ppermute | solution.py:510
  18.8 2.3 %collective-permute-start.2 = (bf16[512,256]{1,0:T(8,128)(2,1)S(1)}, bf16[512,256]{1,0:T(8,128)(2,1)S(1)}, u32[]{:S(2)}, u32[]{:S(2)}) collective-permute-start(bf16[512,256]{1,0:T(8,128)(2,1)S(1)} %pair_kernel.4._s.a), channel_id=1, source_target_pairs={{0,12},{4,8},{8,4},{12,0},{16,28},{20,24},{24,20},{28,16},{32,44},... | collective-permute-start | bytes 786440 | tf_op jit(solution)/shard_map/ppermute | solution.py:518
  21.1 1.7 %first_kernel.2 = (f32[8,512]{1,0:T(8,128)S(1)}, f32[8,512]{1,0:T(8,128)S(1)}, f32[128,512]{1,0:T(8,128)S(1)}) custom-call(bf16[256,512]{1,0:T(8,128)(2,1)S(1)} %get-tuple-element.85.q_t, bf16[512,256]{1,0:T(8,128)(2,1)S(1)} %get-tuple-element.86.k, bf16[256,512]{1,0:T(8,128)(2,1)S(1)} %get-tuple-element.87.v_t, bf16[512,256]{1,0:T(8,128)(2,1)S(1)} %pair_kernel.4._s.a), custom_call_target="tpu_custom_call" | custom-call | flops 1000000000 | bytes 2000000 | tf_op jit(solution)/shard_map/first_kernel/pallas_call | solution.py:497
  24.6 1.8 %collective-permute-start.7 = (bf16[192,256]{1,0:T(8,128)(2,1)S(1)}, bf16[192,256]{1,0:T(8,128)(2,1)S(1)}, u32[]{:S(2)}, u32[]{:S(2)}) collective-permute-start(bf16[192,256]{1,0:T(8,128)(2,1)S(1)} %get-tuple-element.90._s.c0.a0), channel_id=1, source_target_pairs={{0,8},{4,12},{8,0},{12,4},{16,24},{20,28},{24,16},{28,20},{32,40},... | collective-permute-start | bytes 294920 | tf_op jit(solution)/shard_map/ppermute | solution.py:518
  26.5 2.2 %collective-permute-start.8 = (bf16[192,256]{1,0:T(8,128)(2,1)S(1)}, bf16[192,256]{1,0:T(8,128)(2,1)S(1)}, u32[]{:S(2)}, u32[]{:S(2)}) collective-permute-start(bf16[192,256]{1,0:T(8,128)(2,1)S(1)} %get-tuple-element.90._s.c0.a0), channel_id=1, source_target_pairs={{0,12},{4,8},{8,4},{12,0},{16,28},{20,24},{24,20},{28,16},{32,44},... | collective-permute-start | bytes 294920 | tf_op jit(solution)/shard_map/ppermute | solution.py:518
  28.6 1.7 %first_kernel.3 = (f32[8,512]{1,0:T(8,128)S(1)}, f32[8,512]{1,0:T(8,128)S(1)}, f32[128,512]{1,0:T(8,128)S(1)}) custom-call(bf16[256,512]{1,0:T(8,128)(2,1)S(1)} %get-tuple-element.85.q_t, bf16[512,256]{1,0:T(8,128)(2,1)S(1)} %get-tuple-element.86.k, bf16[256,512]{1,0:T(8,128)(2,1)S(1)} %get-tuple-element.87.v_t, bf16[192,256]{1,0:T(8,128)(2,1)S(1)} %get-tuple-element.90._s.c0.a0), custom_call_target="tpu_custom_call" | custom-call | flops 1000000000 | bytes 2000000 | tf_op jit(solution)/shard_map/first_kernel/pallas_call | solution.py:497
  32.7 1.7 %collective-permute-start.10 = (f32[72,128]{1,0:T(8,128)S(1)}, f32[72,128]{1,0:T(8,128)S(1)}, u32[]{:S(2)}, u32[]{:S(2)}) collective-permute-start(f32[72,128]{1,0:T(8,128)S(1)} %get-tuple-element.94._p3.r0), channel_id=1, source_target_pairs={{0,128},{4,132},{8,136},{12,140},{16,144},{20,148},{24,152},{28,15... | collective-permute-start | bytes 110600 | tf_op jit(solution)/shard_map/ppermute | solution.py:510
  34.4 1.8 %collective-permute-start.11 = (f32[72,128]{1,0:T(8,128)S(1)}, f32[72,128]{1,0:T(8,128)S(1)}, u32[]{:S(2)}, u32[]{:S(2)}) collective-permute-start(f32[72,128]{1,0:T(8,128)S(1)} %get-tuple-element.94._p3.r0), channel_id=1, source_target_pairs={{0,192},{4,196},{8,200},{12,204},{16,208},{20,212},{24,216},{28,22... | collective-permute-start | bytes 110600 | tf_op jit(solution)/shard_map/ppermute | solution.py:510
  36.5 2.9 %third_kernel.1 = (f32[8,128]{1,0:T(8,128)S(1)}, f32[8,128]{1,0:T(8,128)S(1)}, f32[256,128]{1,0:T(8,128)S(1)}, bf16[512,256]{1,0:T(8,128)(2,1)S(1)}, bf16[256,51...) custom-call(s32[4]{0:T(128)S(1)} %pad_add_fusion.pos, ...), custom_call_target="tpu_custom_call" | custom-call | flops 4000000000 | bytes 8000000 | tf_op jit(solution)/shard_map/third_kernel/pallas_call | solution.py:497
  40.2 1.4 %fourth_kernel.1 = (f32[8,512]{1,0:T(8,128)S(1)}, f32[8,512]{1,0:T(8,128)S(1)}, bf16[256,512]{1,0:T(8,128)(2,1)S(1)}, f32[272,256]{1,0:T(8,128)S(1)}, bf16[272,2...) custom-call(s32[4]{0:T(128)S(1)} %pad_add_fusion.pos, ...), custom_call_target="tpu_custom_call" | custom-call | flops 3000000000 | bytes 6000000 | tf_op jit(solution)/shard_map/fourth_kernel/pallas_call | solution.py:497
  42.6 2.3 %collective-permute-start.18 = (bf16[512,256]{1,0:T(8,128)(2,1)S(1)}, bf16[512,256]{1,0:T(8,128)(2,1)S(1)}, u32[]{:S(2)}, u32[]{:S(2)}) collective-permute-start(bf16[512,256]{1,0:T(8,128)(2,1)S(1)} %get-tuple-element.125._s), channel_id=1, source_target_pairs={{0,12},{4,8},{8,4},{12,0},{16,28},{20,24},{24,20},{28,16},{32,44},... | collective-permute-start | bytes 786440 | tf_op jit(solution)/shard_map/ppermute | solution.py:518
  44.9 1.2 %collective-permute-start.17 = (bf16[272,256]{1,0:T(8,128)(2,1)S(1)}, bf16[272,256]{1,0:T(8,128)(2,1)S(1)}, u32[]{:S(2)}, u32[]{:S(2)}) collective-permute-start(bf16[272,256]{1,0:T(8,128)(2,1)S(1)} %get-tuple-element.113), channel_id=1, source_target_pairs={{0,192},{4,196},{8,200},{12,204},{16,208},{20,212},{24,216},{28,22... | collective-permute-start | bytes 417800 | tf_op jit(solution)/shard_map/ppermute | solution.py:510
  46.1 3.5 %collective-permute-start.16 = (bf16[272,256]{1,0:T(8,128)(2,1)S(1)}, bf16[272,256]{1,0:T(8,128)(2,1)S(1)}, u32[]{:S(2)}, u32[]{:S(2)}) collective-permute-start(bf16[272,256]{1,0:T(8,128)(2,1)S(1)} %get-tuple-element.112), channel_id=1, source_target_pairs={{0,128},{4,132},{8,136},{12,140},{16,144},{20,148},{24,152},{28,15... | collective-permute-start | bytes 417800 | tf_op jit(solution)/shard_map/ppermute | solution.py:510
  49.6 1.8 %third_back_kernel.1 = (f32[512,256]{1,0:T(8,128)S(1)}, f32[512,256]{1,0:T(8,128)S(1)}, f32[256,128]{1,0:T(8,128)S(1)}, f32[512,128]{1,0:T(8,128)S(1)}, f32[512,128]{1,0:T(8,128)S(1)}, /*index=5*/f32[128,512]{1,0:T(8,128)S(1)}) custom-call(bf16[512,256]{1,0:T(8,128)(2,1)S(1)} %pair_kernel.4._s.a, bf16[512,256]{1,0:T(8,128)(2,1)S(1)} %collective-permute-done.2.b, ...), custom_call_target="tpu_custom_call" | custom-call | flops 3000000000 | bytes 6000000 | tf_op jit(solution)/shard_map/third_back_kernel/pallas_call | solution.py:497
  52.5 1.6 %collective-permute-done.16.b2 = bf16[272,256]{1,0:T(8,128)(2,1)S(1)} collective-permute-done((bf16[272,256]{1,0:T(8,128)(2,1)S(1)}, bf16[272,256]{1,0:T(8,128)(2,1)S(1)}, u32[]{:S(2)}, u32[]{:S(2)}) %collective-permute-start.16) | collective-permute-done | bytes 139296 | tf_op jit(solution)/shard_map/ppermute | solution.py:510
  55.5 2.5 %collective-permute-start.25 = (bf16[320,256]{1,0:T(8,128)(2,1)S(1)}, bf16[320,256]{1,0:T(8,128)(2,1)S(1)}, u32[]{:S(2)}, u32[]{:S(2)}) collective-permute-start(bf16[320,256]{1,0:T(8,128)(2,1)S(1)} %get-tuple-element.148), channel_id=1, source_target_pairs={{0,8},{4,12},{8,0},{12,4},{16,24},{20,28},{24,16},{28,20},{32,40},... | collective-permute-start | bytes 491528 | tf_op jit(solution)/shard_map/ppermute | solution.py:518
  58.0 2.2 %collective-permute-start.26 = (bf16[320,256]{1,0:T(8,128)(2,1)S(1)}, bf16[320,256]{1,0:T(8,128)(2,1)S(1)}, u32[]{:S(2)}, u32[]{:S(2)}) collective-permute-start(bf16[320,256]{1,0:T(8,128)(2,1)S(1)} %get-tuple-element.149), channel_id=1, source_target_pairs={{0,12},{4,8},{8,4},{12,0},{16,28},{20,24},{24,20},{28,16},{32,44},... | collective-permute-start | bytes 491528 | tf_op jit(solution)/shard_map/ppermute | solution.py:518
  60.3 1.3 %collective-permute-start.24 = (bf16[512,256]{1,0:T(8,128)(2,1)S(1)}, bf16[512,256]{1,0:T(8,128)(2,1)S(1)}, u32[]{:S(2)}, u32[]{:S(2)}) collective-permute-start(bf16[512,256]{1,0:T(8,128)(2,1)S(1)} %get-tuple-element.147), channel_id=1, source_target_pairs={{0,2},{1,3},{2,0},{3,1},{4,6},{5,7},{6,4},{7,5},{8,10},{9,11},{10,... | collective-permute-start | bytes 786440 | tf_op jit(solution)/shard_map/ppermute | solution.py:522
  61.6 1.4 %pair_back_kernel.1 = (f32[512,128]{1,0:T(8,128)S(1)}, f32[512,128]{1,0:T(8,128)S(1)}, f32[128,512]{1,0:T(8,128)S(1)}) custom-call(bf16[512,256]{1,0:T(8,128)(2,1)S(1)} %get-tuple-element.84._s.q, bf16[256,512]{1,0:T(8,128)(2,1)S(1)} %get-tuple-element.85.q_t, bf16[512,256]{1,0:T(8,128)(2,1)S(1)} %get-tuple-element.86.k, ...), custom_call_target="tpu_custom_call" | custom-call | flops 3000000000 | bytes 6000000 | tf_op jit(solution)/shard_map/pair_back_kernel/pallas_call | solution.py:497
  63.1 1.3 %collective-permute-start.19 = (f32[64,128]{1,0:T(8,128)S(1)}, f32[64,128]{1,0:T(8,128)S(1)}, u32[]{:S(2)}, u32[]{:S(2)}) collective-permute-start(f32[64,128]{1,0:T(8,128)S(1)} %get-tuple-element.128.own), channel_id=1, source_target_pairs={{0,192},{4,196},{8,200},{12,204},{16,208},{20,212},{24,216},{28,22... | collective-permute-start | bytes 98312 | tf_op jit(solution)/shard_map/ppermute | solution.py:510
  64.5 3.9 %collective-permute-done.19.got = f32[64,128]{1,0:T(8,128)S(1)} collective-permute-done((f32[64,128]{1,0:T(8,128)S(1)}, f32[64,128]{1,0:T(8,128)S(1)}, u32[]{:S(2)}, u32[]{:S(2)}) %collective-permute-start.19) | collective-permute-done | bytes 32800 | tf_op jit(solution)/shard_map/ppermute | solution.py:510
  69.4 1.6 %collective-permute-start.27 = (bf16[80,256]{1,0:T(8,128)(2,1)S(1)}, bf16[80,256]{1,0:T(8,128)(2,1)S(1)}, u32[]{:S(2)}, u32[]{:S(2)}) collective-permute-start(bf16[80,256]{1,0:T(8,128)(2,1)S(1)} %get-tuple-element.150._s), channel_id=1, source_target_pairs={{0,16},{4,20},{8,24},{12,28},{16,0},{20,4},{24,8},{28,12},{32,48},... | collective-permute-start | bytes 122888 | tf_op jit(solution)/shard_map/ppermute | solution.py:514
  70.9 3.6 %collective-permute-start.28 = (bf16[80,256]{1,0:T(8,128)(2,1)S(1)}, bf16[80,256]{1,0:T(8,128)(2,1)S(1)}, u32[]{:S(2)}, u32[]{:S(2)}) collective-permute-start(bf16[80,256]{1,0:T(8,128)(2,1)S(1)} %get-tuple-element.154), channel_id=1, source_target_pairs={{0,32},{4,36},{8,40},{12,44},{16,48},{20,52},{24,56},{28,60},{32,0... | collective-permute-start | bytes 122888 | tf_op jit(solution)/shard_map/ppermute | solution.py:514
  74.6 1.4 %collective-permute-start.29 = (bf16[80,256]{1,0:T(8,128)(2,1)S(1)}, bf16[80,256]{1,0:T(8,128)(2,1)S(1)}, u32[]{:S(2)}, u32[]{:S(2)}) collective-permute-start(bf16[80,256]{1,0:T(8,128)(2,1)S(1)} %get-tuple-element.155), channel_id=1, source_target_pairs={{0,48},{4,52},{8,56},{12,60},{16,32},{20,36},{24,40},{28,44},{32,1... | collective-permute-start | bytes 122888 | tf_op jit(solution)/shard_map/ppermute | solution.py:514
  76.0 2.8 %natural_kernel.1 = (bf16[512,256]{1,0:T(8,128)(2,1)}, bf16[512,256]{1,0:T(8,128)(2,1)S(1)}, bf16[512,256]{1,0:T(8,128)(2,1)S(1)}, f32[32,256]{1,0:T(8,128)S(1)}...) custom-call(s32[4]{0:T(128)S(1)} %pad_add_fusion.pos, f32[64,128]{1,0:T(8,128)S(1)} %get-tuple-element.129.e0, ...), custom_call_target="tpu_custom_call" | custom-call | flops 3000000000 | bytes 6000000 | tf_op jit(solution)/shard_map/natural_kernel/pallas_call | solution.py:497
  79.2 1.9 %collective-permute-done.29.b3 = bf16[80,256]{1,0:T(8,128)(2,1)S(1)} collective-permute-done((bf16[80,256]{1,0:T(8,128)(2,1)S(1)}, bf16[80,256]{1,0:T(8,128)(2,1)S(1)}, u32[]{:S(2)}, u32[]{:S(2)}) %collective-permute-start.29) | collective-permute-done | bytes 40992 | tf_op jit(solution)/shard_map/ppermute | solution.py:514
  81.1 1.8 %last_kernel.1 = (bf16[512,256]{1,0:T(8,128)(2,1)}, bf16[512,256]{1,0:T(8,128)(2,1)}, f32[16,256]{1,0:T(8,128)}) custom-call(s32[4]{0:T(128)S(1)} %pad_add_fusion.pos, f32[80,256]{1,0:T(8,128)S(1)} %get-tuple-element.153.own, bf16[80,256]{1,0:T(8,128)(2,1)S(1)} %collective-permute-done.27.b1, bf16[80,256]{1,0:T(8,128)(2,1)S(1)} %collective-permute-done.28.b2, ...), custom_call_target="tpu_custom_call" | custom-call | flops 1000000000 | bytes 2000000 | tf_op jit(solution)/shard_map/last_kernel/pallas_call | solution.py:497
  (64 shorter events, 13.9 us)
Async XLA Ops:
  3.5 5.9 %copy-start.3 = (bf16[512,256]{1,0:T(8,128)(2,1)S(1)}, bf16[512,256]{1,0:T(8,128)(2,1)}, u32[]{:S(2)}) copy-start(bf16[512,256]{1,0:T(8,128)(2,1)} %q.1) | copy-start | bytes 786436
  3.5 9.5 %collective-permute-start.1 = (bf16[64,256]{1,0:T(8,128)(2,1)S(1)}, bf16[64,256]{1,0:T(8,128)(2,1)S(1)}, u32[]{:S(2)}, u32[]{:S(2)}) collective-permute-start(bf16[64,256]{1,0:T(8,128)(2,1)S(1)} %pick3_kernel.1._p3.a), channel_id=1, source_target_pairs={{0,16},{4,20},{8,24},{12,28},{16,0},{20,4},{24,8},{28,12},{32,48},... | collective-permute-start | bytes 98312 | tf_op jit(solution)/shard_map/ppermute | solution.py:514
  7.7 11.0 %collective-permute-start = (bf16[256,256]{1,0:T(8,128)(2,1)S(1)}, bf16[256,256]{1,0:T(8,128)(2,1)S(1)}, u32[]{:S(2)}, u32[]{:S(2)}) collective-permute-start(bf16[256,256]{1,0:T(8,128)(2,1)S(1)} %pick2_kernel.1._s.a), channel_id=1, source_target_pairs={{0,4},{4,0},{8,12},{12,8},{16,20},{20,16},{24,28},{28,24},{32,36},... | collective-permute-start | bytes 393224 | tf_op jit(solution)/shard_map/ppermute | solution.py:518
  11.4 5.3 %collective-permute-start.4 = (bf16[16,256]{1,0:T(8,128)(2,1)S(1)}, bf16[16,256]{1,0:T(8,128)(2,1)S(1)}, u32[]{:S(2)}, u32[]{:S(2)}) collective-permute-start(bf16[16,256]{1,0:T(8,128)(2,1)S(1)} %get-tuple-element.89.a), channel_id=1, source_target_pairs={{0,64},{4,68},{8,72},{12,76},{16,80},{20,84},{24,88},{28,92},{32,9... | collective-permute-start | bytes 24584 | tf_op jit(solution)/shard_map/ppermute | solution.py:510
  13.0 9.8 %collective-permute-start.3 = (bf16[128,256]{1,0:T(8,128)(2,1)S(1)}, bf16[128,256]{1,0:T(8,128)(2,1)S(1)}, u32[]{:S(2)}, u32[]{:S(2)}) collective-permute-start(bf16[128,256]{1,0:T(8,128)(2,1)S(1)} %pair_kernel.3._s), channel_id=1, source_target_pairs={{0,48},{4,52},{8,56},{12,60},{16,32},{20,36},{24,40},{28,44},{32,1... | collective-permute-start | bytes 196616 | tf_op jit(solution)/shard_map/ppermute | solution.py:514
  16.7 6.1 %collective-permute-start.5 = (bf16[32,256]{1,0:T(8,128)(2,1)S(1)}, bf16[32,256]{1,0:T(8,128)(2,1)S(1)}, u32[]{:S(2)}, u32[]{:S(2)}) collective-permute-start(bf16[32,256]{1,0:T(8,128)(2,1)S(1)} %pair_kernel.5.qa), channel_id=1, source_target_pairs={{0,192},{4,196},{8,200},{12,204},{16,208},{20,212},{24,216},{28,22... | collective-permute-start | bytes 49160 | tf_op jit(solution)/shard_map/ppermute | solution.py:510
  18.8 11.6 %collective-permute-start.2 = (bf16[512,256]{1,0:T(8,128)(2,1)S(1)}, bf16[512,256]{1,0:T(8,128)(2,1)S(1)}, u32[]{:S(2)}, u32[]{:S(2)}) collective-permute-start(bf16[512,256]{1,0:T(8,128)(2,1)S(1)} %pair_kernel.4._s.a), channel_id=1, source_target_pairs={{0,12},{4,8},{8,4},{12,0},{16,28},{20,24},{24,20},{28,16},{32,44},... | collective-permute-start | bytes 786440 | tf_op jit(solution)/shard_map/ppermute | solution.py:518
  22.8 7.6 %collective-permute-start.13 = (bf16[512,256]{1,0:T(8,128)(2,1)S(1)}, bf16[512,256]{1,0:T(8,128)(2,1)S(1)}, u32[]{:S(2)}, u32[]{:S(2)}) collective-permute-start(bf16[512,256]{1,0:T(8,128)(2,1)S(1)} %get-tuple-element.101.c0), channel_id=1, source_target_pairs={{0,2},{1,3},{2,0},{3,1},{4,6},{5,7},{6,4},{7,5},{8,10},{9,11},{10,... | collective-permute-start | bytes 786440 | tf_op jit(solution)/shard_map/ppermute | solution.py:522
  23.9 7.9 %collective-permute-start.6 = (bf16[192,256]{1,0:T(8,128)(2,1)S(1)}, bf16[192,256]{1,0:T(8,128)(2,1)S(1)}, u32[]{:S(2)}, u32[]{:S(2)}) collective-permute-start(bf16[192,256]{1,0:T(8,128)(2,1)S(1)} %get-tuple-element.90._s.c0.a0), channel_id=1, source_target_pairs={{0,4},{4,0},{8,12},{12,8},{16,20},{20,16},{24,28},{28,24},{32,36},... | collective-permute-start | bytes 294920 | tf_op jit(solution)/shard_map/ppermute | solution.py:518
  24.6 7.3 %collective-permute-start.7 = (bf16[192,256]{1,0:T(8,128)(2,1)S(1)}, bf16[192,256]{1,0:T(8,128)(2,1)S(1)}, u32[]{:S(2)}, u32[]{:S(2)}) collective-permute-start(bf16[192,256]{1,0:T(8,128)(2,1)S(1)} %get-tuple-element.90._s.c0.a0), channel_id=1, source_target_pairs={{0,8},{4,12},{8,0},{12,4},{16,24},{20,28},{24,16},{28,20},{32,40},... | collective-permute-start | bytes 294920 | tf_op jit(solution)/shard_map/ppermute | solution.py:518
  26.5 5.8 %collective-permute-start.8 = (bf16[192,256]{1,0:T(8,128)(2,1)S(1)}, bf16[192,256]{1,0:T(8,128)(2,1)S(1)}, u32[]{:S(2)}, u32[]{:S(2)}) collective-permute-start(bf16[192,256]{1,0:T(8,128)(2,1)S(1)} %get-tuple-element.90._s.c0.a0), channel_id=1, source_target_pairs={{0,12},{4,8},{8,4},{12,0},{16,28},{20,24},{24,20},{28,16},{32,44},... | collective-permute-start | bytes 294920 | tf_op jit(solution)/shard_map/ppermute | solution.py:518
  30.4 6.1 %collective-permute-start.12 = (bf16[512,256]{1,0:T(8,128)(2,1)S(1)}, bf16[512,256]{1,0:T(8,128)(2,1)S(1)}, u32[]{:S(2)}, u32[]{:S(2)}) collective-permute-start(bf16[512,256]{1,0:T(8,128)(2,1)S(1)} %get-tuple-element.101.c0), channel_id=1, source_target_pairs={{0,1},{1,0},{2,3},{3,2},{4,5},{5,4},{6,7},{7,6},{8,9},{9,8},{10,11... | collective-permute-start | bytes 786440 | tf_op jit(solution)/shard_map/ppermute | solution.py:522
  30.5 6.0 %collective-permute-start.14 = (bf16[512,256]{1,0:T(8,128)(2,1)S(1)}, bf16[512,256]{1,0:T(8,128)(2,1)S(1)}, u32[]{:S(2)}, u32[]{:S(2)}) collective-permute-start(bf16[512,256]{1,0:T(8,128)(2,1)S(1)} %collective-permute-done.13.c2), channel_id=1, source_target_pairs={{0,1},{1,0},{2,3},{3,2},{4,5},{5,4},{6,7},{7,6},{8,9},{9,8},{10,11... | collective-permute-start | bytes 786440 | tf_op jit(solution)/shard_map/ppermute | solution.py:522
  32.3 4.2 %copy-start = (bf16[256,1024]{1,0:T(8,128)(2,1)S(1)}, bf16[256,1024]{1,0:T(8,128)(2,1)}, u32[]{:S(2)}) copy-start(bf16[256,1024]{1,0:T(8,128)(2,1)} %w.3) | copy-start | bytes 1572868
  32.7 6.7 %collective-permute-start.10 = (f32[72,128]{1,0:T(8,128)S(1)}, f32[72,128]{1,0:T(8,128)S(1)}, u32[]{:S(2)}, u32[]{:S(2)}) collective-permute-start(f32[72,128]{1,0:T(8,128)S(1)} %get-tuple-element.94._p3.r0), channel_id=1, source_target_pairs={{0,128},{4,132},{8,136},{12,140},{16,144},{20,148},{24,152},{28,15... | collective-permute-start | bytes 110600 | tf_op jit(solution)/shard_map/ppermute | solution.py:510
  34.4 5.2 %collective-permute-start.11 = (f32[72,128]{1,0:T(8,128)S(1)}, f32[72,128]{1,0:T(8,128)S(1)}, u32[]{:S(2)}, u32[]{:S(2)}) collective-permute-start(f32[72,128]{1,0:T(8,128)S(1)} %get-tuple-element.94._p3.r0), channel_id=1, source_target_pairs={{0,192},{4,196},{8,200},{12,204},{16,208},{20,212},{24,216},{28,22... | collective-permute-start | bytes 110600 | tf_op jit(solution)/shard_map/ppermute | solution.py:510
  36.3 4.0 %collective-permute-start.9 = (f32[72,128]{1,0:T(8,128)S(1)}, f32[72,128]{1,0:T(8,128)S(1)}, u32[]{:S(2)}, u32[]{:S(2)}) collective-permute-start(f32[72,128]{1,0:T(8,128)S(1)} %get-tuple-element.94._p3.r0), channel_id=1, source_target_pairs={{0,64},{4,68},{8,72},{12,76},{16,80},{20,84},{24,88},{28,92},{32,9... | collective-permute-start | bytes 110600 | tf_op jit(solution)/shard_map/ppermute | solution.py:510
  42.6 11.9 %collective-permute-start.18 = (bf16[512,256]{1,0:T(8,128)(2,1)S(1)}, bf16[512,256]{1,0:T(8,128)(2,1)S(1)}, u32[]{:S(2)}, u32[]{:S(2)}) collective-permute-start(bf16[512,256]{1,0:T(8,128)(2,1)S(1)} %get-tuple-element.125._s), channel_id=1, source_target_pairs={{0,12},{4,8},{8,4},{12,0},{16,28},{20,24},{24,20},{28,16},{32,44},... | collective-permute-start | bytes 786440 | tf_op jit(solution)/shard_map/ppermute | solution.py:518
  44.9 7.6 %collective-permute-start.17 = (bf16[272,256]{1,0:T(8,128)(2,1)S(1)}, bf16[272,256]{1,0:T(8,128)(2,1)S(1)}, u32[]{:S(2)}, u32[]{:S(2)}) collective-permute-start(bf16[272,256]{1,0:T(8,128)(2,1)S(1)} %get-tuple-element.113), channel_id=1, source_target_pairs={{0,192},{4,196},{8,200},{12,204},{16,208},{20,212},{24,216},{28,22... | collective-permute-start | bytes 417800 | tf_op jit(solution)/shard_map/ppermute | solution.py:510
  46.1 6.4 %collective-permute-start.15 = (bf16[272,256]{1,0:T(8,128)(2,1)S(1)}, bf16[272,256]{1,0:T(8,128)(2,1)S(1)}, u32[]{:S(2)}, u32[]{:S(2)}) collective-permute-start(bf16[272,256]{1,0:T(8,128)(2,1)S(1)} %get-tuple-element.111), channel_id=1, source_target_pairs={{0,64},{4,68},{8,72},{12,76},{16,80},{20,84},{24,88},{28,92},{32,9... | collective-permute-start | bytes 417800 | tf_op jit(solution)/shard_map/ppermute | solution.py:510
  46.1 8.0 %collective-permute-start.16 = (bf16[272,256]{1,0:T(8,128)(2,1)S(1)}, bf16[272,256]{1,0:T(8,128)(2,1)S(1)}, u32[]{:S(2)}, u32[]{:S(2)}) collective-permute-start(bf16[272,256]{1,0:T(8,128)(2,1)S(1)} %get-tuple-element.112), channel_id=1, source_target_pairs={{0,128},{4,132},{8,136},{12,140},{16,144},{20,148},{24,152},{28,15... | collective-permute-start | bytes 417800 | tf_op jit(solution)/shard_map/ppermute | solution.py:510
  55.3 4.9 %collective-permute-start.23 = (bf16[1024,256]{1,0:T(8,128)(2,1)S(1)}, bf16[1024,256]{1,0:T(8,128)(2,1)S(1)}, u32[]{:S(2)}, u32[]{:S(2)}) collective-permute-start(bf16[1024,256]{1,0:T(8,128)(2,1)S(1)} %get-tuple-element.145), channel_id=1, source_target_pairs={{0,1},{1,0},{2,3},{3,2},{4,5},{5,4},{6,7},{7,6},{8,9},{9,8},{10,11... | collective-permute-start | bytes 1572872 | tf_op jit(solution)/shard_map/ppermute | solution.py:522
  55.4 7.6 %collective-permute-start.21 = (bf16[320,256]{1,0:T(8,128)(2,1)S(1)}, bf16[320,256]{1,0:T(8,128)(2,1)S(1)}, u32[]{:S(2)}, u32[]{:S(2)}) collective-permute-start(bf16[320,256]{1,0:T(8,128)(2,1)S(1)} %get-tuple-element.135._s), channel_id=1, source_target_pairs={{0,4},{4,0},{8,12},{12,8},{16,20},{20,16},{24,28},{28,24},{32,36},... | collective-permute-start | bytes 491528 | tf_op jit(solution)/shard_map/ppermute | solution.py:518
  55.5 13.0 %collective-permute-start.25 = (bf16[320,256]{1,0:T(8,128)(2,1)S(1)}, bf16[320,256]{1,0:T(8,128)(2,1)S(1)}, u32[]{:S(2)}, u32[]{:S(2)}) collective-permute-start(bf16[320,256]{1,0:T(8,128)(2,1)S(1)} %get-tuple-element.148), channel_id=1, source_target_pairs={{0,8},{4,12},{8,0},{12,4},{16,24},{20,28},{24,16},{28,20},{32,40},... | collective-permute-start | bytes 491528 | tf_op jit(solution)/shard_map/ppermute | solution.py:518
  58.0 10.7 %collective-permute-start.26 = (bf16[320,256]{1,0:T(8,128)(2,1)S(1)}, bf16[320,256]{1,0:T(8,128)(2,1)S(1)}, u32[]{:S(2)}, u32[]{:S(2)}) collective-permute-start(bf16[320,256]{1,0:T(8,128)(2,1)S(1)} %get-tuple-element.149), channel_id=1, source_target_pairs={{0,12},{4,8},{8,4},{12,0},{16,28},{20,24},{24,20},{28,16},{32,44},... | collective-permute-start | bytes 491528 | tf_op jit(solution)/shard_map/ppermute | solution.py:518
  60.3 15.7 %collective-permute-start.24 = (bf16[512,256]{1,0:T(8,128)(2,1)S(1)}, bf16[512,256]{1,0:T(8,128)(2,1)S(1)}, u32[]{:S(2)}, u32[]{:S(2)}) collective-permute-start(bf16[512,256]{1,0:T(8,128)(2,1)S(1)} %get-tuple-element.147), channel_id=1, source_target_pairs={{0,2},{1,3},{2,0},{3,1},{4,6},{5,7},{6,4},{7,5},{8,10},{9,11},{10,... | collective-permute-start | bytes 786440 | tf_op jit(solution)/shard_map/ppermute | solution.py:522
  63.0 12.9 %collective-permute-start.22 = (bf16[256,256]{1,0:T(8,128)(2,1)S(1)}, bf16[256,256]{1,0:T(8,128)(2,1)S(1)}, u32[]{:S(2)}, u32[]{:S(2)}) collective-permute-start(bf16[256,256]{1,0:T(8,128)(2,1)S(1)} %get-tuple-element.140._s), channel_id=1, source_target_pairs={{0,4},{4,0},{8,12},{12,8},{16,20},{20,16},{24,28},{28,24},{32,36},... | collective-permute-start | bytes 393224 | tf_op jit(solution)/shard_map/ppermute | solution.py:518
  63.1 5.2 %collective-permute-start.19 = (f32[64,128]{1,0:T(8,128)S(1)}, f32[64,128]{1,0:T(8,128)S(1)}, u32[]{:S(2)}, u32[]{:S(2)}) collective-permute-start(f32[64,128]{1,0:T(8,128)S(1)} %get-tuple-element.128.own), channel_id=1, source_target_pairs={{0,192},{4,196},{8,200},{12,204},{16,208},{20,212},{24,216},{28,22... | collective-permute-start | bytes 98312 | tf_op jit(solution)/shard_map/ppermute | solution.py:510
  68.4 6.1 %collective-permute-start.20 = (f32[64,128]{1,0:T(8,128)S(1)}, f32[64,128]{1,0:T(8,128)S(1)}, u32[]{:S(2)}, u32[]{:S(2)}) collective-permute-start(f32[64,128]{1,0:T(8,128)S(1)} %get-tuple-element.130), channel_id=1, source_target_pairs={{0,64},{4,68},{8,72},{12,76},{16,80},{20,84},{24,88},{28,92},{32,9... | collective-permute-start | bytes 98312 | tf_op jit(solution)/shard_map/ppermute | solution.py:510
  69.4 9.4 %collective-permute-start.27 = (bf16[80,256]{1,0:T(8,128)(2,1)S(1)}, bf16[80,256]{1,0:T(8,128)(2,1)S(1)}, u32[]{:S(2)}, u32[]{:S(2)}) collective-permute-start(bf16[80,256]{1,0:T(8,128)(2,1)S(1)} %get-tuple-element.150._s), channel_id=1, source_target_pairs={{0,16},{4,20},{8,24},{12,28},{16,0},{20,4},{24,8},{28,12},{32,48},... | collective-permute-start | bytes 122888 | tf_op jit(solution)/shard_map/ppermute | solution.py:514
  70.9 8.2 %collective-permute-start.28 = (bf16[80,256]{1,0:T(8,128)(2,1)S(1)}, bf16[80,256]{1,0:T(8,128)(2,1)S(1)}, u32[]{:S(2)}, u32[]{:S(2)}) collective-permute-start(bf16[80,256]{1,0:T(8,128)(2,1)S(1)} %get-tuple-element.154), channel_id=1, source_target_pairs={{0,32},{4,36},{8,40},{12,44},{16,48},{20,52},{24,56},{28,60},{32,0... | collective-permute-start | bytes 122888 | tf_op jit(solution)/shard_map/ppermute | solution.py:514
  74.6 6.6 %collective-permute-start.29 = (bf16[80,256]{1,0:T(8,128)(2,1)S(1)}, bf16[80,256]{1,0:T(8,128)(2,1)S(1)}, u32[]{:S(2)}, u32[]{:S(2)}) collective-permute-start(bf16[80,256]{1,0:T(8,128)(2,1)S(1)} %get-tuple-element.155), channel_id=1, source_target_pairs={{0,48},{4,52},{8,56},{12,60},{16,32},{20,36},{24,40},{28,44},{32,1... | collective-permute-start | bytes 122888 | tf_op jit(solution)/shard_map/ppermute | solution.py:514
  (3 other events, 3.6 us)
